TPU v7x, 256 devices: a whole 4x4x8 slice. The times are simulated.
256 devices in a mesh: space: 64 (over y_lo, z, x), group: 4 (over y_hi, core).
Axes of the slice: x: 4, y: 4 (y_hi: 2, y_lo: 2; y = y_hi * 2 + y_lo), z: 8, core: 2. Of those that a mesh axis runs over, the one named last changes fastest.
Arguments:
- species: float32 [54, 256, 128, 128], P(None, 'space', 'group'), may hold values from 0 to 0.4
- diffusion: float32 [54], replicated, may hold values from 0.01 to 0.1
- gas_temp: float32 [256, 128, 128], P('space', 'group'), may hold values from 0.6 to 1.6
- gas_density: float32 [256, 128, 128], P('space', 'group'), may hold values from 0.5 to 2
- gas_velocity: float32 [3, 256, 128, 128], P(None, 'space', 'group'), may hold values from -1 to 1
- drop_radius: float32 [1048576], P(('space', 'group')), may hold values from 0.5 to 2
- drop_temp: float32 [1048576], P(('space', 'group')), may hold values from 0.6 to 1.2
- drop_velocity: float32 [3, 1048576], P(None, ('space', 'group')), may hold values from -2 to 2
- parcel_cells: int32 [8, 1048576], P(None, ('space', 'group')), may hold values from 0 to 98303, as said below
- parcel_weights: float32 [8, 1048576], P(None, ('space', 'group')), as said below
- parcel_counts: int32 [64], P('space'), may hold values from 2048 to 16384, as said below
Outputs:
- species_next: float32 [54, 256, 128, 128], P(None, 'space', 'group')
- gas_sources: float32 [7, 256, 128, 128], P(None, 'space', 'group')
- parcel_state: float32 [5, 1048576], P(None, ('space', 'group'))
Inputs may be any that keep to these rules, and one draw needn't show every extreme that they name: `parcel_cells`: the eight global indices of a parcel are the corners of one box of 2 x 2 x 2 cells, corner c at offsets (c // 4, c // 2 % 2, c % 2) from the first; that first cell lies in the parcel's slab or in the plane just before it, and the box lies inside the grid. `parcel_weights`: the eight weights of a parcel are non-negative trilinear weights and sum to one. `parcel_counts`: some slab is full in every draw.
All inputs are finite; a program needn't handle non-finite values.
Results may differ from a plain program's by a relative error of at most 0.000058.
Values sent between devices are 32-bit elements; how exact they have to be, the bound alone decides.
No kernel may reach another device: no remote copies, remote signals or barrier semaphores. Data moves between devices by JAX's collectives and lax.ppermute only.
A program may use at most 256 MiB of HBM per device.

v0:
```python
import functools

import jax
import jax.numpy as jnp
from jax import lax
from jax.experimental import pallas as pl
from jax.experimental.pallas import tpu as pltpu
from jax.sharding import PartitionSpec as P

time_step = 0.05
evap_coef = 0.5
heat_coef = 0.15
latent_coef = 0.2
enthalpy_coef = 1.3
source_coef = 0.5
courant = 0.3

LANES = 128
PARTS = (54,)
MANY = 18
CHUNK = 512
PHYS = 1024
WINDOW = 256
YPAD = 40
ROWS_WIDTH = 9 * LANES
F32 = jnp.float32
BF16 = jnp.bfloat16
NT = (((1,), (1,)), ((), ()))


def halves(value):
    high = value.astype(BF16)
    return high, (value - high.astype(F32)).astype(BF16)


def hat(index, start, fraction):
    away = index - start
    return jnp.where(away == 0.0, 1.0 - fraction, jnp.where(away == 1.0, fraction, 0.0))


def iota(shape, dim):
    return lax.broadcasted_iota(jnp.int32, shape, dim)


def one_hot(dst_row, aligned):
    rel = dst_row - aligned.astype(F32)
    return jnp.where(iota((WINDOW, LANES), 0).astype(F32) == rel, 1.0, 0.0).astype(BF16)


def cells_of(width):
    return (width - ROWS_WIDTH) // 9 * 8


def physics(interp, radius, drop_temp, velocity):
    heat, density, speed, fuel = interp[0], interp[1], interp[2:5], interp[5]
    slip = [g - v for g, v in zip(speed, velocity)]
    slip_square = slip[0] * slip[0] + slip[1] * slip[1] + slip[2] * slip[2]
    log_flow = jnp.log(1.0 + density * radius * slip_square)
    sherwood = 2.0 + 0.6 * jnp.exp(0.25 * log_flow)
    surface = 0.5 / (1.0 + jnp.exp(-4.0 * (drop_temp - 1.0)))
    evap = evap_coef * radius * density * sherwood * jnp.log((1.0 - fuel) / (1.0 - surface))
    mass = radius * radius * radius
    ratio = 1.0 - time_step * evap / mass
    new_radius = radius * jnp.exp(jnp.log(ratio) * (1.0 / 3.0))
    rate = time_step * (1.0 + 0.15 * jnp.exp(0.35 * log_flow)) / (2.0 * radius * radius)
    change = [rate * s for s in slip]
    new_velocity = [v + c for v, c in zip(velocity, change)]
    heat_rate = heat_coef * sherwood / (radius * radius)
    new_temp = drop_temp + time_step * (
        heat_rate * (heat - drop_temp) - latent_coef * evap / mass
    )
    vapour = time_step * evap
    lost = [mass * (v - n) for v, n in zip(velocity, new_velocity)]
    momentum = [m + vapour * v for m, v in zip(lost, velocity)]
    heat_gain = -time_step * mass * heat_rate * (heat - drop_temp)
    enthalpy = enthalpy_coef * vapour * new_temp
    drag = lost[0] * speed[0] + lost[1] * speed[1] + lost[2] * speed[2]
    return [new_radius, new_temp] + new_velocity, [vapour] + momentum + [heat_gain, enthalpy, drag]


def parcel_kernel(
    info_ref,
    pk_ref,
    lo_ref,
    temp_ref,
    dens_ref,
    vel_ref,
    fuel_ref,
    hi_ref,
    main_ref,
    dlo_ref,
    dhi_ref,
    state_ref,
    own_dst_ref,
    off_ref,
    dst_ref,
    cell_scr,
    off_smem,
    sem,
    pieces,
    cv,
    row_scr,
    ft,
    a_hi,
    a_lo,
    interp,
    src,
    dep,
):
    groups = pk_ref.shape[0]
    each = cells_of(pk_ref.shape[2]) // 8
    capacity = each * 8
    slots = groups * capacity
    blocks = slots // LANES
    count, group = info_ref[0], info_ref[1]

    per_line = each // LANES
    for b in range(blocks):
        q, r = divmod(b, capacity // LANES)
        line, at = divmod(r, per_line)
        at = capacity + at * LANES
        cell_scr[b : b + 1, :] = pk_ref[q, line : line + 1, at : at + LANES]
    cell = cell_scr[...].astype(jnp.int32)
    slot = iota((blocks, LANES), 0) * LANES + iota((blocks, LANES), 1)
    y_of = ((cell >> 7) & 127) - group * 32
    mine = jnp.logical_and(slot < count, jnp.logical_and(y_of >= -1, y_of < 32))
    ones = jnp.where(mine, 1.0, 0.0).astype(BF16)
    before = jnp.where(iota((LANES, LANES), 0) < iota((LANES, LANES), 1), 1.0, 0.0).astype(BF16)
    after = jnp.where(iota((LANES, LANES), 1) < iota((LANES, LANES), 0), 1.0, 0.0).astype(BF16)
    full = jnp.ones((LANES, LANES), BF16)
    within = jnp.dot(ones, before, preferred_element_type=F32)
    row_sum = jnp.dot(ones, full, preferred_element_type=F32).astype(BF16)
    offset = jnp.dot(after, row_sum, preferred_element_type=F32)
    dst = jnp.where(mine, within + offset, -1.0)
    dst_ref[...] = dst
    own_dst_ref[...] = jnp.where(y_of >= 0, dst, -1.0)
    counts = lax.dot_general(jnp.ones((16, LANES), BF16), ones, NT, preferred_element_type=F32)
    counts = counts.astype(BF16)
    starts = jnp.dot(counts, before, preferred_element_type=F32)
    total = jnp.dot(counts, full, preferred_element_type=F32)
    first = iota((8, LANES), 0) == 0
    off_ref[...] = jnp.where(first, starts[0:8], total[0:8]).astype(jnp.int32)
    copy = pltpu.make_async_copy(off_ref, off_smem, sem)
    copy.start()

    def split(q, carry):
        for line in range(8):
            cells = pk_ref[q, line : line + 1, capacity : capacity + each]
            cells = jnp.broadcast_to(cells, (8, each)).astype(jnp.int32)
            row = iota((8, each), 0)
            y_place = ((cells >> 7) & 127) - group * 32
            place = jnp.where(row == 0, cells >> 14, jnp.where(row == 1, y_place, cells & 127))
            values = pk_ref[q, :, line * each : (line + 1) * each]
            high, low = halves(jnp.concatenate([values, place.astype(F32)], axis=0))
            at = pl.ds(pl.multiple_of(q * capacity + line * each, each), each)
            pieces[0:16, at] = high
            pieces[16:32, at] = low
        return carry

    lax.fori_loop(0, groups, split, 0)

    zero = jnp.zeros((256, LANES), F32)
    own = [temp_ref, dens_ref, vel_ref.at[0], vel_ref.at[1], vel_ref.at[2], fuel_ref.at[0]]
    planes = temp_ref.shape[0]
    rows = temp_ref.shape[1]
    row_start = capacity + each
    after_me = jnp.minimum(group + 1, groups - 1)
    before_me = jnp.maximum(group - 1, 0)
    for f in range(6):
        row_scr[...] = zero
        for x in range(planes + 2):
            if x == 0:
                block = lo_ref[f, 0]
            elif x == planes + 1:
                block = hi_ref[f, 0]
            else:
                block = own[f][x - 1]
            row_scr[x * YPAD : x * YPAD + rows, :] = block
            block, line = row_place(planes, f, x, 0)
            at = row_start + block * LANES
            following = pk_ref[after_me, line : line + 1, at : at + LANES]
            row_scr[x * YPAD + rows : x * YPAD + rows + 1, :] = following
            block, line = row_place(planes, f, x, 1)
            at = row_start + block * LANES
            former = pk_ref[before_me, line : line + 1, at : at + LANES]
            row_scr[(x + 1) * YPAD - 1 : (x + 1) * YPAD, :] = former
        high, low = halves(row_scr[...].T)
        at = slice(f * LANES, (f + 1) * LANES)
        ft[at, 0:256] = high
        ft[at, 256:512] = low
        ft[at, 512:768] = high

    cv[...] = jnp.zeros(cv.shape, F32)
    state_ref[...] = jnp.zeros(state_ref.shape, F32)
    dep[...] = jnp.zeros(dep.shape, F32)
    copy.wait()
    live = off_smem[1, 0]

    def compact(i, carry):
        got = []
        for j in range(8):
            b = i * 8 + j
            aligned = (off_smem[0, b] >> 7) << 7
            hot = one_hot(dst_ref[pl.ds(b, 1), :], aligned)
            block = pieces[:, pl.ds(pl.multiple_of(b * LANES, LANES), LANES)]
            got.append((aligned, lax.dot_general(block, hot, NT, preferred_element_type=F32)))
        for aligned, both in got:
            at = pl.ds(pl.multiple_of(aligned, LANES), WINDOW)
            cv[:, at] += both[0:16] + both[16:32]
        return carry

    lax.fori_loop(0, blocks // 8, compact, 0)

    def gather(c, carry):
        at = pl.ds(pl.multiple_of(c * CHUNK, CHUNK), CHUNK)
        valid = c * CHUNK + iota((1, CHUNK), 1) < live
        fx, fy, fz = cv[0:1, at], cv[1:2, at], cv[2:3, at]
        x0, z0 = cv[8:9, at], cv[10:11, at]
        y0 = jnp.where(valid, cv[9:10, at], 1000.0)
        line = iota((YPAD, CHUNK), 0)
        wy = hat(jnp.where(line == YPAD - 1, -1, line).astype(F32), y0, fy)
        parts = [wy * hat(float(x), x0, fx) for x in range(planes + 2)]
        parts.append(jnp.zeros((256 - (planes + 2) * YPAD, CHUNK), F32))
        high, low = halves(jnp.concatenate(parts, axis=0))
        a_hi[c] = high
        a_lo[c] = low
        stacked = jnp.concatenate([high, high, low], axis=0)
        lines = jnp.dot(ft[...], stacked, preferred_element_type=F32)
        wz = hat(iota((LANES, CHUNK), 0).astype(F32), z0, fz)
        for f in range(6):
            interp[f : f + 1, at] = jnp.sum(
                lines[f * LANES : (f + 1) * LANES] * wz, axis=0, keepdims=True
            )
        return carry

    chunks = (live + CHUNK - 1) // CHUNK
    lax.fori_loop(0, chunks, gather, 0)

    def step(c, carry):
        at = pl.ds(pl.multiple_of(c * PHYS, PHYS), PHYS)
        valid = c * PHYS + iota((1, PHYS), 1) < live
        inside = [jnp.where(valid, interp[f : f + 1, at], 0.0) for f in range(6)]
        radius = jnp.where(valid, cv[3:4, at], 1.0)
        velocity = [cv[d : d + 1, at] for d in (5, 6, 7)]
        new, sources = physics(inside, radius, cv[4:5, at], velocity)
        for s in range(5):
            state_ref[s : s + 1, at] = jnp.where(valid, new[s], 0.0)
        for k in range(7):
            src[k : k + 1, at] = jnp.where(valid, sources[k], 0.0)
        return carry

    lax.fori_loop(0, (live + PHYS - 1) // PHYS, step, 0)

    def deposit(c, carry):
        at = pl.ds(pl.multiple_of(c * CHUNK, CHUNK), CHUNK)
        wz = hat(iota((LANES, CHUNK), 0).astype(F32), cv[10:11, at], cv[2:3, at])
        high, low = halves(jnp.concatenate([wz * src[k : k + 1, at] for k in range(7)], axis=0))
        left = jnp.concatenate([high, low, high], axis=1)
        right = jnp.concatenate([a_hi[c], a_hi[c], a_lo[c]], axis=1)
        dep[...] += lax.dot_general(left, right, NT, preferred_element_type=F32)
        return carry

    lax.fori_loop(0, chunks, deposit, 0)

    for k in range(7):
        cells = dep[k * LANES : (k + 1) * LANES, :].T
        for x in range(planes + 2):
            block = cells[x * YPAD : x * YPAD + rows]
            if x == 0:
                dlo_ref[k, 0] = block
            elif x == planes + 1:
                dhi_ref[k, 0] = block
            else:
                main_ref[k, x - 1] = block


def spread_kernel(info_ref, off_ref, dst_ref, state_ref, *outs_and_scratch):
    outs, both_scr = outs_and_scratch[:-1], outs_and_scratch[-1]
    high, low = halves(state_ref[...])
    both_scr[0:16, :] = jnp.concatenate([high, low], axis=0)
    group = info_ref[1]
    each = dst_ref.shape[0] // len(outs)
    for d, out in enumerate(outs):
        owner = lax.rem(group + d, len(outs))

        def spread(i, carry):
            for j in range(8):
                b = owner * each + i * 8 + j
                aligned = (off_ref[0, b] >> 7) << 7
                hot = one_hot(dst_ref[pl.ds(b, 1), :], aligned)
                block = both_scr[:, pl.ds(pl.multiple_of(aligned, LANES), WINDOW)]
                got = jnp.dot(block, hot, preferred_element_type=F32)
                at = pl.ds(pl.multiple_of((i * 8 + j) * LANES, LANES), LANES)
                out[:, at] = got[0:8] + got[8:16]
            return carry

        lax.fori_loop(0, each // 8, spread, 0)


def prepare_kernel(
    cells_ref,
    weights_ref,
    radius_ref,
    temp_ref,
    velocity_ref,
    gas_temp_ref,
    dens_ref,
    vel_ref,
    species_ref,
    packed_ref,
    top_ref,
    bottom_ref,
    up_ref,
    down_ref,
    right_ref,
    left_ref,
):
    planes, rows = species_ref.shape[1:3]
    up_ref[...] = species_ref[:, planes - 2 : planes]
    down_ref[...] = species_ref[:, 0:2]
    right_ref[...] = species_ref[:, :, rows - 2 : rows]
    left_ref[...] = species_ref[:, :, 0:2]

    @pl.when(pl.program_id(0) == 0)
    def _():
        w = [weights_ref[c : c + 1, :] for c in range(8)]
        slots = cells_ref.shape[1]
        each = slots // 8
        packed_ref[0:1, 0:slots] = (w[4] + w[5]) + (w[6] + w[7])
        packed_ref[1:2, 0:slots] = (w[2] + w[3]) + (w[6] + w[7])
        packed_ref[2:3, 0:slots] = (w[1] + w[3]) + (w[5] + w[7])
        packed_ref[3:4, 0:slots] = radius_ref[...].reshape(1, -1)
        packed_ref[4:5, 0:slots] = temp_ref[...].reshape(1, -1)
        packed_ref[5:8, 0:slots] = velocity_ref[...]
        for i in range(8):
            first = cells_ref[0:1, i * each : (i + 1) * each]
            packed_ref[i : i + 1, slots : slots + each] = first.astype(F32)
        own = [gas_temp_ref, dens_ref, vel_ref.at[0], vel_ref.at[1], vel_ref.at[2],
               species_ref.at[0]]
        for f in range(6):
            top_ref[f, 0] = own[f][planes - 1]
            bottom_ref[f, 0] = own[f][0]


def assemble_kernel(packed_ref, lo_ref, temp_ref, dens_ref, vel_ref, fuel_ref, hi_ref, out_ref):
    start = packed_ref.shape[1]
    out_ref[:, 0:start] = packed_ref[...]
    planes, rows = temp_ref.shape[0:2]
    own = [temp_ref, dens_ref, vel_ref.at[0], vel_ref.at[1], vel_ref.at[2], fuel_ref.at[0]]
    for f in range(6):
        for x in range(planes + 2):
            if x == 0:
                plane = lo_ref.at[f, 0]
            elif x == planes + 1:
                plane = hi_ref.at[f, 0]
            else:
                plane = own[f].at[x - 1]
            for side, y in enumerate((0, rows - 1)):
                block, line = row_place(planes, f, x, side)
                at = start + block * LANES
                out_ref[line : line + 1, at : at + LANES] = plane[y : y + 1, :]


def row_place(planes, f, x, side):
    return divmod((f * (planes + 2) + x) * 2 + side, 8)


def transport_kernel(
    first_part,
    first_block,
    diff_ref,
    y_ref,
    xlo_ref,
    xhi_ref,
    ylo_ref,
    yhi_ref,
    ux_ref,
    dens_ref,
    *rest,
):
    if first_part:
        main_ref, below_ref, above_ref, out_ref, gas_ref, pad = rest

        @pl.when(pl.program_id(0) == 0)
        def _():
            last = main_ref.shape[1] - 1
            for k in range(main_ref.shape[0]):
                for x in range(last + 1):
                    total = main_ref[k, x]
                    if x == 0:
                        total = total + below_ref[k, 0]
                    if x == last:
                        total = total + above_ref[k, 0]
                    gas_ref[k, x] = total

        vap_ref = gas_ref.at[0]
    else:
        vap_ref, _, out_ref, pad = rest
    species, planes, rows, depth = y_ref.shape
    at = iota((rows, depth), 1)
    left1 = jnp.where(at >= 1, 16.0, 0.0)
    left2 = jnp.where(at >= 2, -1.0, 0.0)
    right1 = jnp.where(at < depth - 1, 16.0, 0.0)
    right2 = jnp.where(at < depth - 2, -1.0, 0.0)
    first = (first_block + pl.program_id(0)) * species
    for x in range(planes):
        speed = ux_ref[x] * (courant / 12.0)
        gain = source_coef * vap_ref[x] / dens_ref[x]

        for s in range(species):
            d12 = diff_ref[first + s] * (1.0 / 12.0)

            def plane(i, s=s):
                if i < 0:
                    return xlo_ref[s, i + 2]
                if i >= planes:
                    return xhi_ref[s, i - planes]
                return y_ref[s, i]

            center = plane(x)
            up1, up2, dn1, dn2 = plane(x + 1), plane(x + 2), plane(x - 1), plane(x - 2)
            pad[s, 6:8, :] = ylo_ref[s, x]
            pad[s, 8 : 8 + rows, :] = center
            pad[s, 8 + rows : 10 + rows, :] = yhi_ref[s, x]
            near = up1 + dn1 + pad[s, 7 : 7 + rows, :] + pad[s, 9 : 9 + rows, :]
            far = up2 + dn2 + pad[s, 6 : 6 + rows, :] + pad[s, 10 : 10 + rows, :]
            along = (
                left1 * pltpu.roll(center, 1, 1)
                + right1 * pltpu.roll(center, depth - 1, 1)
                + left2 * pltpu.roll(center, 2, 1)
                + right2 * pltpu.roll(center, depth - 2, 1)
            )
            slope = 8.0 * (up1 - dn1) - (up2 - dn2)
            flag = jnp.where(first + s == 0, 1.0, 0.0)
            laplace = 16.0 * near - far + along - 90.0 * center
            out_ref[s, x] = center + d12 * laplace - speed * slope + gain * (flag - center)


def per_device(
    species,
    diffusion,
    gas_temp,
    gas_density,
    gas_velocity,
    drop_radius,
    drop_temp,
    drop_velocity,
    parcel_cells,
    parcel_weights,
    parcel_counts,
):
    count_s = lax.axis_size("space")
    groups = lax.axis_size("group")
    planes, rows, depth = gas_temp.shape
    kinds = species.shape[0]
    capacity = drop_radius.shape[0]
    slots = capacity * groups
    blocks = slots // LANES
    ahead = [(i, i + 1) for i in range(count_s - 1)]
    back = [(b, a) for a, b in ahead]
    g_ahead = [(i, i + 1) for i in range(groups - 1)]
    g_back = [(b, a) for a, b in g_ahead]
    group = lax.axis_index("group")
    info = jnp.stack([parcel_counts[0], group.astype(jnp.int32)])

    whole = lambda shape: pl.BlockSpec(shape, lambda i, n=len(shape): (0,) * n)
    smem = pl.BlockSpec(memory_space=pltpu.SMEM)
    hbm = pl.BlockSpec(memory_space=pl.ANY)
    shaped = lambda *shape: jax.ShapeDtypeStruct(shape, F32)
    limit = pltpu.CompilerParams(vmem_limit_bytes=62 * 2**20)

    def by_kind(first, *shape):
        return pl.BlockSpec((MANY,) + shape, lambda i: (first + i, 0, 0, 0))

    packed, top, bottom, x_up, x_down, y_right, y_left = pl.pallas_call(
        prepare_kernel,
        grid=(kinds // MANY,),
        in_specs=[
            whole((8, capacity)),
            whole((8, capacity)),
            whole((capacity,)),
            whole((capacity,)),
            whole((3, capacity)),
            whole((planes, rows, depth)),
            whole((planes, rows, depth)),
            whole((3, planes, rows, depth)),
            by_kind(0, planes, rows, depth),
        ],
        out_specs=[
            whole((8, capacity // 8 * 9)),
            whole((6, 1, rows, depth)),
            whole((6, 1, rows, depth)),
            by_kind(0, 2, rows, depth),
            by_kind(0, 2, rows, depth),
            by_kind(0, planes, 2, depth),
            by_kind(0, planes, 2, depth),
        ],
        out_shape=[
            shaped(8, capacity // 8 * 9),
            shaped(6, 1, rows, depth),
            shaped(6, 1, rows, depth),
            shaped(kinds, 2, rows, depth),
            shaped(kinds, 2, rows, depth),
            shaped(kinds, planes, 2, depth),
            shaped(kinds, planes, 2, depth),
        ],
        compiler_params=limit,
        name="prepare",
    )(
        parcel_cells, parcel_weights, drop_radius, drop_temp, drop_velocity,
        gas_temp, gas_density, gas_velocity, species,
    )
    field_lo = lax.ppermute(top, "space", ahead)
    field_hi = lax.ppermute(bottom, "space", back)
    width = capacity // 8 * 9 + ROWS_WIDTH
    sent = pl.pallas_call(
        assemble_kernel,
        grid=(1,),
        in_specs=[
            whole((8, capacity // 8 * 9)),
            whole((6, 1, rows, depth)),
            whole((planes, rows, depth)),
            whole((planes, rows, depth)),
            whole((3, planes, rows, depth)),
            whole((1, planes, rows, depth)),
            whole((6, 1, rows, depth)),
        ],
        out_specs=whole((8, width)),
        out_shape=shaped(8, width),
        compiler_params=limit,
        name="assemble",
    )(packed, field_lo, gas_temp, gas_density, gas_velocity, species, field_hi)
    parcels = lax.all_gather(sent, "group", axis=0)

    x_up, x_down, y_right, y_left, parcels = lax.optimization_barrier(
        (x_up, x_down, y_right, y_left, parcels)
    )
    x_lo = lax.ppermute(x_up, "space", ahead)
    x_hi = lax.ppermute(x_down, "space", back)
    y_lo = lax.ppermute(y_right, "group", g_ahead)
    y_hi = lax.ppermute(y_left, "group", g_back)

    reach = slots + WINDOW
    main, dep_lo, dep_hi, state, dst, off = pl.pallas_call(
        parcel_kernel,
        grid=(1,),
        in_specs=[
            smem,
            whole((groups, 8, width)),
            whole((6, 1, rows, depth)),
            whole((planes, rows, depth)),
            whole((planes, rows, depth)),
            whole((3, planes, rows, depth)),
            whole((1, planes, rows, depth)),
            whole((6, 1, rows, depth)),
        ],
        out_specs=[
            whole((7, planes, rows, depth)),
            whole((7, 1, rows, depth)),
            whole((7, 1, rows, depth)),
            whole((8, reach)),
            whole((blocks, LANES)),
            whole((8, LANES)),
        ],
        out_shape=[
            shaped(7, planes, rows, depth),
            shaped(7, 1, rows, depth),
            shaped(7, 1, rows, depth),
            shaped(8, reach),
            shaped(blocks, LANES),
            jax.ShapeDtypeStruct((8, LANES), jnp.int32),
        ],
        scratch_shapes=[
            pltpu.VMEM((blocks, LANES), F32),
            pltpu.VMEM((blocks, LANES), F32),
            pltpu.SMEM((8, LANES), jnp.int32),
            pltpu.SemaphoreType.DMA,
            pltpu.VMEM((32, slots), BF16),
            pltpu.VMEM((16, reach), F32),
            pltpu.VMEM((256, LANES), F32),
            pltpu.VMEM((6 * LANES, 768), BF16),
            pltpu.VMEM((slots // CHUNK, 256, CHUNK), BF16),
            pltpu.VMEM((slots // CHUNK, 256, CHUNK), BF16),
            pltpu.VMEM((8, slots), F32),
            pltpu.VMEM((8, slots), F32),
            pltpu.VMEM((7 * LANES, 256), F32),
        ],
        compiler_params=limit,
        name="parcels",
    )(info, parcels, field_lo, gas_temp, gas_density, gas_velocity, species, field_hi)

    from_below = lax.ppermute(dep_hi, "space", ahead)
    from_above = lax.ppermute(dep_lo, "space", back)

    from_below, from_above, state = lax.optimization_barrier((from_below, from_above, state))
    spread = pl.pallas_call(
        spread_kernel,
        grid=(1,),
        in_specs=[smem, smem, whole((blocks, LANES)), whole((8, reach))],
        out_specs=[whole((8, capacity))] * groups,
        out_shape=[shaped(8, capacity)] * groups,
        scratch_shapes=[pltpu.VMEM((16, reach), BF16)],
        compiler_params=limit,
        name="spread",
    )(info, off, dst, state)
    new_state = spread[0]
    for d in range(1, groups):
        route = [(i, (i + d) % groups) for i in range(groups)]
        new_state = new_state + lax.ppermute(spread[d], "group", route)
    old_state = jnp.concatenate([drop_radius[None], drop_temp[None], drop_velocity], axis=0)
    slot = group * capacity + jnp.arange(capacity, dtype=jnp.int32)
    live = slot < parcel_counts[0]
    parcel_state = jnp.where(live[None], new_state[0:5], old_state)

    gas = pl.BlockSpec((planes, rows, depth), lambda i: (0, 0, 0))
    row0 = pl.BlockSpec((None, planes, rows, depth), lambda i: (0, 0, 0, 0))
    all_gas = whole((7, planes, rows, depth))
    rim = whole((7, 1, rows, depth))
    species_next = gas_sources = None
    at = 0
    for c, size in enumerate(PARTS):
        first = at // MANY
        at += size
        out_specs = [by_kind(first, planes, rows, depth)]
        out_shape = [shaped(*species.shape)]
        if c == 0:
            extra, extra_specs = (main, from_below, from_above), [all_gas, rim, rim]
            out_specs.append(all_gas)
            out_shape.append(shaped(7, planes, rows, depth))
        else:
            extra, extra_specs = (gas_sources, species_next), [row0, hbm]
        got = pl.pallas_call(
            functools.partial(transport_kernel, c == 0, first),
            grid=(size // MANY,),
            in_specs=[
                smem,
                by_kind(first, planes, rows, depth),
                by_kind(first, 2, rows, depth),
                by_kind(first, 2, rows, depth),
                by_kind(first, planes, 2, depth),
                by_kind(first, planes, 2, depth),
                row0,
                gas,
            ]
            + extra_specs,
            out_specs=out_specs,
            out_shape=out_shape,
            input_output_aliases={} if c == 0 else {9: 0},
            scratch_shapes=[pltpu.VMEM((MANY, rows + 16, depth), F32)],
            compiler_params=limit,
            name="transport",
        )(diffusion, species, x_lo, x_hi, y_lo, y_hi, gas_velocity, gas_density, *extra)
        species_next = got[0]
        if c == 0:
            gas_sources = got[1]
    return (species_next, gas_sources, parcel_state)


def solution(mesh):
    in_specs = (
        P(None, "space", "group", None),
        P(),
        P("space", "group", None),
        P("space", "group", None),
        P(None, "space", "group", None),
        P(("space", "group")),
        P(("space", "group")),
        P(None, ("space", "group")),
        P(None, ("space", "group")),
        P(None, ("space", "group")),
        P("space"),
    )
    out_specs = (
        P(None, "space", "group", None),
        P(None, "space", "group", None),
        P(None, ("space", "group")),
    )
    return jax.shard_map(
        per_device, mesh=mesh, in_specs=in_specs, out_specs=out_specs, check_vma=False
    )
```

profile of v0, /device:TPU:103, one launch (start us, length us, event | category | flops | bytes accessed | tf_op | source)
XLA Modules:
  0.0 118.9 jit_solution(1962267329941115142)
XLA Ops:
  0.6 5.2 %prepare.1 = (f32[8,4608]{1,0:T(8,128)}, f32[6,1,32,128]{3,2,1,0:T(8,128)}, f32[6,1,32,128]{3,2,1,0:T(8,128)}, f32[54,2,32,128]{3,2,1,0:T(8,128)}, f32[54,2,32,1...) custom-call(s32[8,4096]{1,0:T(8,128)} %cells_ref.1, f32[8,4096]{1,0:T(8,128)} %weights_ref.1, ...), custom_call_target="tpu_custom_call" | custom-call | tf_op jit(solution)/shard_map/prepare/pallas_call | solution.py:475
  5.9 4.7 %collective-permute-start = (f32[6,1,32,128]{3,2,1,0:T(8,128)}, f32[6,1,32,128]{3,2,1,0:T(8,128)S(1)}, u32[]{:S(2)}, u32[]{:S(2)}) collective-permute-start(f32[6,1,32,128]{3,2,1,0:T(8,128)} %get-tuple-element.35), channel_id=1, source_target_pairs={{0,4},{4,8},{8,12},{12,16},{16,20},{20,24},{24,28},{28,32},{32,36}... | collective-permute-start | bytes 294920 | tf_op jit(solution)/shard_map/ppermute | solution.py:513
  10.5 1.9 %collective-permute-start.1 = (f32[6,1,32,128]{3,2,1,0:T(8,128)}, f32[6,1,32,128]{3,2,1,0:T(8,128)S(1)}, u32[]{:S(2)}, u32[]{:S(2)}) collective-permute-start(f32[6,1,32,128]{3,2,1,0:T(8,128)} %get-tuple-element.36), channel_id=1, source_target_pairs={{4,0},{8,4},{12,8},{16,12},{20,16},{24,20},{28,24},{32,28},{36,32}... | collective-permute-start | bytes 294920 | tf_op jit(solution)/shard_map/ppermute | solution.py:514
  12.5 0.0 collective-permute-done.lo_ref
  12.5 0.0 copy-start.1
  12.5 6.9 %collective-permute-done.1.hi_ref = f32[6,1,32,128]{3,2,1,0:T(8,128)S(1)} collective-permute-done((f32[6,1,32,128]{3,2,1,0:T(8,128)}, f32[6,1,32,128]{3,2,1,0:T(8,128)S(1)}, u32[]{:S(2)}, u32[]{:S(2)}) %collective-permute-start.1) | collective-permute-done | bytes 98336 | tf_op jit(solution)/shard_map/ppermute | solution.py:514
  19.4 0.0 copy-start.2
  19.4 0.0 copy-done.1
  19.4 0.6 copy-done.2
  20.1 1.9 %assemble.1 = f32[8,5760]{1,0:T(8,128)} custom-call(f32[8,4608]{1,0:T(8,128)} %get-tuple-element.34.packed_ref, f32[6,1,32,128]{3,2,1,0:T(8,128)} %copy-done.1, f32[4,32,128]{2,1,0:T(8,128)} %temp_ref.5, f32[4,32,128]{2,1,0:T(8,128)} %dens_ref.7, f32[3,4,32,128]{3,2,1,0:T(8,128)} %ux_ref.1, f32[54,4,32,128]{3,2,1,0:T(8,128)} %y_ref.1, ...), custom_call_target="tpu_custom_call" | custom-call | tf_op jit(solution)/shard_map/assemble/pallas_call | solution.py:516
  22.0 12.6 %all-gather = f32[32,5760]{1,0:T(8,128)} all-gather(f32[8,5760]{1,0:T(8,128)} %assemble.1), channel_id=2, replica_groups=mesh['space'=64,'group'=4] {'group'}, dimensions={0}, use_global_device_ids=true | all-gather | bytes 921600 | tf_op jit(solution)/shard_map/all_gather | solution.py:533
  34.6 1.9 %collective-permute-start.2 = (f32[54,2,32,128]{3,2,1,0:T(8,128)}, f32[54,2,32,128]{3,2,1,0:T(8,128)S(1)}, u32[]{:S(2)}, u32[]{:S(2)}) collective-permute-start(f32[54,2,32,128]{3,2,1,0:T(8,128)} %get-tuple-element.37), channel_id=1, source_target_pairs={{0,4},{4,8},{8,12},{12,16},{16,20},{20,24},{24,28},{28,32},{32,36}... | collective-permute-start | bytes 5308424 | tf_op jit(solution)/shard_map/ppermute | solution.py:538
  36.5 3.4 %collective-permute-start.3 = (f32[54,2,32,128]{3,2,1,0:T(8,128)}, f32[54,2,32,128]{3,2,1,0:T(8,128)}, u32[]{:S(2)}, u32[]{:S(2)}) collective-permute-start(f32[54,2,32,128]{3,2,1,0:T(8,128)} %get-tuple-element.38), channel_id=1, source_target_pairs={{4,0},{8,4},{12,8},{16,12},{20,16},{24,20},{28,24},{32,28},{36,32}... | collective-permute-start | bytes 5308424 | tf_op jit(solution)/shard_map/ppermute | solution.py:539
  40.6 0.7 pad_add_fusion.info_ref
  41.2 0.0 copy-start.3
  41.2 0.0 copy-start.7
  41.2 0.0 copy-start.8
  41.2 21.4 %parcels.1 = (f32[7,4,32,128]{3,2,1,0:T(8,128)}, f32[7,1,32,128]{3,2,1,0:T(8,128)}, f32[7,1,32,128]{3,2,1,0:T(8,128)}, f32[8,16640]{1,0:T(8,128)}, f32[128,128]{1,0:T(8,128)}, /*index=5*/s32[8,128]{1,0:T(8,128)}) custom-call(s32[2]{0:T(128)} %pad_add_fusion.info_ref, f32[4,8,5760]{2,1,0:T(8,128)} %bitcast.6, f32[6,1,32,128]{3,2,1,0:T(8,128)} %copy-done.1, ...), custom_call_target="tpu_custom_call" | custom-call | tf_op jit(solution)/shard_map/parcels/pallas_call | solution.py:544
  62.6 7.0 %collective-permute-start.6 = (f32[7,1,32,128]{3,2,1,0:T(8,128)}, f32[7,1,32,128]{3,2,1,0:T(8,128)S(1)}, u32[]{:S(2)}, u32[]{:S(2)}) collective-permute-start(f32[7,1,32,128]{3,2,1,0:T(8,128)} %get-tuple-element.43), channel_id=1, source_target_pairs={{0,4},{4,8},{8,12},{12,16},{16,20},{20,24},{24,28},{28,32},{32,36}... | collective-permute-start | bytes 344072 | tf_op jit(solution)/shard_map/ppermute | solution.py:592
  69.6 1.9 %collective-permute-start.7 = (f32[7,1,32,128]{3,2,1,0:T(8,128)}, f32[7,1,32,128]{3,2,1,0:T(8,128)}, u32[]{:S(2)}, u32[]{:S(2)}) collective-permute-start(f32[7,1,32,128]{3,2,1,0:T(8,128)} %get-tuple-element.44), channel_id=1, source_target_pairs={{4,0},{8,4},{12,8},{16,12},{20,16},{24,20},{28,24},{32,28},{36,32}... | collective-permute-start | bytes 344072 | tf_op jit(solution)/shard_map/ppermute | solution.py:593
  71.6 7.8 %collective-permute-done.6.rest_1_ = f32[7,1,32,128]{3,2,1,0:T(8,128)S(1)} collective-permute-done((f32[7,1,32,128]{3,2,1,0:T(8,128)}, f32[7,1,32,128]{3,2,1,0:T(8,128)S(1)}, u32[]{:S(2)}, u32[]{:S(2)}) %collective-permute-start.6) | collective-permute-done | bytes 114720 | tf_op jit(solution)/shard_map/ppermute | solution.py:592
  79.3 0.0 copy-start.6
  79.3 5.2 %collective-permute-done.7.rest_2_ = f32[7,1,32,128]{3,2,1,0:T(8,128)} collective-permute-done((f32[7,1,32,128]{3,2,1,0:T(8,128)}, f32[7,1,32,128]{3,2,1,0:T(8,128)}, u32[]{:S(2)}, u32[]{:S(2)}) %collective-permute-start.7) | collective-permute-done | bytes 114720 | tf_op jit(solution)/shard_map/ppermute | solution.py:593
  84.6 5.0 %spread.1 = (f32[8,4096]{1,0:T(8,128)}, f32[8,4096]{1,0:T(8,128)}, f32[8,4096]{1,0:T(8,128)}, f32[8,4096]{1,0:T(8,128)}) custom-call(s32[2]{0:T(128)} %pad_add_fusion.info_ref, s32[8,128]{1,0:T(8,128)} %get-tuple-element.50.off_ref, f32[128,128]{1,0:T(8,128)} %get-tuple-element.51.dst_ref, f32[8,16640]{1,0:T(8,128)} %get-tuple-element.52.state_ref), custom_call_target="tpu_custom_call" | custom-call | tf_op jit(solution)/shard_map/spread/pallas_call | solution.py:596
  89.6 2.3 %collective-permute-start.8 = (f32[8,4096]{1,0:T(8,128)}, f32[8,4096]{1,0:T(8,128)S(1)}, u32[]{:S(2)}, u32[]{:S(2)}) collective-permute-start(f32[8,4096]{1,0:T(8,128)} %get-tuple-element.54), channel_id=1, source_target_pairs={{0,1},{1,2},{2,3},{3,0},{4,5},{5,6},{6,7},{7,4},{8,9},{9,10},{10,1... | collective-permute-start | bytes 393224 | tf_op jit(solution)/shard_map/ppermute | solution.py:609
  91.9 1.5 %collective-permute-start.9 = (f32[8,4096]{1,0:T(8,128)}, f32[8,4096]{1,0:T(8,128)S(1)}, u32[]{:S(2)}, u32[]{:S(2)}) collective-permute-start(f32[8,4096]{1,0:T(8,128)} %get-tuple-element.55), channel_id=1, source_target_pairs={{0,2},{1,3},{2,0},{3,1},{4,6},{5,7},{6,4},{7,5},{8,10},{9,11},{10,... | collective-permute-start | bytes 393224 | tf_op jit(solution)/shard_map/ppermute | solution.py:609
  93.4 0.0 collective-permute-start.10
  93.4 1.6 %collective-permute-done.8 = f32[8,4096]{1,0:T(8,128)S(1)} collective-permute-done((f32[8,4096]{1,0:T(8,128)}, f32[8,4096]{1,0:T(8,128)S(1)}, u32[]{:S(2)}, u32[]{:S(2)}) %collective-permute-start.8) | collective-permute-done | bytes 131104 | tf_op jit(solution)/shard_map/ppermute | solution.py:609
  95.0 5.8 %collective-permute-start.4 = (f32[54,4,2,128]{3,2,1,0:T(2,128)}, f32[54,4,2,128]{3,2,1,0:T(2,128)S(1)}, u32[]{:S(2)}, u32[]{:S(2)}) collective-permute-start(f32[54,4,2,128]{3,2,1,0:T(2,128)} %get-tuple-element.39), channel_id=1, source_target_pairs={{0,1},{1,2},{2,3},{4,5},{5,6},{6,7},{8,9},{9,10},{10,11},{12,13},{... | collective-permute-start | bytes 663560 | tf_op jit(solution)/shard_map/ppermute | solution.py:540
  100.8 0.0 collective-permute-done.9
  100.8 1.9 %collective-permute-start.5 = (f32[54,4,2,128]{3,2,1,0:T(2,128)}, f32[54,4,2,128]{3,2,1,0:T(2,128)S(1)}, u32[]{:S(2)}, u32[]{:S(2)}) collective-permute-start(f32[54,4,2,128]{3,2,1,0:T(2,128)} %get-tuple-element.40), channel_id=1, source_target_pairs={{1,0},{2,1},{3,2},{5,4},{6,5},{7,6},{9,8},{10,9},{11,10},{13,12},{... | collective-permute-start | bytes 663560 | tf_op jit(solution)/shard_map/ppermute | solution.py:541
  102.7 0.0 collective-permute-done.10
  102.7 0.0 copy-done.3
  102.7 0.0 copy-done.7
  102.7 0.0 copy-done.8
  102.8 1.6 %fusion = f32[5,4096]{1,0:T(8,128)} fusion(f32[8,4096]{1,0:T(8,128)S(1)} %collective-permute-done.10, f32[8,4096]{1,0:T(8,128)S(1)} %collective-permute-done.9, f32[8,4096]{1,0:T(8,128)S(1)} %collective-permute-done.8, f32[8,4096]{1,0:T(8,128)} %get-tuple-element.53, f32[3,4096]{1,0:T(4,128)S(1)} %copy-done.3, f32[1,4096]{1,0:T(1,128)S(1)} %bitcast.8, ...), kind=kLoop, calls=%fused_computation.1 | loop fusion | flops 122880 | bytes 495616 | tf_op jit(solution)/shard_map/jit(_where)/select_n | solution.py:613
  104.4 0.0 collective-permute-done.4.ylo_ref
  104.4 0.0 copy-start.4
  104.4 5.4 %collective-permute-done.5.yhi_ref = f32[54,4,2,128]{3,2,1,0:T(2,128)S(1)} collective-permute-done((f32[54,4,2,128]{3,2,1,0:T(2,128)}, f32[54,4,2,128]{3,2,1,0:T(2,128)S(1)}, u32[]{:S(2)}, u32[]{:S(2)}) %collective-permute-start.5) | collective-permute-done | bytes 221216 | tf_op jit(solution)/shard_map/ppermute | solution.py:541
  109.8 0.0 copy-start.5
  109.8 0.0 collective-permute-done.2.xlo_ref
  109.8 0.0 copy-done.4
  109.8 0.0 copy-start
  109.8 0.0 collective-permute-done.3.xhi_ref
  109.8 0.7 copy-done.5
  110.4 0.0 copy-done.6
  110.4 0.6 copy-done
  111.1 7.8 %transport.1 = (f32[54,4,32,128]{3,2,1,0:T(8,128)}, f32[7,4,32,128]{3,2,1,0:T(8,128)}) custom-call(f32[54]{0:T(128)} %diff_ref.1, f32[54,4,32,128]{3,2,1,0:T(8,128)} %y_ref.1, f32[54,2,32,128]{3,2,1,0:T(8,128)} %copy-done, f32[54,2,32,128]{3,2,1,0:T(8,128)} %collective-permute-done.3.xhi_ref, f32[54,4,2,128]{3,2,1,0:T(2,128)} %copy-done.4, ...), custom_call_target="tpu_custom_call" | custom-call | tf_op jit(solution)/shard_map/transport/pallas_call | solution.py:632
  (1 shorter events, 0.0 us)
Async XLA Ops:
  5.9 6.6 %collective-permute-start = (f32[6,1,32,128]{3,2,1,0:T(8,128)}, f32[6,1,32,128]{3,2,1,0:T(8,128)S(1)}, u32[]{:S(2)}, u32[]{:S(2)}) collective-permute-start(f32[6,1,32,128]{3,2,1,0:T(8,128)} %get-tuple-element.35), channel_id=1, source_target_pairs={{0,4},{4,8},{8,12},{12,16},{16,20},{20,24},{24,28},{28,32},{32,36}... | collective-permute-start | bytes 294920 | tf_op jit(solution)/shard_map/ppermute | solution.py:513
  10.5 8.9 %collective-permute-start.1 = (f32[6,1,32,128]{3,2,1,0:T(8,128)}, f32[6,1,32,128]{3,2,1,0:T(8,128)S(1)}, u32[]{:S(2)}, u32[]{:S(2)}) collective-permute-start(f32[6,1,32,128]{3,2,1,0:T(8,128)} %get-tuple-element.36), channel_id=1, source_target_pairs={{4,0},{8,4},{12,8},{16,12},{20,16},{24,20},{28,24},{32,28},{36,32}... | collective-permute-start | bytes 294920 | tf_op jit(solution)/shard_map/ppermute | solution.py:514
  12.5 7.0 %copy-start.1 = (f32[6,1,32,128]{3,2,1,0:T(8,128)}, f32[6,1,32,128]{3,2,1,0:T(8,128)S(1)}, u32[]{:S(2)}) copy-start(f32[6,1,32,128]{3,2,1,0:T(8,128)S(1)} %collective-permute-done.lo_ref) | copy-start | bytes 294916
  19.4 0.6 copy-start.2
  34.6 75.1 %collective-permute-start.2 = (f32[54,2,32,128]{3,2,1,0:T(8,128)}, f32[54,2,32,128]{3,2,1,0:T(8,128)S(1)}, u32[]{:S(2)}, u32[]{:S(2)}) collective-permute-start(f32[54,2,32,128]{3,2,1,0:T(8,128)} %get-tuple-element.37), channel_id=1, source_target_pairs={{0,4},{4,8},{8,12},{12,16},{16,20},{20,24},{24,28},{28,32},{32,36}... | collective-permute-start | bytes 5308424 | tf_op jit(solution)/shard_map/ppermute | solution.py:538
  36.5 73.2 %collective-permute-start.3 = (f32[54,2,32,128]{3,2,1,0:T(8,128)}, f32[54,2,32,128]{3,2,1,0:T(8,128)}, u32[]{:S(2)}, u32[]{:S(2)}) collective-permute-start(f32[54,2,32,128]{3,2,1,0:T(8,128)} %get-tuple-element.38), channel_id=1, source_target_pairs={{4,0},{8,4},{12,8},{16,12},{20,16},{24,20},{28,24},{32,28},{36,32}... | collective-permute-start | bytes 5308424 | tf_op jit(solution)/shard_map/ppermute | solution.py:539
  41.2 61.5 %copy-start.3 = (f32[3,4096]{1,0:T(4,128)S(1)}, f32[3,4096]{1,0:T(4,128)}, u32[]{:S(2)}) copy-start(f32[3,4096]{1,0:T(4,128)} %velocity_ref.1) | copy-start | bytes 147460
  41.2 61.5 %copy-start.7 = (f32[4096]{0:T(1024)S(1)}, f32[4096]{0:T(1024)}, u32[]{:S(2)}) copy-start(f32[4096]{0:T(1024)} %radius_ref.1) | copy-start | bytes 49156
  41.2 61.5 %copy-start.8 = (f32[4096]{0:T(1024)S(1)}, f32[4096]{0:T(1024)}, u32[]{:S(2)}) copy-start(f32[4096]{0:T(1024)} %temp_ref.3) | copy-start | bytes 49156
  62.6 16.7 %collective-permute-start.6 = (f32[7,1,32,128]{3,2,1,0:T(8,128)}, f32[7,1,32,128]{3,2,1,0:T(8,128)S(1)}, u32[]{:S(2)}, u32[]{:S(2)}) collective-permute-start(f32[7,1,32,128]{3,2,1,0:T(8,128)} %get-tuple-element.43), channel_id=1, source_target_pairs={{0,4},{4,8},{8,12},{12,16},{16,20},{20,24},{24,28},{28,32},{32,36}... | collective-permute-start | bytes 344072 | tf_op jit(solution)/shard_map/ppermute | solution.py:592
  69.6 14.9 %collective-permute-start.7 = (f32[7,1,32,128]{3,2,1,0:T(8,128)}, f32[7,1,32,128]{3,2,1,0:T(8,128)}, u32[]{:S(2)}, u32[]{:S(2)}) collective-permute-start(f32[7,1,32,128]{3,2,1,0:T(8,128)} %get-tuple-element.44), channel_id=1, source_target_pairs={{4,0},{8,4},{12,8},{16,12},{20,16},{24,20},{28,24},{32,28},{36,32}... | collective-permute-start | bytes 344072 | tf_op jit(solution)/shard_map/ppermute | solution.py:593
  79.3 31.1 %copy-start.6 = (f32[7,1,32,128]{3,2,1,0:T(8,128)}, f32[7,1,32,128]{3,2,1,0:T(8,128)S(1)}, u32[]{:S(2)}) copy-start(f32[7,1,32,128]{3,2,1,0:T(8,128)S(1)} %collective-permute-done.6.rest_1_) | copy-start | bytes 344068
  89.6 5.4 %collective-permute-start.8 = (f32[8,4096]{1,0:T(8,128)}, f32[8,4096]{1,0:T(8,128)S(1)}, u32[]{:S(2)}, u32[]{:S(2)}) collective-permute-start(f32[8,4096]{1,0:T(8,128)} %get-tuple-element.54), channel_id=1, source_target_pairs={{0,1},{1,2},{2,3},{3,0},{4,5},{5,6},{6,7},{7,4},{8,9},{9,10},{10,1... | collective-permute-start | bytes 393224 | tf_op jit(solution)/shard_map/ppermute | solution.py:609
  91.9 8.9 %collective-permute-start.9 = (f32[8,4096]{1,0:T(8,128)}, f32[8,4096]{1,0:T(8,128)S(1)}, u32[]{:S(2)}, u32[]{:S(2)}) collective-permute-start(f32[8,4096]{1,0:T(8,128)} %get-tuple-element.55), channel_id=1, source_target_pairs={{0,2},{1,3},{2,0},{3,1},{4,6},{5,7},{6,4},{7,5},{8,10},{9,11},{10,... | collective-permute-start | bytes 393224 | tf_op jit(solution)/shard_map/ppermute | solution.py:609
  93.4 9.3 %collective-permute-start.10 = (f32[8,4096]{1,0:T(8,128)}, f32[8,4096]{1,0:T(8,128)S(1)}, u32[]{:S(2)}, u32[]{:S(2)}) collective-permute-start(f32[8,4096]{1,0:T(8,128)} %get-tuple-element.56), channel_id=1, source_target_pairs={{0,3},{1,0},{2,1},{3,2},{4,7},{5,4},{6,5},{7,6},{8,11},{9,8},{10,9... | collective-permute-start | bytes 393224 | tf_op jit(solution)/shard_map/ppermute | solution.py:609
  95.0 9.4 %collective-permute-start.4 = (f32[54,4,2,128]{3,2,1,0:T(2,128)}, f32[54,4,2,128]{3,2,1,0:T(2,128)S(1)}, u32[]{:S(2)}, u32[]{:S(2)}) collective-permute-start(f32[54,4,2,128]{3,2,1,0:T(2,128)} %get-tuple-element.39), channel_id=1, source_target_pairs={{0,1},{1,2},{2,3},{4,5},{5,6},{6,7},{8,9},{9,10},{10,11},{12,13},{... | collective-permute-start | bytes 663560 | tf_op jit(solution)/shard_map/ppermute | solution.py:540
  100.8 9.0 %collective-permute-start.5 = (f32[54,4,2,128]{3,2,1,0:T(2,128)}, f32[54,4,2,128]{3,2,1,0:T(2,128)S(1)}, u32[]{:S(2)}, u32[]{:S(2)}) collective-permute-start(f32[54,4,2,128]{3,2,1,0:T(2,128)} %get-tuple-element.40), channel_id=1, source_target_pairs={{1,0},{2,1},{3,2},{5,4},{6,5},{7,6},{9,8},{10,9},{11,10},{13,12},{... | collective-permute-start | bytes 663560 | tf_op jit(solution)/shard_map/ppermute | solution.py:541
  104.4 5.4 %copy-start.4 = (f32[54,4,2,128]{3,2,1,0:T(2,128)}, f32[54,4,2,128]{3,2,1,0:T(2,128)S(1)}, u32[]{:S(2)}) copy-start(f32[54,4,2,128]{3,2,1,0:T(2,128)S(1)} %collective-permute-done.4.ylo_ref) | copy-start | bytes 663556
  109.8 0.7 copy-start.5
  109.8 1.3 %copy-start = (f32[54,2,32,128]{3,2,1,0:T(8,128)}, f32[54,2,32,128]{3,2,1,0:T(8,128)S(1)}, u32[]{:S(2)}) copy-start(f32[54,2,32,128]{3,2,1,0:T(8,128)S(1)} %collective-permute-done.2.xlo_ref) | copy-start | bytes 5308420
where the time goes:
time: 119 us
  Pallas kernels  41.4 us (35%)
  starting transfers between devices  32.3 us (27%)
  waiting for transfers between devices  26.9 us (23%)
  blocking collectives  12.6 us (11%)
  other arithmetic  2.3 us (2%)
  local copies, waits for them, and re-layouts  1.95 us (2%)
  between operations  1.44 us (1%)
    pallas_call x1, Pallas kernels, per_device(): pl.pallas_call(parcel_kernel, grid=(1,), in_specs=[smem, whole((groups, 8...  21.4 us
    all_gather x1, blocking collectives, per_device(): parcels = lax.all_gather(sent, 'group', axis=0)  12.6 us
    pallas_call x1, Pallas kernels, per_device(): pl.pallas_call(functools.partial(transport_kernel, c == 0, first), grid=(...  7.84 us
    ppermute x1, waiting for transfers between devices, per_device(): from_below = lax.ppermute(dep_hi, 'space', ahead)  7.76 us
    ppermute x1, starting transfers between devices, per_device(): from_below = lax.ppermute(dep_hi, 'space', ahead)  7 us
    ppermute x1, waiting for transfers between devices, per_device(): field_hi = lax.ppermute(bottom, 'space', back)  6.94 us
    ppermute x1, starting transfers between devices, per_device(): y_lo = lax.ppermute(y_right, 'group', g_ahead)  5.78 us
    ppermute x1, waiting for transfers between devices, per_device(): y_hi = lax.ppermute(y_left, 'group', g_back)  5.36 us
  transfers between devices with their start and end apart: 11, of which 5 were waited for; matrix products, arithmetic and copies ran while one was open for 2% of the time, Pallas kernels for 22%

commit v1 on v0

--- a/solution.py
+++ b/solution.py
@@ -18,7 +18,7 @@
 LANES = 128
 PARTS = (54,)
 MANY = 18
-CHUNK = 512
+CHUNK = 1024
 PHYS = 1024
 WINDOW = 256
 YPAD = 40
@@ -538,7 +538,6 @@
     x_lo = lax.ppermute(x_up, "space", ahead)
     x_hi = lax.ppermute(x_down, "space", back)
     y_lo = lax.ppermute(y_right, "group", g_ahead)
-    y_hi = lax.ppermute(y_left, "group", g_back)
 
     reach = slots + WINDOW
     main, dep_lo, dep_hi, state, dst, off = pl.pallas_call(
@@ -592,7 +591,6 @@
     from_below = lax.ppermute(dep_hi, "space", ahead)
     from_above = lax.ppermute(dep_lo, "space", back)
 
-    from_below, from_above, state = lax.optimization_barrier((from_below, from_above, state))
     spread = pl.pallas_call(
         spread_kernel,
         grid=(1,),
@@ -603,15 +601,15 @@
         compiler_params=limit,
         name="spread",
     )(info, off, dst, state)
-    new_state = spread[0]
+    y_lo, y_left, spread = lax.optimization_barrier((y_lo, y_left, spread))
+    y_hi = lax.ppermute(y_left, "group", g_back)
+    y_lo, y_hi, from_below, from_above, spread = lax.optimization_barrier(
+        (y_lo, y_hi, from_below, from_above, spread)
+    )
+    returned = [spread[0]]
     for d in range(1, groups):
         route = [(i, (i + d) % groups) for i in range(groups)]
-        new_state = new_state + lax.ppermute(spread[d], "group", route)
-    old_state = jnp.concatenate([drop_radius[None], drop_temp[None], drop_velocity], axis=0)
-    slot = group * capacity + jnp.arange(capacity, dtype=jnp.int32)
-    live = slot < parcel_counts[0]
-    parcel_state = jnp.where(live[None], new_state[0:5], old_state)
-
+        returned.append(lax.ppermute(spread[d], "group", route))
     gas = pl.BlockSpec((planes, rows, depth), lambda i: (0, 0, 0))
     row0 = pl.BlockSpec((None, planes, rows, depth), lambda i: (0, 0, 0, 0))
     all_gas = whole((7, planes, rows, depth))
@@ -653,6 +651,12 @@
         species_next = got[0]
         if c == 0:
             gas_sources = got[1]
+    species_next, returned = lax.optimization_barrier((species_next, returned))
+    new_state = sum(returned[1:], returned[0])
+    old_state = jnp.concatenate([drop_radius[None], drop_temp[None], drop_velocity], axis=0)
+    slot = group * capacity + jnp.arange(capacity, dtype=jnp.int32)
+    live = slot < parcel_counts[0]
+    parcel_state = jnp.where(live[None], new_state[0:5], old_state)
     return (species_next, gas_sources, parcel_state)
 
 

time: 119 us -> 104 us (0.87)
  the two profiles are of different devices: /device:TPU:103 before, /device:TPU:25 now
where the time goes in v1:
time: 104 us; the launch traced here: 105 us
  starting transfers between devices  42.8 us (41%)
  Pallas kernels  41.6 us (40%)
  blocking collectives  10.6 us (10%)
  waiting for transfers between devices  4.04 us (4%)
  other arithmetic  2.38 us (2%)
  local copies, waits for them, and re-layouts  1.9 us (2%)
  between operations  1.44 us (1%)
    pallas_call x1, Pallas kernels, per_device(): pl.pallas_call(parcel_kernel, grid=(1,), in_specs=[smem, whole((groups, 8...  21.5 us
    all_gather x1, blocking collectives, per_device(): parcels = lax.all_gather(sent, 'group', axis=0)  10.6 us
    ppermute x1, starting transfers between devices, per_device(): field_hi = lax.ppermute(bottom, 'space', back)  8.66 us
    ppermute x1, starting transfers between devices, per_device(): x_hi = lax.ppermute(x_down, 'space', back)  8.15 us
    pallas_call x1, Pallas kernels, per_device(): pl.pallas_call(functools.partial(transport_kernel, c == 0, first), grid=(...  7.95 us
    ppermute x1, starting transfers between devices, per_device(): from_above = lax.ppermute(dep_lo, 'space', back)  7.58 us
    ppermute x3, starting transfers between devices, per_device(): returned.append(lax.ppermute(spread[d], 'group', route))  6.49 us
    pallas_call x1, Pallas kernels, per_device(): pl.pallas_call(prepare_kernel, grid=(kinds // MANY,), in_specs=[whole((8,...  5.23 us
  transfers between devices with their start and end apart: 11, of which 4 were waited for; matrix products, arithmetic and copies ran while one was open for 1% of the time, Pallas kernels for 33%

profile of v1, /device:TPU:25, one launch (start us, length us, event | category | flops | bytes accessed | tf_op | source)
XLA Modules:
  0.0 104.8 jit_solution(13029306207182717372)
XLA Ops:
  0.6 5.2 %prepare.1 = (f32[8,4608]{1,0:T(8,128)}, f32[6,1,32,128]{3,2,1,0:T(8,128)}, f32[6,1,32,128]{3,2,1,0:T(8,128)}, f32[54,2,32,128]{3,2,1,0:T(8,128)}, f32[54,2,32,1...) custom-call(s32[8,4096]{1,0:T(8,128)} %cells_ref.1, f32[8,4096]{1,0:T(8,128)} %weights_ref.1, ...), custom_call_target="tpu_custom_call" | custom-call | tf_op jit(solution)/shard_map/prepare/pallas_call | solution.py:475
  5.9 3.1 %collective-permute-start = (f32[6,1,32,128]{3,2,1,0:T(8,128)}, f32[6,1,32,128]{3,2,1,0:T(8,128)S(1)}, u32[]{:S(2)}, u32[]{:S(2)}) collective-permute-start(f32[6,1,32,128]{3,2,1,0:T(8,128)} %get-tuple-element.51), channel_id=1, source_target_pairs={{0,4},{4,8},{8,12},{12,16},{16,20},{20,24},{24,28},{28,32},{32,36}... | collective-permute-start | bytes 294920 | tf_op jit(solution)/shard_map/ppermute | solution.py:513
  9.0 8.7 %collective-permute-start.1 = (f32[6,1,32,128]{3,2,1,0:T(8,128)}, f32[6,1,32,128]{3,2,1,0:T(8,128)S(1)}, u32[]{:S(2)}, u32[]{:S(2)}) collective-permute-start(f32[6,1,32,128]{3,2,1,0:T(8,128)} %get-tuple-element.52), channel_id=1, source_target_pairs={{4,0},{8,4},{12,8},{16,12},{20,16},{24,20},{28,24},{32,28},{36,32}... | collective-permute-start | bytes 294920 | tf_op jit(solution)/shard_map/ppermute | solution.py:514
  17.6 0.8 collective-permute-done.lo_ref
  18.4 0.0 copy-start.1
  18.4 1.1 %collective-permute-done.1.hi_ref = f32[6,1,32,128]{3,2,1,0:T(8,128)S(1)} collective-permute-done((f32[6,1,32,128]{3,2,1,0:T(8,128)}, f32[6,1,32,128]{3,2,1,0:T(8,128)S(1)}, u32[]{:S(2)}, u32[]{:S(2)}) %collective-permute-start.1) | collective-permute-done | bytes 98336 | tf_op jit(solution)/shard_map/ppermute | solution.py:514
  19.6 0.0 copy-start.2
  19.6 0.0 copy-done.1
  19.6 0.6 copy-done.2
  20.2 1.9 %assemble.1 = f32[8,5760]{1,0:T(8,128)} custom-call(f32[8,4608]{1,0:T(8,128)} %get-tuple-element.50.packed_ref, f32[6,1,32,128]{3,2,1,0:T(8,128)} %copy-done.1, f32[4,32,128]{2,1,0:T(8,128)} %temp_ref.5, f32[4,32,128]{2,1,0:T(8,128)} %dens_ref.7, f32[3,4,32,128]{3,2,1,0:T(8,128)} %ux_ref.1, f32[54,4,32,128]{3,2,1,0:T(8,128)} %y_ref.1, ...), custom_call_target="tpu_custom_call" | custom-call | tf_op jit(solution)/shard_map/assemble/pallas_call | solution.py:516
  22.2 10.6 %all-gather = f32[32,5760]{1,0:T(8,128)} all-gather(f32[8,5760]{1,0:T(8,128)} %assemble.1), channel_id=2, replica_groups=mesh['space'=64,'group'=4] {'group'}, dimensions={0}, use_global_device_ids=true | all-gather | bytes 921600 | tf_op jit(solution)/shard_map/all_gather | solution.py:533
  32.8 1.9 %collective-permute-start.2 = (f32[54,2,32,128]{3,2,1,0:T(8,128)}, f32[54,2,32,128]{3,2,1,0:T(8,128)S(1)}, u32[]{:S(2)}, u32[]{:S(2)}) collective-permute-start(f32[54,2,32,128]{3,2,1,0:T(8,128)} %get-tuple-element.53), channel_id=1, source_target_pairs={{0,4},{4,8},{8,12},{12,16},{16,20},{20,24},{24,28},{28,32},{32,36}... | collective-permute-start | bytes 5308424 | tf_op jit(solution)/shard_map/ppermute | solution.py:538
  34.7 8.1 %collective-permute-start.3 = (f32[54,2,32,128]{3,2,1,0:T(8,128)}, f32[54,2,32,128]{3,2,1,0:T(8,128)}, u32[]{:S(2)}, u32[]{:S(2)}) collective-permute-start(f32[54,2,32,128]{3,2,1,0:T(8,128)} %get-tuple-element.54), channel_id=1, source_target_pairs={{4,0},{8,4},{12,8},{16,12},{20,16},{24,20},{28,24},{32,28},{36,32}... | collective-permute-start | bytes 5308424 | tf_op jit(solution)/shard_map/ppermute | solution.py:539
  42.8 1.3 %collective-permute-start.4 = (f32[54,4,2,128]{3,2,1,0:T(2,128)}, f32[54,4,2,128]{3,2,1,0:T(2,128)S(1)}, u32[]{:S(2)}, u32[]{:S(2)}) collective-permute-start(f32[54,4,2,128]{3,2,1,0:T(2,128)} %get-tuple-element.55), channel_id=1, source_target_pairs={{0,1},{1,2},{2,3},{4,5},{5,6},{6,7},{8,9},{9,10},{10,11},{12,13},{... | collective-permute-start | bytes 663560 | tf_op jit(solution)/shard_map/ppermute | solution.py:540
  44.8 0.6 pad_add_fusion.info_ref
  45.4 21.5 %parcels.1 = (f32[7,4,32,128]{3,2,1,0:T(8,128)}, f32[7,1,32,128]{3,2,1,0:T(8,128)}, f32[7,1,32,128]{3,2,1,0:T(8,128)}, f32[8,16640]{1,0:T(8,128)}, f32[128,128]{1,0:T(8,128)}, /*index=5*/s32[8,128]{1,0:T(8,128)}) custom-call(s32[2]{0:T(128)} %pad_add_fusion.info_ref, f32[4,8,5760]{2,1,0:T(8,128)} %bitcast.6, f32[6,1,32,128]{3,2,1,0:T(8,128)} %copy-done.1, ...), custom_call_target="tpu_custom_call" | custom-call | tf_op jit(solution)/shard_map/parcels/pallas_call | solution.py:543
  66.9 5.0 %spread.1 = (f32[8,4096]{1,0:T(8,128)}, f32[8,4096]{1,0:T(8,128)}, f32[8,4096]{1,0:T(8,128)}, f32[8,4096]{1,0:T(8,128)}) custom-call(s32[2]{0:T(128)} %pad_add_fusion.info_ref, s32[8,128]{1,0:T(8,128)} %get-tuple-element.58.off_ref, f32[128,128]{1,0:T(8,128)} %get-tuple-element.59.dst_ref, f32[8,16640]{1,0:T(8,128)} %get-tuple-element.60.state_ref), custom_call_target="tpu_custom_call" | custom-call | tf_op jit(solution)/shard_map/spread/pallas_call | solution.py:594
  71.9 0.0 collective-permute-done.4.ylo_ref
  71.9 0.0 copy-start.4
  71.9 3.7 %collective-permute-start.5 = (f32[54,4,2,128]{3,2,1,0:T(2,128)}, f32[54,4,2,128]{3,2,1,0:T(2,128)}, u32[]{:S(2)}, u32[]{:S(2)}) collective-permute-start(f32[54,4,2,128]{3,2,1,0:T(2,128)} %get-tuple-element.66), channel_id=1, source_target_pairs={{1,0},{2,1},{3,2},{5,4},{6,5},{7,6},{9,8},{10,9},{11,10},{13,12},{... | collective-permute-start | bytes 663560 | tf_op jit(solution)/shard_map/ppermute | solution.py:605
  75.7 1.9 %collective-permute-start.6 = (f32[7,1,32,128]{3,2,1,0:T(8,128)}, f32[7,1,32,128]{3,2,1,0:T(8,128)}, u32[]{:S(2)}, u32[]{:S(2)}) collective-permute-start(f32[7,1,32,128]{3,2,1,0:T(8,128)} %get-tuple-element.67), channel_id=1, source_target_pairs={{0,4},{4,8},{8,12},{12,16},{16,20},{20,24},{24,28},{28,32},{32,36}... | collective-permute-start | bytes 344072 | tf_op jit(solution)/shard_map/ppermute | solution.py:591
  77.6 7.6 %collective-permute-start.7 = (f32[7,1,32,128]{3,2,1,0:T(8,128)}, f32[7,1,32,128]{3,2,1,0:T(8,128)}, u32[]{:S(2)}, u32[]{:S(2)}) collective-permute-start(f32[7,1,32,128]{3,2,1,0:T(8,128)} %get-tuple-element.68), channel_id=1, source_target_pairs={{4,0},{8,4},{12,8},{16,12},{20,16},{24,20},{28,24},{32,28},{36,32}... | collective-permute-start | bytes 344072 | tf_op jit(solution)/shard_map/ppermute | solution.py:592
  85.2 0.6 collective-permute-done.6.rest_1_
  85.7 1.5 %collective-permute-done.7.rest_2_ = f32[7,1,32,128]{3,2,1,0:T(8,128)} collective-permute-done((f32[7,1,32,128]{3,2,1,0:T(8,128)}, f32[7,1,32,128]{3,2,1,0:T(8,128)}, u32[]{:S(2)}, u32[]{:S(2)}) %collective-permute-start.7) | collective-permute-done | bytes 114720 | tf_op jit(solution)/shard_map/ppermute | solution.py:592
  87.2 0.0 collective-permute-done.5.yhi_ref
  87.3 3.6 %collective-permute-start.10 = (f32[8,4096]{1,0:T(8,128)}, f32[8,4096]{1,0:T(8,128)}, u32[]{:S(2)}, u32[]{:S(2)}) collective-permute-start(f32[8,4096]{1,0:T(8,128)} %get-tuple-element.82), channel_id=1, source_target_pairs={{0,3},{1,0},{2,1},{3,2},{4,7},{5,4},{6,5},{7,6},{8,11},{9,8},{10,9... | collective-permute-start | bytes 393224 | tf_op jit(solution)/shard_map/ppermute | solution.py:612
  90.9 0.0 collective-permute-start.8
  90.9 2.9 %collective-permute-start.9 = (f32[8,4096]{1,0:T(8,128)}, f32[8,4096]{1,0:T(8,128)}, u32[]{:S(2)}, u32[]{:S(2)}) collective-permute-start(f32[8,4096]{1,0:T(8,128)} %get-tuple-element.81), channel_id=1, source_target_pairs={{0,2},{1,3},{2,0},{3,1},{4,6},{5,7},{6,4},{7,5},{8,10},{9,11},{10,... | collective-permute-start | bytes 393224 | tf_op jit(solution)/shard_map/ppermute | solution.py:612
  93.8 0.0 collective-permute-done.2.xlo_ref
  93.8 0.0 copy-start
  93.8 0.0 collective-permute-done.3.xhi_ref
  93.8 0.0 copy-done.4
  93.8 1.2 %copy-done = f32[54,2,32,128]{3,2,1,0:T(8,128)} copy-done((f32[54,2,32,128]{3,2,1,0:T(8,128)}, f32[54,2,32,128]{3,2,1,0:T(8,128)S(1)}, u32[]{:S(2)}) %copy-start) | copy-done | bytes 1769496
  95.0 0.0 copy-start.3
  95.0 0.0 copy-start.5
  95.0 0.0 copy-start.6
  95.0 0.0 copy-start.7
  95.0 7.9 %transport.1 = (f32[54,4,32,128]{3,2,1,0:T(8,128)}, f32[7,4,32,128]{3,2,1,0:T(8,128)}) custom-call(f32[54]{0:T(128)} %diff_ref.1, f32[54,4,32,128]{3,2,1,0:T(8,128)} %y_ref.1, f32[54,2,32,128]{3,2,1,0:T(8,128)} %copy-done, f32[54,2,32,128]{3,2,1,0:T(8,128)} %collective-permute-done.3.xhi_ref, f32[54,4,2,128]{3,2,1,0:T(2,128)} %copy-done.4, ...), custom_call_target="tpu_custom_call" | custom-call | tf_op jit(solution)/shard_map/transport/pallas_call | solution.py:630
  103.0 0.0 collective-permute-done.10
  103.0 0.0 collective-permute-done.8
  103.0 0.0 collective-permute-done.9
  103.0 0.0 copy-done.3
  103.0 0.0 copy-done.5
  103.0 0.0 copy-done.6
  103.0 0.0 copy-done.7
  103.0 1.8 %fusion = f32[5,4096]{1,0:T(8,128)} fusion(f32[8,4096]{1,0:T(8,128)} %collective-permute-done.10, f32[8,4096]{1,0:T(8,128)} %collective-permute-done.9, f32[8,4096]{1,0:T(8,128)} %collective-permute-done.8, f32[8,4096]{1,0:T(8,128)S(1)} %copy-done.5, f32[3,4096]{1,0:T(4,128)S(1)} %copy-done.3, f32[1,4096]{1,0:T(1,128)S(1)} %bitcast.8, ...), kind=kLoop, calls=%fused_computation.1 | loop fusion | flops 122880 | bytes 495616 | tf_op jit(solution)/shard_map/jit(_where)/select_n | solution.py:659
  (1 shorter events, 0.0 us)
Async XLA Ops:
  5.9 12.6 %collective-permute-start = (f32[6,1,32,128]{3,2,1,0:T(8,128)}, f32[6,1,32,128]{3,2,1,0:T(8,128)S(1)}, u32[]{:S(2)}, u32[]{:S(2)}) collective-permute-start(f32[6,1,32,128]{3,2,1,0:T(8,128)} %get-tuple-element.51), channel_id=1, source_target_pairs={{0,4},{4,8},{8,12},{12,16},{16,20},{20,24},{24,28},{28,32},{32,36}... | collective-permute-start | bytes 294920 | tf_op jit(solution)/shard_map/ppermute | solution.py:513
  9.0 10.6 %collective-permute-start.1 = (f32[6,1,32,128]{3,2,1,0:T(8,128)}, f32[6,1,32,128]{3,2,1,0:T(8,128)S(1)}, u32[]{:S(2)}, u32[]{:S(2)}) collective-permute-start(f32[6,1,32,128]{3,2,1,0:T(8,128)} %get-tuple-element.52), channel_id=1, source_target_pairs={{4,0},{8,4},{12,8},{16,12},{20,16},{24,20},{28,24},{32,28},{36,32}... | collective-permute-start | bytes 294920 | tf_op jit(solution)/shard_map/ppermute | solution.py:514
  18.4 1.1 %copy-start.1 = (f32[6,1,32,128]{3,2,1,0:T(8,128)}, f32[6,1,32,128]{3,2,1,0:T(8,128)S(1)}, u32[]{:S(2)}) copy-start(f32[6,1,32,128]{3,2,1,0:T(8,128)S(1)} %collective-permute-done.lo_ref) | copy-start | bytes 294916
  19.6 0.7 copy-start.2
  32.8 61.0 %collective-permute-start.2 = (f32[54,2,32,128]{3,2,1,0:T(8,128)}, f32[54,2,32,128]{3,2,1,0:T(8,128)S(1)}, u32[]{:S(2)}, u32[]{:S(2)}) collective-permute-start(f32[54,2,32,128]{3,2,1,0:T(8,128)} %get-tuple-element.53), channel_id=1, source_target_pairs={{0,4},{4,8},{8,12},{12,16},{16,20},{20,24},{24,28},{28,32},{32,36}... | collective-permute-start | bytes 5308424 | tf_op jit(solution)/shard_map/ppermute | solution.py:538
  34.7 59.1 %collective-permute-start.3 = (f32[54,2,32,128]{3,2,1,0:T(8,128)}, f32[54,2,32,128]{3,2,1,0:T(8,128)}, u32[]{:S(2)}, u32[]{:S(2)}) collective-permute-start(f32[54,2,32,128]{3,2,1,0:T(8,128)} %get-tuple-element.54), channel_id=1, source_target_pairs={{4,0},{8,4},{12,8},{16,12},{20,16},{24,20},{28,24},{32,28},{36,32}... | collective-permute-start | bytes 5308424 | tf_op jit(solution)/shard_map/ppermute | solution.py:539
  42.8 29.1 %collective-permute-start.4 = (f32[54,4,2,128]{3,2,1,0:T(2,128)}, f32[54,4,2,128]{3,2,1,0:T(2,128)S(1)}, u32[]{:S(2)}, u32[]{:S(2)}) collective-permute-start(f32[54,4,2,128]{3,2,1,0:T(2,128)} %get-tuple-element.55), channel_id=1, source_target_pairs={{0,1},{1,2},{2,3},{4,5},{5,6},{6,7},{8,9},{9,10},{10,11},{12,13},{... | collective-permute-start | bytes 663560 | tf_op jit(solution)/shard_map/ppermute | solution.py:540
  71.9 21.9 %copy-start.4 = (f32[54,4,2,128]{3,2,1,0:T(2,128)}, f32[54,4,2,128]{3,2,1,0:T(2,128)S(1)}, u32[]{:S(2)}) copy-start(f32[54,4,2,128]{3,2,1,0:T(2,128)S(1)} %collective-permute-done.4.ylo_ref) | copy-start | bytes 663556
  71.9 15.3 %collective-permute-start.5 = (f32[54,4,2,128]{3,2,1,0:T(2,128)}, f32[54,4,2,128]{3,2,1,0:T(2,128)}, u32[]{:S(2)}, u32[]{:S(2)}) collective-permute-start(f32[54,4,2,128]{3,2,1,0:T(2,128)} %get-tuple-element.66), channel_id=1, source_target_pairs={{1,0},{2,1},{3,2},{5,4},{6,5},{7,6},{9,8},{10,9},{11,10},{13,12},{... | collective-permute-start | bytes 663560 | tf_op jit(solution)/shard_map/ppermute | solution.py:605
  75.7 10.1 %collective-permute-start.6 = (f32[7,1,32,128]{3,2,1,0:T(8,128)}, f32[7,1,32,128]{3,2,1,0:T(8,128)}, u32[]{:S(2)}, u32[]{:S(2)}) collective-permute-start(f32[7,1,32,128]{3,2,1,0:T(8,128)} %get-tuple-element.67), channel_id=1, source_target_pairs={{0,4},{4,8},{8,12},{12,16},{16,20},{20,24},{24,28},{28,32},{32,36}... | collective-permute-start | bytes 344072 | tf_op jit(solution)/shard_map/ppermute | solution.py:591
  77.6 9.7 %collective-permute-start.7 = (f32[7,1,32,128]{3,2,1,0:T(8,128)}, f32[7,1,32,128]{3,2,1,0:T(8,128)}, u32[]{:S(2)}, u32[]{:S(2)}) collective-permute-start(f32[7,1,32,128]{3,2,1,0:T(8,128)} %get-tuple-element.68), channel_id=1, source_target_pairs={{4,0},{8,4},{12,8},{16,12},{20,16},{24,20},{28,24},{32,28},{36,32}... | collective-permute-start | bytes 344072 | tf_op jit(solution)/shard_map/ppermute | solution.py:592
  87.3 15.7 %collective-permute-start.10 = (f32[8,4096]{1,0:T(8,128)}, f32[8,4096]{1,0:T(8,128)}, u32[]{:S(2)}, u32[]{:S(2)}) collective-permute-start(f32[8,4096]{1,0:T(8,128)} %get-tuple-element.82), channel_id=1, source_target_pairs={{0,3},{1,0},{2,1},{3,2},{4,7},{5,4},{6,5},{7,6},{8,11},{9,8},{10,9... | collective-permute-start | bytes 393224 | tf_op jit(solution)/shard_map/ppermute | solution.py:612
  90.9 12.1 %collective-permute-start.8 = (f32[8,4096]{1,0:T(8,128)}, f32[8,4096]{1,0:T(8,128)}, u32[]{:S(2)}, u32[]{:S(2)}) collective-permute-start(f32[8,4096]{1,0:T(8,128)} %get-tuple-element.80), channel_id=1, source_target_pairs={{0,1},{1,2},{2,3},{3,0},{4,5},{5,6},{6,7},{7,4},{8,9},{9,10},{10,1... | collective-permute-start | bytes 393224 | tf_op jit(solution)/shard_map/ppermute | solution.py:612
  90.9 12.1 %collective-permute-start.9 = (f32[8,4096]{1,0:T(8,128)}, f32[8,4096]{1,0:T(8,128)}, u32[]{:S(2)}, u32[]{:S(2)}) collective-permute-start(f32[8,4096]{1,0:T(8,128)} %get-tuple-element.81), channel_id=1, source_target_pairs={{0,2},{1,3},{2,0},{3,1},{4,6},{5,7},{6,4},{7,5},{8,10},{9,11},{10,... | collective-permute-start | bytes 393224 | tf_op jit(solution)/shard_map/ppermute | solution.py:612
  93.8 1.3 %copy-start = (f32[54,2,32,128]{3,2,1,0:T(8,128)}, f32[54,2,32,128]{3,2,1,0:T(8,128)S(1)}, u32[]{:S(2)}) copy-start(f32[54,2,32,128]{3,2,1,0:T(8,128)S(1)} %collective-permute-done.2.xlo_ref) | copy-start | bytes 5308420
  95.0 8.0 %copy-start.3 = (f32[3,4096]{1,0:T(4,128)S(1)}, f32[3,4096]{1,0:T(4,128)}, u32[]{:S(2)}) copy-start(f32[3,4096]{1,0:T(4,128)} %velocity_ref.1) | copy-start | bytes 147460
  95.0 8.0 %copy-start.5 = (f32[8,4096]{1,0:T(8,128)S(1)}, f32[8,4096]{1,0:T(8,128)}, u32[]{:S(2)}) copy-start(f32[8,4096]{1,0:T(8,128)} %get-tuple-element.85) | copy-start | bytes 393220
  95.0 8.0 %copy-start.6 = (f32[4096]{0:T(1024)S(1)}, f32[4096]{0:T(1024)}, u32[]{:S(2)}) copy-start(f32[4096]{0:T(1024)} %radius_ref.1) | copy-start | bytes 49156
  95.0 8.0 %copy-start.7 = (f32[4096]{0:T(1024)S(1)}, f32[4096]{0:T(1024)}, u32[]{:S(2)}) copy-start(f32[4096]{0:T(1024)} %temp_ref.3) | copy-start | bytes 49156

commit v2 on v1

--- a/solution.py
+++ b/solution.py
@@ -18,8 +18,7 @@
 LANES = 128
 PARTS = (54,)
 MANY = 18
-CHUNK = 1024
-PHYS = 1024
+CHUNK = 1536
 WINDOW = 256
 YPAD = 40
 ROWS_WIDTH = 9 * LANES
@@ -237,8 +236,8 @@
     lax.fori_loop(0, chunks, gather, 0)
 
     def step(c, carry):
-        at = pl.ds(pl.multiple_of(c * PHYS, PHYS), PHYS)
-        valid = c * PHYS + iota((1, PHYS), 1) < live
+        at = pl.ds(pl.multiple_of(c * CHUNK, CHUNK), CHUNK)
+        valid = c * CHUNK + iota((1, CHUNK), 1) < live
         inside = [jnp.where(valid, interp[f : f + 1, at], 0.0) for f in range(6)]
         radius = jnp.where(valid, cv[3:4, at], 1.0)
         velocity = [cv[d : d + 1, at] for d in (5, 6, 7)]
@@ -249,7 +248,7 @@
             src[k : k + 1, at] = jnp.where(valid, sources[k], 0.0)
         return carry
 
-    lax.fori_loop(0, (live + PHYS - 1) // PHYS, step, 0)
+    lax.fori_loop(0, (live + CHUNK - 1) // CHUNK, step, 0)
 
     def deposit(c, carry):
         at = pl.ds(pl.multiple_of(c * CHUNK, CHUNK), CHUNK)
@@ -274,16 +273,13 @@
                 main_ref[k, x - 1] = block
 
 
-def spread_kernel(info_ref, off_ref, dst_ref, state_ref, *outs_and_scratch):
-    outs, both_scr = outs_and_scratch[:-1], outs_and_scratch[-1]
+def spread_kernel(off_ref, dst_ref, state_ref, out_ref, both_scr):
     high, low = halves(state_ref[...])
     both_scr[0:16, :] = jnp.concatenate([high, low], axis=0)
-    group = info_ref[1]
-    each = dst_ref.shape[0] // len(outs)
-    for d, out in enumerate(outs):
-        owner = lax.rem(group + d, len(outs))
-
-        def spread(i, carry):
+    each = dst_ref.shape[0] // out_ref.shape[0]
+    for owner in range(out_ref.shape[0]):
+
+        def spread(i, carry, owner=owner):
             for j in range(8):
                 b = owner * each + i * 8 + j
                 aligned = (off_ref[0, b] >> 7) << 7
@@ -291,13 +287,24 @@
                 block = both_scr[:, pl.ds(pl.multiple_of(aligned, LANES), WINDOW)]
                 got = jnp.dot(block, hot, preferred_element_type=F32)
                 at = pl.ds(pl.multiple_of((i * 8 + j) * LANES, LANES), LANES)
-                out[:, at] = got[0:8] + got[8:16]
+                out_ref[owner, :, at] = got[0:8] + got[8:16]
             return carry
 
         lax.fori_loop(0, each // 8, spread, 0)
 
 
-def prepare_kernel(
+def state_kernel(info_ref, returned_ref, radius_ref, temp_ref, velocity_ref, out_ref):
+    slots = velocity_ref.shape[1]
+    new = returned_ref[0] + returned_ref[1]
+    for owner in range(2, returned_ref.shape[0]):
+        new = new + returned_ref[owner]
+    live = info_ref[1] * slots + iota((1, slots), 1) < info_ref[0]
+    out_ref[0:1, :] = jnp.where(live, new[0:1], radius_ref[...].reshape(1, -1))
+    out_ref[1:2, :] = jnp.where(live, new[1:2], temp_ref[...].reshape(1, -1))
+    out_ref[2:5, :] = jnp.where(live, new[2:5], velocity_ref[...])
+
+
+def pack_kernel(
     cells_ref,
     weights_ref,
     radius_ref,
@@ -306,40 +313,36 @@
     gas_temp_ref,
     dens_ref,
     vel_ref,
-    species_ref,
+    fuel_ref,
     packed_ref,
     top_ref,
     bottom_ref,
-    up_ref,
-    down_ref,
-    right_ref,
-    left_ref,
 ):
+    planes = gas_temp_ref.shape[0]
+    own = [gas_temp_ref, dens_ref, vel_ref.at[0], vel_ref.at[1], vel_ref.at[2], fuel_ref.at[0]]
+    for f in range(6):
+        top_ref[f, 0] = own[f][planes - 1]
+        bottom_ref[f, 0] = own[f][0]
+    w = [weights_ref[c : c + 1, :] for c in range(8)]
+    slots = cells_ref.shape[1]
+    each = slots // 8
+    packed_ref[0:1, 0:slots] = (w[4] + w[5]) + (w[6] + w[7])
+    packed_ref[1:2, 0:slots] = (w[2] + w[3]) + (w[6] + w[7])
+    packed_ref[2:3, 0:slots] = (w[1] + w[3]) + (w[5] + w[7])
+    packed_ref[3:4, 0:slots] = radius_ref[...].reshape(1, -1)
+    packed_ref[4:5, 0:slots] = temp_ref[...].reshape(1, -1)
+    packed_ref[5:8, 0:slots] = velocity_ref[...]
+    for i in range(8):
+        first = cells_ref[0:1, i * each : (i + 1) * each]
+        packed_ref[i : i + 1, slots : slots + each] = first.astype(F32)
+
+
+def rims_kernel(species_ref, up_ref, down_ref, right_ref, left_ref):
     planes, rows = species_ref.shape[1:3]
     up_ref[...] = species_ref[:, planes - 2 : planes]
     down_ref[...] = species_ref[:, 0:2]
     right_ref[...] = species_ref[:, :, rows - 2 : rows]
     left_ref[...] = species_ref[:, :, 0:2]
-
-    @pl.when(pl.program_id(0) == 0)
-    def _():
-        w = [weights_ref[c : c + 1, :] for c in range(8)]
-        slots = cells_ref.shape[1]
-        each = slots // 8
-        packed_ref[0:1, 0:slots] = (w[4] + w[5]) + (w[6] + w[7])
-        packed_ref[1:2, 0:slots] = (w[2] + w[3]) + (w[6] + w[7])
-        packed_ref[2:3, 0:slots] = (w[1] + w[3]) + (w[5] + w[7])
-        packed_ref[3:4, 0:slots] = radius_ref[...].reshape(1, -1)
-        packed_ref[4:5, 0:slots] = temp_ref[...].reshape(1, -1)
-        packed_ref[5:8, 0:slots] = velocity_ref[...]
-        for i in range(8):
-            first = cells_ref[0:1, i * each : (i + 1) * each]
-            packed_ref[i : i + 1, slots : slots + each] = first.astype(F32)
-        own = [gas_temp_ref, dens_ref, vel_ref.at[0], vel_ref.at[1], vel_ref.at[2],
-               species_ref.at[0]]
-        for f in range(6):
-            top_ref[f, 0] = own[f][planes - 1]
-            bottom_ref[f, 0] = own[f][0]
 
 
 def assemble_kernel(packed_ref, lo_ref, temp_ref, dens_ref, vel_ref, fuel_ref, hi_ref, out_ref):
@@ -472,9 +475,9 @@
     def by_kind(first, *shape):
         return pl.BlockSpec((MANY,) + shape, lambda i: (first + i, 0, 0, 0))
 
-    packed, top, bottom, x_up, x_down, y_right, y_left = pl.pallas_call(
-        prepare_kernel,
-        grid=(kinds // MANY,),
+    packed, top, bottom = pl.pallas_call(
+        pack_kernel,
+        grid=(1,),
         in_specs=[
             whole((8, capacity)),
             whole((8, capacity)),
@@ -484,32 +487,44 @@
             whole((planes, rows, depth)),
             whole((planes, rows, depth)),
             whole((3, planes, rows, depth)),
-            by_kind(0, planes, rows, depth),
+            whole((1, planes, rows, depth)),
         ],
         out_specs=[
             whole((8, capacity // 8 * 9)),
             whole((6, 1, rows, depth)),
             whole((6, 1, rows, depth)),
+        ],
+        out_shape=[
+            shaped(8, capacity // 8 * 9),
+            shaped(6, 1, rows, depth),
+            shaped(6, 1, rows, depth),
+        ],
+        compiler_params=limit,
+        name="pack",
+    )(
+        parcel_cells, parcel_weights, drop_radius, drop_temp, drop_velocity,
+        gas_temp, gas_density, gas_velocity, species,
+    )
+    species_cut, packed = lax.optimization_barrier((species, packed))
+    x_up, x_down, y_right, y_left = pl.pallas_call(
+        rims_kernel,
+        grid=(kinds // MANY,),
+        in_specs=[by_kind(0, planes, rows, depth)],
+        out_specs=[
             by_kind(0, 2, rows, depth),
             by_kind(0, 2, rows, depth),
             by_kind(0, planes, 2, depth),
             by_kind(0, planes, 2, depth),
         ],
         out_shape=[
-            shaped(8, capacity // 8 * 9),
-            shaped(6, 1, rows, depth),
-            shaped(6, 1, rows, depth),
             shaped(kinds, 2, rows, depth),
             shaped(kinds, 2, rows, depth),
             shaped(kinds, planes, 2, depth),
             shaped(kinds, planes, 2, depth),
         ],
         compiler_params=limit,
-        name="prepare",
-    )(
-        parcel_cells, parcel_weights, drop_radius, drop_temp, drop_velocity,
-        gas_temp, gas_density, gas_velocity, species,
-    )
+        name="rims",
+    )(species_cut)
     field_lo = lax.ppermute(top, "space", ahead)
     field_hi = lax.ppermute(bottom, "space", back)
     width = capacity // 8 * 9 + ROWS_WIDTH
@@ -530,6 +545,9 @@
         compiler_params=limit,
         name="assemble",
     )(packed, field_lo, gas_temp, gas_density, gas_velocity, species, field_hi)
+    sent, x_up, x_down, y_right, y_left = lax.optimization_barrier(
+        (sent, x_up, x_down, y_right, y_left)
+    )
     parcels = lax.all_gather(sent, "group", axis=0)
 
     x_up, x_down, y_right, y_left, parcels = lax.optimization_barrier(
@@ -539,7 +557,8 @@
     x_hi = lax.ppermute(x_down, "space", back)
     y_lo = lax.ppermute(y_right, "group", g_ahead)
 
-    reach = slots + WINDOW
+    chunks = pl.cdiv(slots, CHUNK)
+    reach = max(chunks * CHUNK, slots + WINDOW)
     main, dep_lo, dep_hi, state, dst, off = pl.pallas_call(
         parcel_kernel,
         grid=(1,),
@@ -578,38 +597,36 @@
             pltpu.VMEM((16, reach), F32),
             pltpu.VMEM((256, LANES), F32),
             pltpu.VMEM((6 * LANES, 768), BF16),
-            pltpu.VMEM((slots // CHUNK, 256, CHUNK), BF16),
-            pltpu.VMEM((slots // CHUNK, 256, CHUNK), BF16),
-            pltpu.VMEM((8, slots), F32),
-            pltpu.VMEM((8, slots), F32),
+            pltpu.VMEM((chunks, 256, CHUNK), BF16),
+            pltpu.VMEM((chunks, 256, CHUNK), BF16),
+            pltpu.VMEM((8, reach), F32),
+            pltpu.VMEM((8, reach), F32),
             pltpu.VMEM((7 * LANES, 256), F32),
         ],
         compiler_params=limit,
         name="parcels",
     )(info, parcels, field_lo, gas_temp, gas_density, gas_velocity, species, field_hi)
 
+    y_lo, y_left, state = lax.optimization_barrier((y_lo, y_left, state))
+    y_hi = lax.ppermute(y_left, "group", g_back)
+
     from_below = lax.ppermute(dep_hi, "space", ahead)
     from_above = lax.ppermute(dep_lo, "space", back)
 
     spread = pl.pallas_call(
         spread_kernel,
         grid=(1,),
-        in_specs=[smem, smem, whole((blocks, LANES)), whole((8, reach))],
-        out_specs=[whole((8, capacity))] * groups,
-        out_shape=[shaped(8, capacity)] * groups,
+        in_specs=[smem, whole((blocks, LANES)), whole((8, reach))],
+        out_specs=whole((groups, 8, capacity)),
+        out_shape=shaped(groups, 8, capacity),
         scratch_shapes=[pltpu.VMEM((16, reach), BF16)],
         compiler_params=limit,
         name="spread",
-    )(info, off, dst, state)
-    y_lo, y_left, spread = lax.optimization_barrier((y_lo, y_left, spread))
-    y_hi = lax.ppermute(y_left, "group", g_back)
+    )(off, dst, state)
     y_lo, y_hi, from_below, from_above, spread = lax.optimization_barrier(
         (y_lo, y_hi, from_below, from_above, spread)
     )
-    returned = [spread[0]]
-    for d in range(1, groups):
-        route = [(i, (i + d) % groups) for i in range(groups)]
-        returned.append(lax.ppermute(spread[d], "group", route))
+    returned = lax.all_to_all(spread, "group", 0, 0)
     gas = pl.BlockSpec((planes, rows, depth), lambda i: (0, 0, 0))
     row0 = pl.BlockSpec((None, planes, rows, depth), lambda i: (0, 0, 0, 0))
     all_gas = whole((7, planes, rows, depth))
@@ -652,11 +669,21 @@
         if c == 0:
             gas_sources = got[1]
     species_next, returned = lax.optimization_barrier((species_next, returned))
-    new_state = sum(returned[1:], returned[0])
-    old_state = jnp.concatenate([drop_radius[None], drop_temp[None], drop_velocity], axis=0)
-    slot = group * capacity + jnp.arange(capacity, dtype=jnp.int32)
-    live = slot < parcel_counts[0]
-    parcel_state = jnp.where(live[None], new_state[0:5], old_state)
+    parcel_state = pl.pallas_call(
+        state_kernel,
+        grid=(1,),
+        in_specs=[
+            smem,
+            whole((groups, 8, capacity)),
+            whole((capacity,)),
+            whole((capacity,)),
+            whole((3, capacity)),
+        ],
+        out_specs=whole((5, capacity)),
+        out_shape=shaped(5, capacity),
+        compiler_params=limit,
+        name="state",
+    )(info, returned, drop_radius, drop_temp, drop_velocity)
     return (species_next, gas_sources, parcel_state)
 
 

time: 104 us -> 102 us (0.981)
  the two profiles are of different devices: /device:TPU:25 before, /device:TPU:1 now
where the time goes in v2:
time: 102 us
  Pallas kernels  41.1 us (40%)
  starting transfers between devices  26.2 us (26%)
  waiting for transfers between devices  18.1 us (18%)
  blocking collectives  12.1 us (12%)
  local copies, waits for them, and re-layouts  2.08 us (2%)
  between operations  1.47 us (1%)
    pallas_call x1, Pallas kernels, per_device(): pl.pallas_call(parcel_kernel, grid=(1,), in_specs=[smem, whole((groups, 8...  17.6 us
    all_gather x1, blocking collectives, per_device(): parcels = lax.all_gather(sent, 'group', axis=0)  12.1 us
    ppermute x1, waiting for transfers between devices, per_device(): y_hi = lax.ppermute(y_left, 'group', g_back)  10.3 us
    pallas_call x1, Pallas kernels, per_device(): pl.pallas_call(functools.partial(transport_kernel, c == 0, first), grid=(...  7.88 us
    ppermute x1, starting transfers between devices, per_device(): x_lo = lax.ppermute(x_up, 'space', ahead)  5.18 us
    pallas_call x1, Pallas kernels, per_device(): pl.pallas_call(spread_kernel, grid=(1,), in_specs=[smem, whole((blocks, L...  5.13 us
    ppermute x1, waiting for transfers between devices, per_device(): from_above = lax.ppermute(dep_lo, 'space', back)  4.87 us
    pallas_call x1, Pallas kernels, per_device(): pl.pallas_call(rims_kernel, grid=(kinds // MANY,), in_specs=[by_kind(0, p...  4.83 us
  transfers between devices with their start and end apart: 9, of which 3 were waited for; matrix products, arithmetic and copies ran while one was open for 1% of the time, Pallas kernels for 35%

profile of v2, /device:TPU:1, one launch (start us, length us, event | category | flops | bytes accessed | tf_op | source)
XLA Modules:
  0.0 101.7 jit_solution(6078219121854623605)
XLA Ops:
  0.6 1.9 %pack.1 = (f32[8,4608]{1,0:T(8,128)}, f32[6,1,32,128]{3,2,1,0:T(8,128)}, f32[6,1,32,128]{3,2,1,0:T(8,128)}) custom-call(s32[8,4096]{1,0:T(8,128)} %cells_ref.1, f32[8,4096]{1,0:T(8,128)} %weights_ref.1, f32[4096]{0:T(1024)} %radius_ref.3, f32[4096]{0:T(1024)} %temp_ref.7, f32[3,4096]{1,0:T(4,128)} %velocity_ref.3, f32[4,32,128]{2,1,0:T(8,128)} %temp_ref.6, ...), custom_call_target="tpu_custom_call" | custom-call | tf_op jit(solution)/shard_map/pack/pallas_call | solution.py:478
  2.5 3.9 %collective-permute-start = (f32[6,1,32,128]{3,2,1,0:T(8,128)}, f32[6,1,32,128]{3,2,1,0:T(8,128)S(1)}, u32[]{:S(2)}, u32[]{:S(2)}) collective-permute-start(f32[6,1,32,128]{3,2,1,0:T(8,128)} %get-tuple-element.42), channel_id=1, source_target_pairs={{0,4},{4,8},{8,12},{12,16},{16,20},{20,24},{24,28},{28,32},{32,36}... | collective-permute-start | bytes 294920 | tf_op jit(solution)/shard_map/ppermute | solution.py:528
  6.5 1.3 %collective-permute-start.1 = (f32[6,1,32,128]{3,2,1,0:T(8,128)}, f32[6,1,32,128]{3,2,1,0:T(8,128)S(1)}, u32[]{:S(2)}, u32[]{:S(2)}) collective-permute-start(f32[6,1,32,128]{3,2,1,0:T(8,128)} %get-tuple-element.43), channel_id=1, source_target_pairs={{4,0},{8,4},{12,8},{16,12},{20,16},{24,20},{28,24},{32,28},{36,32}... | collective-permute-start | bytes 294920 | tf_op jit(solution)/shard_map/ppermute | solution.py:529
  7.8 4.8 %rims.1 = (f32[54,2,32,128]{3,2,1,0:T(8,128)}, f32[54,2,32,128]{3,2,1,0:T(8,128)}, f32[54,4,2,128]{3,2,1,0:T(2,128)}, f32[54,4,2,128]{3,2,1,0:T(2,128)}) custom-call(f32[54,4,32,128]{3,2,1,0:T(8,128)} %y_ref.1), custom_call_target="tpu_custom_call" | custom-call | tf_op jit(solution)/shard_map/rims/pallas_call | solution.py:509
  12.6 0.0 copy-start.8
  12.6 0.0 collective-permute-done.lo_ref
  12.6 0.0 copy-start.1
  12.6 0.0 collective-permute-done.1.hi_ref
  12.6 0.6 copy-done.1
  13.3 0.0 copy-start.2
  13.3 0.6 copy-done.2
  13.9 1.9 %assemble.1 = f32[8,5760]{1,0:T(8,128)} custom-call(f32[8,4608]{1,0:T(8,128)} %get-tuple-element.41.packed_ref, f32[6,1,32,128]{3,2,1,0:T(8,128)} %copy-done.1, f32[4,32,128]{2,1,0:T(8,128)} %temp_ref.6, f32[4,32,128]{2,1,0:T(8,128)} %dens_ref.7, f32[3,4,32,128]{3,2,1,0:T(8,128)} %ux_ref.1, f32[54,4,32,128]{3,2,1,0:T(8,128)} %y_ref.1, ...), custom_call_target="tpu_custom_call" | custom-call | tf_op jit(solution)/shard_map/assemble/pallas_call | solution.py:531
  15.8 12.1 %all-gather = f32[32,5760]{1,0:T(8,128)} all-gather(f32[8,5760]{1,0:T(8,128)} %assemble.1), channel_id=2, replica_groups=mesh['space'=64,'group'=4] {'group'}, dimensions={0}, use_global_device_ids=true | all-gather | bytes 921600 | tf_op jit(solution)/shard_map/all_gather | solution.py:551
  28.0 5.2 %collective-permute-start.2 = (f32[54,2,32,128]{3,2,1,0:T(8,128)}, f32[54,2,32,128]{3,2,1,0:T(8,128)}, u32[]{:S(2)}, u32[]{:S(2)}) collective-permute-start(f32[54,2,32,128]{3,2,1,0:T(8,128)} %get-tuple-element.54), channel_id=1, source_target_pairs={{0,4},{4,8},{8,12},{12,16},{16,20},{20,24},{24,28},{28,32},{32,36}... | collective-permute-start | bytes 5308424 | tf_op jit(solution)/shard_map/ppermute | solution.py:556
  33.1 1.3 %collective-permute-start.3 = (f32[54,2,32,128]{3,2,1,0:T(8,128)}, f32[54,2,32,128]{3,2,1,0:T(8,128)}, u32[]{:S(2)}, u32[]{:S(2)}) collective-permute-start(f32[54,2,32,128]{3,2,1,0:T(8,128)} %get-tuple-element.55), channel_id=1, source_target_pairs={{4,0},{8,4},{12,8},{16,12},{20,16},{24,20},{28,24},{32,28},{36,32}... | collective-permute-start | bytes 5308424 | tf_op jit(solution)/shard_map/ppermute | solution.py:557
  34.4 0.0 copy-done.8
  34.4 3.6 %collective-permute-start.4 = (f32[54,4,2,128]{3,2,1,0:T(2,128)S(1)}, f32[54,4,2,128]{3,2,1,0:T(2,128)S(1)}, u32[]{:S(2)}, u32[]{:S(2)}) collective-permute-start(f32[54,4,2,128]{3,2,1,0:T(2,128)S(1)} %copy-done.8), channel_id=1, source_target_pairs={{0,1},{1,2},{2,3},{4,5},{5,6},{6,7},{8,9},{9,10},{10,11},{12,13},{... | collective-permute-start | bytes 663560 | tf_op jit(solution)/shard_map/ppermute | solution.py:558
  38.7 0.6 pad_add_fusion.info_ref
  39.2 0.0 copy-start.7
  39.2 17.6 %parcels.1 = (f32[7,4,32,128]{3,2,1,0:T(8,128)}, f32[7,1,32,128]{3,2,1,0:T(8,128)}, f32[7,1,32,128]{3,2,1,0:T(8,128)}, f32[8,16896]{1,0:T(8,128)}, f32[128,128]{1,0:T(8,128)}, /*index=5*/s32[8,128]{1,0:T(8,128)}) custom-call(s32[2]{0:T(128)} %pad_add_fusion.info_ref, f32[4,8,5760]{2,1,0:T(8,128)} %bitcast.2, f32[6,1,32,128]{3,2,1,0:T(8,128)} %copy-done.1, ...), custom_call_target="tpu_custom_call" | custom-call | tf_op jit(solution)/shard_map/parcels/pallas_call | solution.py:562
  56.9 0.0 collective-permute-done.4.ylo_ref
  56.9 0.0 copy-start.3
  56.9 0.0 copy-done.7
  56.9 1.9 %collective-permute-start.5 = (f32[54,4,2,128]{3,2,1,0:T(2,128)S(1)}, f32[54,4,2,128]{3,2,1,0:T(2,128)S(1)}, u32[]{:S(2)}, u32[]{:S(2)}) collective-permute-start(f32[54,4,2,128]{3,2,1,0:T(2,128)S(1)} %copy-done.7), channel_id=1, source_target_pairs={{1,0},{2,1},{3,2},{5,4},{6,5},{7,6},{9,8},{10,9},{11,10},{13,12},{... | collective-permute-start | bytes 663560 | tf_op jit(solution)/shard_map/ppermute | solution.py:611
  58.9 4.3 %collective-permute-start.6 = (f32[7,1,32,128]{3,2,1,0:T(8,128)}, f32[7,1,32,128]{3,2,1,0:T(8,128)S(1)}, u32[]{:S(2)}, u32[]{:S(2)}) collective-permute-start(f32[7,1,32,128]{3,2,1,0:T(8,128)} %get-tuple-element.62), channel_id=1, source_target_pairs={{0,4},{4,8},{8,12},{12,16},{16,20},{20,24},{24,28},{28,32},{32,36}... | collective-permute-start | bytes 344072 | tf_op jit(solution)/shard_map/ppermute | solution.py:613
  63.1 1.3 %collective-permute-start.7 = (f32[7,1,32,128]{3,2,1,0:T(8,128)}, f32[7,1,32,128]{3,2,1,0:T(8,128)S(1)}, u32[]{:S(2)}, u32[]{:S(2)}) collective-permute-start(f32[7,1,32,128]{3,2,1,0:T(8,128)} %get-tuple-element.63), channel_id=1, source_target_pairs={{4,0},{8,4},{12,8},{16,12},{20,16},{24,20},{28,24},{32,28},{36,32}... | collective-permute-start | bytes 344072 | tf_op jit(solution)/shard_map/ppermute | solution.py:614
  64.4 5.1 %spread.1 = f32[4,8,4096]{2,1,0:T(8,128)} custom-call(s32[8,128]{1,0:T(8,128)} %get-tuple-element.64.off_ref, f32[128,128]{1,0:T(8,128)} %get-tuple-element.65.dst_ref, f32[8,16896]{1,0:T(8,128)} %get-tuple-element.66.state_ref), custom_call_target="tpu_custom_call" | custom-call | tf_op jit(solution)/shard_map/spread/pallas_call | solution.py:616
  69.6 3.0 %collective-permute-done.6.rest_1_ = f32[7,1,32,128]{3,2,1,0:T(8,128)S(1)} collective-permute-done((f32[7,1,32,128]{3,2,1,0:T(8,128)}, f32[7,1,32,128]{3,2,1,0:T(8,128)S(1)}, u32[]{:S(2)}, u32[]{:S(2)}) %collective-permute-start.6) | collective-permute-done | bytes 114720 | tf_op jit(solution)/shard_map/ppermute | solution.py:613
  72.5 0.0 copy-start.5
  72.6 4.9 %collective-permute-done.7.rest_2_ = f32[7,1,32,128]{3,2,1,0:T(8,128)S(1)} collective-permute-done((f32[7,1,32,128]{3,2,1,0:T(8,128)}, f32[7,1,32,128]{3,2,1,0:T(8,128)S(1)}, u32[]{:S(2)}, u32[]{:S(2)}) %collective-permute-start.7) | collective-permute-done | bytes 114720 | tf_op jit(solution)/shard_map/ppermute | solution.py:614
  77.4 0.0 copy-start.6
  77.4 10.3 %collective-permute-done.5.yhi_ref = f32[54,4,2,128]{3,2,1,0:T(2,128)S(1)} collective-permute-done((f32[54,4,2,128]{3,2,1,0:T(2,128)S(1)}, f32[54,4,2,128]{3,2,1,0:T(2,128)S(1)}, u32[]{:S(2)}, u32[]{:S(2)}) %collective-permute-start.5) | collective-permute-done | bytes 221216 | tf_op jit(solution)/shard_map/ppermute | solution.py:611
  87.7 0.0 copy-start.4
  87.7 3.5 %all-to-all-start = ((f32[4,8,4096]{2,1,0:T(8,128)}), f32[4,8,4096]{2,1,0:T(8,128)S(1)}, u32[]{:S(2)}, u32[]{:S(2)}) async-start(f32[4,8,4096]{2,1,0:T(8,128)} %spread.1), calls=%async_computation | async-start | bytes 1048576 | tf_op jit(solution)/shard_map/all_to_all | solution.py:629
  91.2 0.0 collective-permute-done.2.xlo_ref
  91.2 0.0 collective-permute-done.3.xhi_ref
  91.2 0.0 copy-done.3
  91.2 0.0 copy-done.5
  91.2 0.0 copy-done.6
  91.2 0.0 copy-done.4
  91.2 7.9 %transport.1 = (f32[54,4,32,128]{3,2,1,0:T(8,128)}, f32[7,4,32,128]{3,2,1,0:T(8,128)}) custom-call(f32[54]{0:T(128)} %diff_ref.1, f32[54,4,32,128]{3,2,1,0:T(8,128)} %y_ref.1, f32[54,2,32,128]{3,2,1,0:T(8,128)} %collective-permute-done.2.xlo_ref, f32[54,2,32,128]{3,2,1,0:T(8,128)} %collective-permute-done.3.xhi_ref, f32[54,4,2,128]{3,2,1,0:T(2,128)} %copy-done.3, ...), custom_call_target="tpu_custom_call" | custom-call | tf_op jit(solution)/shard_map/transport/pallas_call | solution.py:647
  99.1 0.0 all-to-all-done.returned_ref
  99.1 0.0 copy-start
  99.1 0.8 copy-done
  99.9 1.8 %state.1 = f32[5,4096]{1,0:T(8,128)} custom-call(s32[2]{0:T(128)} %pad_add_fusion.info_ref, f32[4,8,4096]{2,1,0:T(8,128)} %copy-done, f32[4096]{0:T(1024)} %radius_ref.3, f32[4096]{0:T(1024)} %temp_ref.7, f32[3,4096]{1,0:T(4,128)} %velocity_ref.3), custom_call_target="tpu_custom_call" | custom-call | tf_op jit(solution)/shard_map/state/pallas_call | solution.py:672
Async XLA Ops:
  2.5 10.1 %collective-permute-start = (f32[6,1,32,128]{3,2,1,0:T(8,128)}, f32[6,1,32,128]{3,2,1,0:T(8,128)S(1)}, u32[]{:S(2)}, u32[]{:S(2)}) collective-permute-start(f32[6,1,32,128]{3,2,1,0:T(8,128)} %get-tuple-element.42), channel_id=1, source_target_pairs={{0,4},{4,8},{8,12},{12,16},{16,20},{20,24},{24,28},{28,32},{32,36}... | collective-permute-start | bytes 294920 | tf_op jit(solution)/shard_map/ppermute | solution.py:528
  6.5 6.2 %collective-permute-start.1 = (f32[6,1,32,128]{3,2,1,0:T(8,128)}, f32[6,1,32,128]{3,2,1,0:T(8,128)S(1)}, u32[]{:S(2)}, u32[]{:S(2)}) collective-permute-start(f32[6,1,32,128]{3,2,1,0:T(8,128)} %get-tuple-element.43), channel_id=1, source_target_pairs={{4,0},{8,4},{12,8},{16,12},{20,16},{24,20},{28,24},{32,28},{36,32}... | collective-permute-start | bytes 294920 | tf_op jit(solution)/shard_map/ppermute | solution.py:529
  12.6 21.8 %copy-start.8 = (f32[54,4,2,128]{3,2,1,0:T(2,128)S(1)}, f32[54,4,2,128]{3,2,1,0:T(2,128)}, u32[]{:S(2)}) copy-start(f32[54,4,2,128]{3,2,1,0:T(2,128)} %get-tuple-element.56) | copy-start | bytes 663556
  12.6 0.6 copy-start.1
  13.3 0.6 copy-start.2
  28.0 63.2 %collective-permute-start.2 = (f32[54,2,32,128]{3,2,1,0:T(8,128)}, f32[54,2,32,128]{3,2,1,0:T(8,128)}, u32[]{:S(2)}, u32[]{:S(2)}) collective-permute-start(f32[54,2,32,128]{3,2,1,0:T(8,128)} %get-tuple-element.54), channel_id=1, source_target_pairs={{0,4},{4,8},{8,12},{12,16},{16,20},{20,24},{24,28},{28,32},{32,36}... | collective-permute-start | bytes 5308424 | tf_op jit(solution)/shard_map/ppermute | solution.py:556
  33.1 58.0 %collective-permute-start.3 = (f32[54,2,32,128]{3,2,1,0:T(8,128)}, f32[54,2,32,128]{3,2,1,0:T(8,128)}, u32[]{:S(2)}, u32[]{:S(2)}) collective-permute-start(f32[54,2,32,128]{3,2,1,0:T(8,128)} %get-tuple-element.55), channel_id=1, source_target_pairs={{4,0},{8,4},{12,8},{16,12},{20,16},{24,20},{28,24},{32,28},{36,32}... | collective-permute-start | bytes 5308424 | tf_op jit(solution)/shard_map/ppermute | solution.py:557
  34.4 22.5 %collective-permute-start.4 = (f32[54,4,2,128]{3,2,1,0:T(2,128)S(1)}, f32[54,4,2,128]{3,2,1,0:T(2,128)S(1)}, u32[]{:S(2)}, u32[]{:S(2)}) collective-permute-start(f32[54,4,2,128]{3,2,1,0:T(2,128)S(1)} %copy-done.8), channel_id=1, source_target_pairs={{0,1},{1,2},{2,3},{4,5},{5,6},{6,7},{8,9},{9,10},{10,11},{12,13},{... | collective-permute-start | bytes 663560 | tf_op jit(solution)/shard_map/ppermute | solution.py:558
  39.2 17.7 %copy-start.7 = (f32[54,4,2,128]{3,2,1,0:T(2,128)S(1)}, f32[54,4,2,128]{3,2,1,0:T(2,128)}, u32[]{:S(2)}) copy-start(f32[54,4,2,128]{3,2,1,0:T(2,128)} %get-tuple-element.61) | copy-start | bytes 663556
  56.9 34.3 %copy-start.3 = (f32[54,4,2,128]{3,2,1,0:T(2,128)}, f32[54,4,2,128]{3,2,1,0:T(2,128)S(1)}, u32[]{:S(2)}) copy-start(f32[54,4,2,128]{3,2,1,0:T(2,128)S(1)} %collective-permute-done.4.ylo_ref) | copy-start | bytes 663556
  56.9 30.8 %collective-permute-start.5 = (f32[54,4,2,128]{3,2,1,0:T(2,128)S(1)}, f32[54,4,2,128]{3,2,1,0:T(2,128)S(1)}, u32[]{:S(2)}, u32[]{:S(2)}) collective-permute-start(f32[54,4,2,128]{3,2,1,0:T(2,128)S(1)} %copy-done.7), channel_id=1, source_target_pairs={{1,0},{2,1},{3,2},{5,4},{6,5},{7,6},{9,8},{10,9},{11,10},{13,12},{... | collective-permute-start | bytes 663560 | tf_op jit(solution)/shard_map/ppermute | solution.py:611
  58.9 13.7 %collective-permute-start.6 = (f32[7,1,32,128]{3,2,1,0:T(8,128)}, f32[7,1,32,128]{3,2,1,0:T(8,128)S(1)}, u32[]{:S(2)}, u32[]{:S(2)}) collective-permute-start(f32[7,1,32,128]{3,2,1,0:T(8,128)} %get-tuple-element.62), channel_id=1, source_target_pairs={{0,4},{4,8},{8,12},{12,16},{16,20},{20,24},{24,28},{28,32},{32,36}... | collective-permute-start | bytes 344072 | tf_op jit(solution)/shard_map/ppermute | solution.py:613
  63.1 14.3 %collective-permute-start.7 = (f32[7,1,32,128]{3,2,1,0:T(8,128)}, f32[7,1,32,128]{3,2,1,0:T(8,128)S(1)}, u32[]{:S(2)}, u32[]{:S(2)}) collective-permute-start(f32[7,1,32,128]{3,2,1,0:T(8,128)} %get-tuple-element.63), channel_id=1, source_target_pairs={{4,0},{8,4},{12,8},{16,12},{20,16},{24,20},{28,24},{32,28},{36,32}... | collective-permute-start | bytes 344072 | tf_op jit(solution)/shard_map/ppermute | solution.py:614
  72.5 18.6 %copy-start.5 = (f32[7,1,32,128]{3,2,1,0:T(8,128)}, f32[7,1,32,128]{3,2,1,0:T(8,128)S(1)}, u32[]{:S(2)}) copy-start(f32[7,1,32,128]{3,2,1,0:T(8,128)S(1)} %collective-permute-done.6.rest_1_) | copy-start | bytes 344068
  77.4 13.8 %copy-start.6 = (f32[7,1,32,128]{3,2,1,0:T(8,128)}, f32[7,1,32,128]{3,2,1,0:T(8,128)S(1)}, u32[]{:S(2)}) copy-start(f32[7,1,32,128]{3,2,1,0:T(8,128)S(1)} %collective-permute-done.7.rest_2_) | copy-start | bytes 344068
  87.7 3.5 %copy-start.4 = (f32[54,4,2,128]{3,2,1,0:T(2,128)}, f32[54,4,2,128]{3,2,1,0:T(2,128)S(1)}, u32[]{:S(2)}) copy-start(f32[54,4,2,128]{3,2,1,0:T(2,128)S(1)} %collective-permute-done.5.yhi_ref) | copy-start | bytes 663556
  87.7 11.4 %all-to-all-start = ((f32[4,8,4096]{2,1,0:T(8,128)}), f32[4,8,4096]{2,1,0:T(8,128)S(1)}, u32[]{:S(2)}, u32[]{:S(2)}) async-start(f32[4,8,4096]{2,1,0:T(8,128)} %spread.1), calls=%async_computation | async-start | bytes 1048576 | tf_op jit(solution)/shard_map/all_to_all | solution.py:629
  99.1 0.8 copy-start

commit v3 on v2

--- a/solution.py
+++ b/solution.py
@@ -21,7 +21,9 @@
 CHUNK = 1536
 WINDOW = 256
 YPAD = 40
-ROWS_WIDTH = 9 * LANES
+OWN_ROWS = 48
+RIM_ROWS = 24
+ROWS_WIDTH = (OWN_ROWS + RIM_ROWS) // 8 * LANES
 F32 = jnp.float32
 BF16 = jnp.bfloat16
 NT = (((1,), (1,)), ((), ()))
@@ -42,8 +44,10 @@
 
 
 def one_hot(dst_row, aligned):
-    rel = dst_row - aligned.astype(F32)
-    return jnp.where(iota((WINDOW, LANES), 0).astype(F32) == rel, 1.0, 0.0).astype(BF16)
+    rel = jnp.broadcast_to(dst_row - aligned.astype(F32), (16, LANES)).astype(BF16)
+    rel = jnp.concatenate([rel] * (WINDOW // 16), axis=0)
+    places = iota((WINDOW, LANES), 0).astype(F32).astype(BF16)
+    return jnp.where(places == rel, jnp.ones_like(rel), jnp.zeros_like(rel))
 
 
 def cells_of(width):
@@ -78,7 +82,7 @@
 
 
 def parcel_kernel(
-    info_ref,
+    count_ref,
     pk_ref,
     lo_ref,
     temp_ref,
@@ -111,7 +115,7 @@
     capacity = each * 8
     slots = groups * capacity
     blocks = slots // LANES
-    count, group = info_ref[0], info_ref[1]
+    count, group = count_ref[0], lax.axis_index("group")
 
     per_line = each // LANES
     for b in range(blocks):
@@ -273,13 +277,17 @@
                 main_ref[k, x - 1] = block
 
 
-def spread_kernel(off_ref, dst_ref, state_ref, out_ref, both_scr):
+def spread_kernel(off_ref, dst_ref, state_ref, *outs_and_scratch):
+    both_scr = outs_and_scratch[-1]
     high, low = halves(state_ref[...])
     both_scr[0:16, :] = jnp.concatenate([high, low], axis=0)
-    each = dst_ref.shape[0] // out_ref.shape[0]
-    for owner in range(out_ref.shape[0]):
-
-        def spread(i, carry, owner=owner):
+    outs = outs_and_scratch[:-1]
+    group = lax.axis_index("group")
+    each = dst_ref.shape[0] // len(outs)
+    for d, out in enumerate(outs):
+        owner = lax.rem(group + d, len(outs))
+
+        def spread(i, carry, owner=owner, out=out):
             for j in range(8):
                 b = owner * each + i * 8 + j
                 aligned = (off_ref[0, b] >> 7) << 7
@@ -287,21 +295,10 @@
                 block = both_scr[:, pl.ds(pl.multiple_of(aligned, LANES), WINDOW)]
                 got = jnp.dot(block, hot, preferred_element_type=F32)
                 at = pl.ds(pl.multiple_of((i * 8 + j) * LANES, LANES), LANES)
-                out_ref[owner, :, at] = got[0:8] + got[8:16]
+                out[:, at] = got[0:8] + got[8:16]
             return carry
 
         lax.fori_loop(0, each // 8, spread, 0)
-
-
-def state_kernel(info_ref, returned_ref, radius_ref, temp_ref, velocity_ref, out_ref):
-    slots = velocity_ref.shape[1]
-    new = returned_ref[0] + returned_ref[1]
-    for owner in range(2, returned_ref.shape[0]):
-        new = new + returned_ref[owner]
-    live = info_ref[1] * slots + iota((1, slots), 1) < info_ref[0]
-    out_ref[0:1, :] = jnp.where(live, new[0:1], radius_ref[...].reshape(1, -1))
-    out_ref[1:2, :] = jnp.where(live, new[1:2], temp_ref[...].reshape(1, -1))
-    out_ref[2:5, :] = jnp.where(live, new[2:5], velocity_ref[...])
 
 
 def pack_kernel(
@@ -335,6 +332,13 @@
     for i in range(8):
         first = cells_ref[0:1, i * each : (i + 1) * each]
         packed_ref[i : i + 1, slots : slots + each] = first.astype(F32)
+    rows = gas_temp_ref.shape[1]
+    for f in range(6):
+        for x in range(planes):
+            for side, y in enumerate((0, rows - 1)):
+                block, line = row_place(planes, f, x + 1, side)
+                at = slots + each + block * LANES
+                packed_ref[line : line + 1, at : at + LANES] = own[f][x, y : y + 1, :]
 
 
 def rims_kernel(species_ref, up_ref, down_ref, right_ref, left_ref):
@@ -345,27 +349,21 @@
     left_ref[...] = species_ref[:, :, 0:2]
 
 
-def assemble_kernel(packed_ref, lo_ref, temp_ref, dens_ref, vel_ref, fuel_ref, hi_ref, out_ref):
-    start = packed_ref.shape[1]
-    out_ref[:, 0:start] = packed_ref[...]
-    planes, rows = temp_ref.shape[0:2]
-    own = [temp_ref, dens_ref, vel_ref.at[0], vel_ref.at[1], vel_ref.at[2], fuel_ref.at[0]]
+def assemble_kernel(packed_ref, lo_ref, hi_ref, out_ref):
+    planes = OWN_ROWS // 12
+    rows = lo_ref.shape[2]
     for f in range(6):
-        for x in range(planes + 2):
-            if x == 0:
-                plane = lo_ref.at[f, 0]
-            elif x == planes + 1:
-                plane = hi_ref.at[f, 0]
-            else:
-                plane = own[f].at[x - 1]
+        for x, plane in ((0, lo_ref.at[f, 0]), (planes + 1, hi_ref.at[f, 0])):
             for side, y in enumerate((0, rows - 1)):
                 block, line = row_place(planes, f, x, side)
-                at = start + block * LANES
+                at = (block - OWN_ROWS // 8) * LANES
                 out_ref[line : line + 1, at : at + LANES] = plane[y : y + 1, :]
 
 
 def row_place(planes, f, x, side):
-    return divmod((f * (planes + 2) + x) * 2 + side, 8)
+    if 0 < x <= planes:
+        return divmod((f * planes + x - 1) * 2 + side, 8)
+    return divmod(planes * 12 + (f * 2 + (x > 0)) * 2 + side, 8)
 
 
 def transport_kernel(
@@ -463,8 +461,6 @@
     back = [(b, a) for a, b in ahead]
     g_ahead = [(i, i + 1) for i in range(groups - 1)]
     g_back = [(b, a) for a, b in g_ahead]
-    group = lax.axis_index("group")
-    info = jnp.stack([parcel_counts[0], group.astype(jnp.int32)])
 
     whole = lambda shape: pl.BlockSpec(shape, lambda i, n=len(shape): (0,) * n)
     smem = pl.BlockSpec(memory_space=pltpu.SMEM)
@@ -475,6 +471,7 @@
     def by_kind(first, *shape):
         return pl.BlockSpec((MANY,) + shape, lambda i: (first + i, 0, 0, 0))
 
+    width = capacity // 8 * 9 + ROWS_WIDTH
     packed, top, bottom = pl.pallas_call(
         pack_kernel,
         grid=(1,),
@@ -490,12 +487,12 @@
             whole((1, planes, rows, depth)),
         ],
         out_specs=[
-            whole((8, capacity // 8 * 9)),
+            whole((8, width)),
             whole((6, 1, rows, depth)),
             whole((6, 1, rows, depth)),
         ],
         out_shape=[
-            shaped(8, capacity // 8 * 9),
+            shaped(8, width),
             shaped(6, 1, rows, depth),
             shaped(6, 1, rows, depth),
         ],
@@ -527,24 +524,17 @@
     )(species_cut)
     field_lo = lax.ppermute(top, "space", ahead)
     field_hi = lax.ppermute(bottom, "space", back)
-    width = capacity // 8 * 9 + ROWS_WIDTH
+    tail = RIM_ROWS // 8 * LANES
     sent = pl.pallas_call(
         assemble_kernel,
         grid=(1,),
-        in_specs=[
-            whole((8, capacity // 8 * 9)),
-            whole((6, 1, rows, depth)),
-            whole((planes, rows, depth)),
-            whole((planes, rows, depth)),
-            whole((3, planes, rows, depth)),
-            whole((1, planes, rows, depth)),
-            whole((6, 1, rows, depth)),
-        ],
-        out_specs=whole((8, width)),
+        in_specs=[hbm, whole((6, 1, rows, depth)), whole((6, 1, rows, depth))],
+        out_specs=pl.BlockSpec((8, tail), lambda i: (0, width // tail - 1)),
         out_shape=shaped(8, width),
+        input_output_aliases={0: 0},
         compiler_params=limit,
         name="assemble",
-    )(packed, field_lo, gas_temp, gas_density, gas_velocity, species, field_hi)
+    )(packed, field_lo, field_hi)
     sent, x_up, x_down, y_right, y_left = lax.optimization_barrier(
         (sent, x_up, x_down, y_right, y_left)
     )
@@ -605,7 +595,7 @@
         ],
         compiler_params=limit,
         name="parcels",
-    )(info, parcels, field_lo, gas_temp, gas_density, gas_velocity, species, field_hi)
+    )(parcel_counts, parcels, field_lo, gas_temp, gas_density, gas_velocity, species, field_hi)
 
     y_lo, y_left, state = lax.optimization_barrier((y_lo, y_left, state))
     y_hi = lax.ppermute(y_left, "group", g_back)
@@ -617,8 +607,8 @@
         spread_kernel,
         grid=(1,),
         in_specs=[smem, whole((blocks, LANES)), whole((8, reach))],
-        out_specs=whole((groups, 8, capacity)),
-        out_shape=shaped(groups, 8, capacity),
+        out_specs=[whole((8, capacity))] * groups,
+        out_shape=[shaped(8, capacity)] * groups,
         scratch_shapes=[pltpu.VMEM((16, reach), BF16)],
         compiler_params=limit,
         name="spread",
@@ -626,7 +616,10 @@
     y_lo, y_hi, from_below, from_above, spread = lax.optimization_barrier(
         (y_lo, y_hi, from_below, from_above, spread)
     )
-    returned = lax.all_to_all(spread, "group", 0, 0)
+    returned = [spread[0]]
+    for d in range(1, groups):
+        route = [(i, (i + d) % groups) for i in range(groups)]
+        returned.append(lax.ppermute(spread[d], "group", route))
     gas = pl.BlockSpec((planes, rows, depth), lambda i: (0, 0, 0))
     row0 = pl.BlockSpec((None, planes, rows, depth), lambda i: (0, 0, 0, 0))
     all_gas = whole((7, planes, rows, depth))
@@ -669,21 +662,11 @@
         if c == 0:
             gas_sources = got[1]
     species_next, returned = lax.optimization_barrier((species_next, returned))
-    parcel_state = pl.pallas_call(
-        state_kernel,
-        grid=(1,),
-        in_specs=[
-            smem,
-            whole((groups, 8, capacity)),
-            whole((capacity,)),
-            whole((capacity,)),
-            whole((3, capacity)),
-        ],
-        out_specs=whole((5, capacity)),
-        out_shape=shaped(5, capacity),
-        compiler_params=limit,
-        name="state",
-    )(info, returned, drop_radius, drop_temp, drop_velocity)
+    new_state = sum(returned[1:], returned[0])
+    old_state = jnp.concatenate([drop_radius[None], drop_temp[None], drop_velocity], axis=0)
+    slot = lax.axis_index("group") * capacity + jnp.arange(capacity, dtype=jnp.int32)
+    live = slot < parcel_counts[0]
+    parcel_state = jnp.where(live[None], new_state[0:5], old_state)
     return (species_next, gas_sources, parcel_state)
 
 

time: 102 us -> 103 us (level)
  Pallas kernels: 41.1 us -> 34.3 us
  waiting for transfers between devices: 18.1 us -> 24 us
  other arithmetic: 0.56 us -> 1.77 us
    ppermute x1, waiting for transfers between devices: 2.98 us -> 8.75 us  [per_device(): from_below = lax.ppermute(dep_hi, 'space', ahead)]
    pallas_call x1, Pallas kernels: 17.6 us -> 13 us  [per_device(): pl.pallas_call(parcel_kernel, grid=(1,), in_specs=[smem, whole((groups, 8...]
    all_to_all x1 -> x0, starting transfers between devices: 3.46 us -> none  [per_device(): returned = lax.all_to_all(spread, 'group', 0, 0)]
    ppermute x0 -> x3, starting transfers between devices: none -> 3.25 us  [per_device(): returned.append(lax.ppermute(spread[d], 'group', route))]
    pallas_call x2 -> x1, Pallas kernels: 3.7 us -> 1.55 us  [per_device(): pl.pallas_call(assemble_kernel, grid=(1,), in_specs=[hbm, whole((6, 1, ro...]
    select_n x0 -> x1, other arithmetic: none -> 1.76 us  [per_device(): parcel_state = jnp.where(live[None], new_state[0:5], old_state)]
    ppermute x1, starting transfers between devices: 5.18 us -> 4.09 us  [per_device(): x_lo = lax.ppermute(x_up, 'space', ahead)]
    ppermute x1, waiting for transfers between devices: 10.3 us -> 11.4 us  [per_device(): y_hi = lax.ppermute(y_left, 'group', g_back)]
  transfers between devices with their start and end apart: 9 -> 11, of which waited for: 3 -> 3; matrix products, arithmetic and copies ran while one was open for 1% -> 0% of each run, Pallas kernels for 35% -> 30%
where the time goes in v3:
time: 103 us; the launch traced here: 102 us
  Pallas kernels  34.3 us (33%)
  starting transfers between devices  25.6 us (25%)
  waiting for transfers between devices  24 us (23%)
  blocking collectives  12.1 us (12%)
  local copies, waits for them, and re-layouts  2.5 us (2%)
  other arithmetic  1.77 us (2%)
  between operations  1.47 us (1%)
    pallas_call x1, Pallas kernels, per_device(): pl.pallas_call(parcel_kernel, grid=(1,), in_specs=[smem, whole((groups, 8...  13 us
    all_gather x1, blocking collectives, per_device(): parcels = lax.all_gather(sent, 'group', axis=0)  12.1 us
    ppermute x1, waiting for transfers between devices, per_device(): y_hi = lax.ppermute(y_left, 'group', g_back)  11.4 us
    ppermute x1, waiting for transfers between devices, per_device(): from_below = lax.ppermute(dep_hi, 'space', ahead)  8.75 us
    pallas_call x1, Pallas kernels, per_device(): pl.pallas_call(functools.partial(transport_kernel, c == 0, first), grid=(...  7.95 us
    pallas_call x1, Pallas kernels, per_device(): pl.pallas_call(spread_kernel, grid=(1,), in_specs=[smem, whole((blocks, L...  4.99 us
    ppermute x1, starting transfers between devices, per_device(): from_below = lax.ppermute(dep_hi, 'space', ahead)  4.92 us
    pallas_call x1, Pallas kernels, per_device(): pl.pallas_call(rims_kernel, grid=(kinds // MANY,), in_specs=[by_kind(0, p...  4.83 us
  transfers between devices with their start and end apart: 11, of which 3 were waited for; matrix products, arithmetic and copies ran while one was open for 0% of the time, Pallas kernels for 30%

profile of v3, /device:TPU:1, one launch (start us, length us, event | category | flops | bytes accessed | tf_op | source)
XLA Modules:
  0.0 101.8 jit_solution(3653489547420736716)
XLA Ops:
  0.6 1.9 %pack.1 = (f32[8,5760]{1,0:T(8,128)}, f32[6,1,32,128]{3,2,1,0:T(8,128)}, f32[6,1,32,128]{3,2,1,0:T(8,128)}) custom-call(s32[8,4096]{1,0:T(8,128)} %cells_ref.1, f32[8,4096]{1,0:T(8,128)} %weights_ref.1, f32[4096]{0:T(1024)} %radius_ref.1, f32[4096]{0:T(1024)} %temp_ref.2, f32[3,4096]{1,0:T(4,128)} %velocity_ref.1, f32[4,32,128]{2,1,0:T(8,128)} %temp_ref.3, ...), custom_call_target="tpu_custom_call" | custom-call | tf_op jit(solution)/shard_map/pack/pallas_call | solution.py:475
  2.6 3.9 %collective-permute-start = (f32[6,1,32,128]{3,2,1,0:T(8,128)}, f32[6,1,32,128]{3,2,1,0:T(8,128)S(1)}, u32[]{:S(2)}, u32[]{:S(2)}) collective-permute-start(f32[6,1,32,128]{3,2,1,0:T(8,128)} %get-tuple-element.52), channel_id=1, source_target_pairs={{0,4},{4,8},{8,12},{12,16},{16,20},{20,24},{24,28},{28,32},{32,36}... | collective-permute-start | bytes 294920 | tf_op jit(solution)/shard_map/ppermute | solution.py:525
  6.5 1.3 %collective-permute-start.1 = (f32[6,1,32,128]{3,2,1,0:T(8,128)}, f32[6,1,32,128]{3,2,1,0:T(8,128)S(1)}, u32[]{:S(2)}, u32[]{:S(2)}) collective-permute-start(f32[6,1,32,128]{3,2,1,0:T(8,128)} %get-tuple-element.53), channel_id=1, source_target_pairs={{4,0},{8,4},{12,8},{16,12},{20,16},{24,20},{28,24},{32,28},{36,32}... | collective-permute-start | bytes 294920 | tf_op jit(solution)/shard_map/ppermute | solution.py:526
  7.8 4.8 %rims.1 = (f32[54,2,32,128]{3,2,1,0:T(8,128)}, f32[54,2,32,128]{3,2,1,0:T(8,128)}, f32[54,4,2,128]{3,2,1,0:T(2,128)}, f32[54,4,2,128]{3,2,1,0:T(2,128)}) custom-call(f32[54,4,32,128]{3,2,1,0:T(8,128)} %y_ref.1), custom_call_target="tpu_custom_call" | custom-call | tf_op jit(solution)/shard_map/rims/pallas_call | solution.py:506
  12.7 0.0 collective-permute-done.lo_ref
  12.7 0.0 copy-start.1
  12.7 0.0 collective-permute-done.1.hi_ref
  12.7 0.6 copy-done.1
  13.3 0.0 copy-start.2
  13.3 0.6 copy-done.2
  13.9 1.5 %assemble.1 = f32[8,5760]{1,0:T(8,128)} custom-call(f32[8,5760]{1,0:T(8,128)} %get-tuple-element.51.packed_ref, f32[6,1,32,128]{3,2,1,0:T(8,128)} %copy-done.1, f32[6,1,32,128]{3,2,1,0:T(8,128)} %copy-done.2), custom_call_target="tpu_custom_call", output_to_operand_aliasing={{}: (0, {})} | custom-call | tf_op jit(solution)/shard_map/assemble/pallas_call | solution.py:528
  15.5 12.1 %all-gather = f32[32,5760]{1,0:T(8,128)} all-gather(f32[8,5760]{1,0:T(8,128)} %assemble.1), channel_id=2, replica_groups=mesh['space'=64,'group'=4] {'group'}, dimensions={0}, use_global_device_ids=true | all-gather | bytes 921600 | tf_op jit(solution)/shard_map/all_gather | solution.py:541
  27.6 4.1 %collective-permute-start.2 = (f32[54,2,32,128]{3,2,1,0:T(8,128)}, f32[54,2,32,128]{3,2,1,0:T(8,128)S(1)}, u32[]{:S(2)}, u32[]{:S(2)}) collective-permute-start(f32[54,2,32,128]{3,2,1,0:T(8,128)} %get-tuple-element.64), channel_id=1, source_target_pairs={{0,4},{4,8},{8,12},{12,16},{16,20},{20,24},{24,28},{28,32},{32,36}... | collective-permute-start | bytes 5308424 | tf_op jit(solution)/shard_map/ppermute | solution.py:546
  31.7 1.3 %collective-permute-start.3 = (f32[54,2,32,128]{3,2,1,0:T(8,128)}, f32[54,2,32,128]{3,2,1,0:T(8,128)}, u32[]{:S(2)}, u32[]{:S(2)}) collective-permute-start(f32[54,2,32,128]{3,2,1,0:T(8,128)} %get-tuple-element.65), channel_id=1, source_target_pairs={{4,0},{8,4},{12,8},{16,12},{20,16},{24,20},{28,24},{32,28},{36,32}... | collective-permute-start | bytes 5308424 | tf_op jit(solution)/shard_map/ppermute | solution.py:547
  33.0 3.6 %collective-permute-start.4 = (f32[54,4,2,128]{3,2,1,0:T(2,128)}, f32[54,4,2,128]{3,2,1,0:T(2,128)S(1)}, u32[]{:S(2)}, u32[]{:S(2)}) collective-permute-start(f32[54,4,2,128]{3,2,1,0:T(2,128)} %get-tuple-element.66), channel_id=1, source_target_pairs={{0,1},{1,2},{2,3},{4,5},{5,6},{6,7},{8,9},{9,10},{10,11},{12,13},{... | collective-permute-start | bytes 663560 | tf_op jit(solution)/shard_map/ppermute | solution.py:548
  37.3 13.0 %parcels.1 = (f32[7,4,32,128]{3,2,1,0:T(8,128)}, f32[7,1,32,128]{3,2,1,0:T(8,128)}, f32[7,1,32,128]{3,2,1,0:T(8,128)}, f32[8,16896]{1,0:T(8,128)}, f32[128,128]{1,0:T(8,128)}, /*index=5*/s32[8,128]{1,0:T(8,128)}) custom-call(s32[1]{0:T(128)} %copy.16.count_ref, f32[4,8,5760]{2,1,0:T(8,128)} %bitcast.5, f32[6,1,32,128]{3,2,1,0:T(8,128)} %copy-done.1, ...), custom_call_target="tpu_custom_call" | custom-call | tf_op jit(solution)/shard_map/parcels/pallas_call | solution.py:552
  50.3 0.0 collective-permute-done.4.ylo_ref
  50.3 0.0 copy-start.4
  50.3 1.9 %collective-permute-start.5 = (f32[54,4,2,128]{3,2,1,0:T(2,128)}, f32[54,4,2,128]{3,2,1,0:T(2,128)}, u32[]{:S(2)}, u32[]{:S(2)}) collective-permute-start(f32[54,4,2,128]{3,2,1,0:T(2,128)} %get-tuple-element.71), channel_id=1, source_target_pairs={{1,0},{2,1},{3,2},{5,4},{6,5},{7,6},{9,8},{10,9},{11,10},{13,12},{... | collective-permute-start | bytes 663560 | tf_op jit(solution)/shard_map/ppermute | solution.py:601
  52.3 4.9 %collective-permute-start.6 = (f32[7,1,32,128]{3,2,1,0:T(8,128)}, f32[7,1,32,128]{3,2,1,0:T(8,128)}, u32[]{:S(2)}, u32[]{:S(2)}) collective-permute-start(f32[7,1,32,128]{3,2,1,0:T(8,128)} %get-tuple-element.72), channel_id=1, source_target_pairs={{0,4},{4,8},{8,12},{12,16},{16,20},{20,24},{24,28},{28,32},{32,36}... | collective-permute-start | bytes 344072 | tf_op jit(solution)/shard_map/ppermute | solution.py:603
  57.2 1.3 %collective-permute-start.7 = (f32[7,1,32,128]{3,2,1,0:T(8,128)}, f32[7,1,32,128]{3,2,1,0:T(8,128)}, u32[]{:S(2)}, u32[]{:S(2)}) collective-permute-start(f32[7,1,32,128]{3,2,1,0:T(8,128)} %get-tuple-element.73), channel_id=1, source_target_pairs={{4,0},{8,4},{12,8},{16,12},{20,16},{24,20},{28,24},{32,28},{36,32}... | collective-permute-start | bytes 344072 | tf_op jit(solution)/shard_map/ppermute | solution.py:604
  58.5 5.0 %spread.1 = (f32[8,4096]{1,0:T(8,128)}, f32[8,4096]{1,0:T(8,128)}, f32[8,4096]{1,0:T(8,128)}, f32[8,4096]{1,0:T(8,128)}) custom-call(s32[8,128]{1,0:T(8,128)} %get-tuple-element.74.off_ref, f32[128,128]{1,0:T(8,128)} %get-tuple-element.75.dst_ref, f32[8,16896]{1,0:T(8,128)} %get-tuple-element.76.state_ref), custom_call_target="tpu_custom_call" | custom-call | tf_op jit(solution)/shard_map/spread/pallas_call | solution.py:606
  63.5 8.8 %collective-permute-done.6.rest_1_ = f32[7,1,32,128]{3,2,1,0:T(8,128)} collective-permute-done((f32[7,1,32,128]{3,2,1,0:T(8,128)}, f32[7,1,32,128]{3,2,1,0:T(8,128)}, u32[]{:S(2)}, u32[]{:S(2)}) %collective-permute-start.6) | collective-permute-done | bytes 114720 | tf_op jit(solution)/shard_map/ppermute | solution.py:603
  72.2 3.9 %collective-permute-done.7.rest_2_ = f32[7,1,32,128]{3,2,1,0:T(8,128)} collective-permute-done((f32[7,1,32,128]{3,2,1,0:T(8,128)}, f32[7,1,32,128]{3,2,1,0:T(8,128)}, u32[]{:S(2)}, u32[]{:S(2)}) %collective-permute-start.7) | collective-permute-done | bytes 114720 | tf_op jit(solution)/shard_map/ppermute | solution.py:604
  76.1 11.4 %collective-permute-done.5.yhi_ref = f32[54,4,2,128]{3,2,1,0:T(2,128)} collective-permute-done((f32[54,4,2,128]{3,2,1,0:T(2,128)}, f32[54,4,2,128]{3,2,1,0:T(2,128)}, u32[]{:S(2)}, u32[]{:S(2)}) %collective-permute-start.5) | collective-permute-done | bytes 221216 | tf_op jit(solution)/shard_map/ppermute | solution.py:601
  87.5 0.0 collective-permute-start.10
  87.5 3.2 %collective-permute-start.8 = (f32[8,4096]{1,0:T(8,128)}, f32[8,4096]{1,0:T(8,128)}, u32[]{:S(2)}, u32[]{:S(2)}) collective-permute-start(f32[8,4096]{1,0:T(8,128)} %get-tuple-element.88), channel_id=1, source_target_pairs={{0,1},{1,2},{2,3},{3,0},{4,5},{5,6},{6,7},{7,4},{8,9},{9,10},{10,1... | collective-permute-start | bytes 393224 | tf_op jit(solution)/shard_map/ppermute | solution.py:622
  90.7 0.0 collective-permute-start.9
  90.7 0.0 collective-permute-done.2.xlo_ref
  90.8 0.0 copy-start
  90.8 0.0 collective-permute-done.3.xhi_ref
  90.8 0.0 copy-done.4
  90.8 1.2 %copy-done = f32[54,2,32,128]{3,2,1,0:T(8,128)} copy-done((f32[54,2,32,128]{3,2,1,0:T(8,128)}, f32[54,2,32,128]{3,2,1,0:T(8,128)S(1)}, u32[]{:S(2)}) %copy-start) | copy-done | bytes 1769496
  92.0 0.0 copy-start.3
  92.0 0.0 copy-start.5
  92.0 0.0 copy-start.6
  92.0 0.0 copy-start.7
  92.0 7.9 %transport.1 = (f32[54,4,32,128]{3,2,1,0:T(8,128)}, f32[7,4,32,128]{3,2,1,0:T(8,128)}) custom-call(f32[54]{0:T(128)} %diff_ref.1, f32[54,4,32,128]{3,2,1,0:T(8,128)} %y_ref.1, f32[54,2,32,128]{3,2,1,0:T(8,128)} %copy-done, f32[54,2,32,128]{3,2,1,0:T(8,128)} %collective-permute-done.3.xhi_ref, f32[54,4,2,128]{3,2,1,0:T(2,128)} %copy-done.4, ...), custom_call_target="tpu_custom_call" | custom-call | tf_op jit(solution)/shard_map/transport/pallas_call | solution.py:640
  100.0 0.0 collective-permute-done.10
  100.0 0.0 collective-permute-done.8
  100.0 0.0 collective-permute-done.9
  100.0 0.0 copy-done.3
  100.0 0.0 copy-done.5
  100.0 0.0 copy-done.6
  100.0 0.0 copy-done.7
  100.0 1.8 %fusion = f32[5,4096]{1,0:T(8,128)} fusion(f32[8,4096]{1,0:T(8,128)} %collective-permute-done.10, f32[8,4096]{1,0:T(8,128)} %collective-permute-done.9, f32[8,4096]{1,0:T(8,128)} %collective-permute-done.8, f32[8,4096]{1,0:T(8,128)S(1)} %copy-done.5, f32[3,4096]{1,0:T(4,128)S(1)} %copy-done.3, f32[1,4096]{1,0:T(1,128)S(1)} %bitcast.7, ...), kind=kLoop, calls=%fused_computation.1 | loop fusion | flops 122880 | bytes 495616 | tf_op jit(solution)/shard_map/jit(_where)/select_n | solution.py:669
  (1 shorter events, 0.0 us)
Async XLA Ops:
  2.6 10.1 %collective-permute-start = (f32[6,1,32,128]{3,2,1,0:T(8,128)}, f32[6,1,32,128]{3,2,1,0:T(8,128)S(1)}, u32[]{:S(2)}, u32[]{:S(2)}) collective-permute-start(f32[6,1,32,128]{3,2,1,0:T(8,128)} %get-tuple-element.52), channel_id=1, source_target_pairs={{0,4},{4,8},{8,12},{12,16},{16,20},{20,24},{24,28},{28,32},{32,36}... | collective-permute-start | bytes 294920 | tf_op jit(solution)/shard_map/ppermute | solution.py:525
  6.5 6.1 %collective-permute-start.1 = (f32[6,1,32,128]{3,2,1,0:T(8,128)}, f32[6,1,32,128]{3,2,1,0:T(8,128)S(1)}, u32[]{:S(2)}, u32[]{:S(2)}) collective-permute-start(f32[6,1,32,128]{3,2,1,0:T(8,128)} %get-tuple-element.53), channel_id=1, source_target_pairs={{4,0},{8,4},{12,8},{16,12},{20,16},{24,20},{28,24},{32,28},{36,32}... | collective-permute-start | bytes 294920 | tf_op jit(solution)/shard_map/ppermute | solution.py:526
  12.7 0.6 copy-start.1
  13.3 0.6 copy-start.2
  27.6 63.1 %collective-permute-start.2 = (f32[54,2,32,128]{3,2,1,0:T(8,128)}, f32[54,2,32,128]{3,2,1,0:T(8,128)S(1)}, u32[]{:S(2)}, u32[]{:S(2)}) collective-permute-start(f32[54,2,32,128]{3,2,1,0:T(8,128)} %get-tuple-element.64), channel_id=1, source_target_pairs={{0,4},{4,8},{8,12},{12,16},{16,20},{20,24},{24,28},{28,32},{32,36}... | collective-permute-start | bytes 5308424 | tf_op jit(solution)/shard_map/ppermute | solution.py:546
  31.7 59.1 %collective-permute-start.3 = (f32[54,2,32,128]{3,2,1,0:T(8,128)}, f32[54,2,32,128]{3,2,1,0:T(8,128)}, u32[]{:S(2)}, u32[]{:S(2)}) collective-permute-start(f32[54,2,32,128]{3,2,1,0:T(8,128)} %get-tuple-element.65), channel_id=1, source_target_pairs={{4,0},{8,4},{12,8},{16,12},{20,16},{24,20},{28,24},{32,28},{36,32}... | collective-permute-start | bytes 5308424 | tf_op jit(solution)/shard_map/ppermute | solution.py:547
  33.0 17.3 %collective-permute-start.4 = (f32[54,4,2,128]{3,2,1,0:T(2,128)}, f32[54,4,2,128]{3,2,1,0:T(2,128)S(1)}, u32[]{:S(2)}, u32[]{:S(2)}) collective-permute-start(f32[54,4,2,128]{3,2,1,0:T(2,128)} %get-tuple-element.66), channel_id=1, source_target_pairs={{0,1},{1,2},{2,3},{4,5},{5,6},{6,7},{8,9},{9,10},{10,11},{12,13},{... | collective-permute-start | bytes 663560 | tf_op jit(solution)/shard_map/ppermute | solution.py:548
  50.3 40.5 %copy-start.4 = (f32[54,4,2,128]{3,2,1,0:T(2,128)}, f32[54,4,2,128]{3,2,1,0:T(2,128)S(1)}, u32[]{:S(2)}) copy-start(f32[54,4,2,128]{3,2,1,0:T(2,128)S(1)} %collective-permute-done.4.ylo_ref) | copy-start | bytes 663556
  50.3 37.1 %collective-permute-start.5 = (f32[54,4,2,128]{3,2,1,0:T(2,128)}, f32[54,4,2,128]{3,2,1,0:T(2,128)}, u32[]{:S(2)}, u32[]{:S(2)}) collective-permute-start(f32[54,4,2,128]{3,2,1,0:T(2,128)} %get-tuple-element.71), channel_id=1, source_target_pairs={{1,0},{2,1},{3,2},{5,4},{6,5},{7,6},{9,8},{10,9},{11,10},{13,12},{... | collective-permute-start | bytes 663560 | tf_op jit(solution)/shard_map/ppermute | solution.py:601
  52.3 19.9 %collective-permute-start.6 = (f32[7,1,32,128]{3,2,1,0:T(8,128)}, f32[7,1,32,128]{3,2,1,0:T(8,128)}, u32[]{:S(2)}, u32[]{:S(2)}) collective-permute-start(f32[7,1,32,128]{3,2,1,0:T(8,128)} %get-tuple-element.72), channel_id=1, source_target_pairs={{0,4},{4,8},{8,12},{12,16},{16,20},{20,24},{24,28},{28,32},{32,36}... | collective-permute-start | bytes 344072 | tf_op jit(solution)/shard_map/ppermute | solution.py:603
  57.2 18.9 %collective-permute-start.7 = (f32[7,1,32,128]{3,2,1,0:T(8,128)}, f32[7,1,32,128]{3,2,1,0:T(8,128)}, u32[]{:S(2)}, u32[]{:S(2)}) collective-permute-start(f32[7,1,32,128]{3,2,1,0:T(8,128)} %get-tuple-element.73), channel_id=1, source_target_pairs={{4,0},{8,4},{12,8},{16,12},{20,16},{24,20},{28,24},{32,28},{36,32}... | collective-permute-start | bytes 344072 | tf_op jit(solution)/shard_map/ppermute | solution.py:604
  87.5 12.5 %collective-permute-start.10 = (f32[8,4096]{1,0:T(8,128)}, f32[8,4096]{1,0:T(8,128)}, u32[]{:S(2)}, u32[]{:S(2)}) collective-permute-start(f32[8,4096]{1,0:T(8,128)} %get-tuple-element.90), channel_id=1, source_target_pairs={{0,3},{1,0},{2,1},{3,2},{4,7},{5,4},{6,5},{7,6},{8,11},{9,8},{10,9... | collective-permute-start | bytes 393224 | tf_op jit(solution)/shard_map/ppermute | solution.py:622
  87.5 12.5 %collective-permute-start.8 = (f32[8,4096]{1,0:T(8,128)}, f32[8,4096]{1,0:T(8,128)}, u32[]{:S(2)}, u32[]{:S(2)}) collective-permute-start(f32[8,4096]{1,0:T(8,128)} %get-tuple-element.88), channel_id=1, source_target_pairs={{0,1},{1,2},{2,3},{3,0},{4,5},{5,6},{6,7},{7,4},{8,9},{9,10},{10,1... | collective-permute-start | bytes 393224 | tf_op jit(solution)/shard_map/ppermute | solution.py:622
  90.7 9.3 %collective-permute-start.9 = (f32[8,4096]{1,0:T(8,128)}, f32[8,4096]{1,0:T(8,128)}, u32[]{:S(2)}, u32[]{:S(2)}) collective-permute-start(f32[8,4096]{1,0:T(8,128)} %get-tuple-element.89), channel_id=1, source_target_pairs={{0,2},{1,3},{2,0},{3,1},{4,6},{5,7},{6,4},{7,5},{8,10},{9,11},{10,... | collective-permute-start | bytes 393224 | tf_op jit(solution)/shard_map/ppermute | solution.py:622
  90.8 1.3 %copy-start = (f32[54,2,32,128]{3,2,1,0:T(8,128)}, f32[54,2,32,128]{3,2,1,0:T(8,128)S(1)}, u32[]{:S(2)}) copy-start(f32[54,2,32,128]{3,2,1,0:T(8,128)S(1)} %collective-permute-done.2.xlo_ref) | copy-start | bytes 5308420
  92.0 8.0 %copy-start.3 = (f32[3,4096]{1,0:T(4,128)S(1)}, f32[3,4096]{1,0:T(4,128)}, u32[]{:S(2)}) copy-start(f32[3,4096]{1,0:T(4,128)} %velocity_ref.1) | copy-start | bytes 147460
  92.0 8.0 %copy-start.5 = (f32[8,4096]{1,0:T(8,128)S(1)}, f32[8,4096]{1,0:T(8,128)}, u32[]{:S(2)}) copy-start(f32[8,4096]{1,0:T(8,128)} %get-tuple-element.93) | copy-start | bytes 393220
  92.0 8.0 %copy-start.6 = (f32[4096]{0:T(1024)S(1)}, f32[4096]{0:T(1024)}, u32[]{:S(2)}) copy-start(f32[4096]{0:T(1024)} %radius_ref.1) | copy-start | bytes 49156
  92.0 8.0 %copy-start.7 = (f32[4096]{0:T(1024)S(1)}, f32[4096]{0:T(1024)}, u32[]{:S(2)}) copy-start(f32[4096]{0:T(1024)} %temp_ref.2) | copy-start | bytes 49156

commit v4 on v3

--- a/solution.py
+++ b/solution.py
@@ -466,7 +466,8 @@
     smem = pl.BlockSpec(memory_space=pltpu.SMEM)
     hbm = pl.BlockSpec(memory_space=pl.ANY)
     shaped = lambda *shape: jax.ShapeDtypeStruct(shape, F32)
-    limit = pltpu.CompilerParams(vmem_limit_bytes=62 * 2**20)
+    limit = pltpu.CompilerParams(vmem_limit_bytes=63 * 2**20)
+    little = pltpu.CompilerParams(vmem_limit_bytes=2 * 2**20)
 
     def by_kind(first, *shape):
         return pl.BlockSpec((MANY,) + shape, lambda i: (first + i, 0, 0, 0))
@@ -532,7 +533,7 @@
         out_specs=pl.BlockSpec((8, tail), lambda i: (0, width // tail - 1)),
         out_shape=shaped(8, width),
         input_output_aliases={0: 0},
-        compiler_params=limit,
+        compiler_params=little,
         name="assemble",
     )(packed, field_lo, field_hi)
     sent, x_up, x_down, y_right, y_left = lax.optimization_barrier(
@@ -543,9 +544,11 @@
     x_up, x_down, y_right, y_left, parcels = lax.optimization_barrier(
         (x_up, x_down, y_right, y_left, parcels)
     )
+    y_lo = lax.ppermute(y_right, "group", g_ahead)
+    y_hi = lax.ppermute(y_left, "group", g_back)
+    x_up, x_down, y_lo, y_hi = lax.optimization_barrier((x_up, x_down, y_lo, y_hi))
     x_lo = lax.ppermute(x_up, "space", ahead)
     x_hi = lax.ppermute(x_down, "space", back)
-    y_lo = lax.ppermute(y_right, "group", g_ahead)
 
     chunks = pl.cdiv(slots, CHUNK)
     reach = max(chunks * CHUNK, slots + WINDOW)
@@ -597,9 +600,6 @@
         name="parcels",
     )(parcel_counts, parcels, field_lo, gas_temp, gas_density, gas_velocity, species, field_hi)
 
-    y_lo, y_left, state = lax.optimization_barrier((y_lo, y_left, state))
-    y_hi = lax.ppermute(y_left, "group", g_back)
-
     from_below = lax.ppermute(dep_hi, "space", ahead)
     from_above = lax.ppermute(dep_lo, "space", back)
 
@@ -613,13 +613,6 @@
         compiler_params=limit,
         name="spread",
     )(off, dst, state)
-    y_lo, y_hi, from_below, from_above, spread = lax.optimization_barrier(
-        (y_lo, y_hi, from_below, from_above, spread)
-    )
-    returned = [spread[0]]
-    for d in range(1, groups):
-        route = [(i, (i + d) % groups) for i in range(groups)]
-        returned.append(lax.ppermute(spread[d], "group", route))
     gas = pl.BlockSpec((planes, rows, depth), lambda i: (0, 0, 0))
     row0 = pl.BlockSpec((None, planes, rows, depth), lambda i: (0, 0, 0, 0))
     all_gas = whole((7, planes, rows, depth))
@@ -661,7 +654,11 @@
         species_next = got[0]
         if c == 0:
             gas_sources = got[1]
-    species_next, returned = lax.optimization_barrier((species_next, returned))
+    species_next, spread = lax.optimization_barrier((species_next, spread))
+    returned = [spread[0]]
+    for d in range(1, groups):
+        route = [(i, (i + d) % groups) for i in range(groups)]
+        returned.append(lax.ppermute(spread[d], "group", route))
     new_state = sum(returned[1:], returned[0])
     old_state = jnp.concatenate([drop_radius[None], drop_temp[None], drop_velocity], axis=0)
     slot = lax.axis_index("group") * capacity + jnp.arange(capacity, dtype=jnp.int32)

time: 103 us -> 109 us (1.058)
  the two profiles are of different devices: /device:TPU:1 before, /device:TPU:25 now
where the time goes in v4:
time: 109 us; the launch traced here: 108 us
  starting transfers between devices  48.2 us (44%)
  Pallas kernels  37.4 us (34%)
  blocking collectives  10.4 us (10%)
  waiting for transfers between devices  8.58 us (8%)
  between operations  1.51 us (1%)
    pallas_call x1, Pallas kernels, per_device(): pl.pallas_call(parcel_kernel, grid=(1,), in_specs=[smem, whole((groups, 8...  17.6 us
    ppermute x3, starting transfers between devices, per_device(): returned.append(lax.ppermute(spread[d], 'group', route))  13.1 us
    all_gather x1, blocking collectives, per_device(): parcels = lax.all_gather(sent, 'group', axis=0)  10.4 us
    ppermute x1, starting transfers between devices, per_device(): field_hi = lax.ppermute(bottom, 'space', back)  8.66 us
    pallas_call x1, Pallas kernels, per_device(): pl.pallas_call(functools.partial(transport_kernel, c == 0, first), grid=(...  7.99 us
    ppermute x1, starting transfers between devices, per_device(): x_hi = lax.ppermute(x_down, 'space', back)  7.58 us
    ppermute x1, starting transfers between devices, per_device(): from_above = lax.ppermute(dep_lo, 'space', back)  7.13 us
    ppermute x3, waiting for transfers between devices, per_device(): returned.append(lax.ppermute(spread[d], 'group', route))  5.14 us
  transfers between devices with their start and end apart: 11, of which 4 were waited for; matrix products, arithmetic and copies ran while one was open for 0% of the time, Pallas kernels for 26%

profile of v4, /device:TPU:25, one launch (start us, length us, event | category | flops | bytes accessed | tf_op | source)
XLA Modules:
  0.0 107.5 jit_solution(14781429805050579855)
XLA Ops:
  0.6 1.9 %pack.1 = (f32[8,5760]{1,0:T(8,128)}, f32[6,1,32,128]{3,2,1,0:T(8,128)}, f32[6,1,32,128]{3,2,1,0:T(8,128)}) custom-call(s32[8,4096]{1,0:T(8,128)} %cells_ref.1, f32[8,4096]{1,0:T(8,128)} %weights_ref.1, f32[4096]{0:T(1024)} %radius_ref.1, f32[4096]{0:T(1024)} %temp_ref.2, f32[3,4096]{1,0:T(4,128)} %velocity_ref.1, f32[4,32,128]{2,1,0:T(8,128)} %temp_ref.3, ...), custom_call_target="tpu_custom_call" | custom-call | tf_op jit(solution)/shard_map/pack/pallas_call | solution.py:476
  2.5 3.1 %collective-permute-start = (f32[6,1,32,128]{3,2,1,0:T(8,128)}, f32[6,1,32,128]{3,2,1,0:T(8,128)S(1)}, u32[]{:S(2)}, u32[]{:S(2)}) collective-permute-start(f32[6,1,32,128]{3,2,1,0:T(8,128)} %get-tuple-element.45), channel_id=1, source_target_pairs={{0,4},{4,8},{8,12},{12,16},{16,20},{20,24},{24,28},{28,32},{32,36}... | collective-permute-start | bytes 294920 | tf_op jit(solution)/shard_map/ppermute | solution.py:526
  5.7 8.7 %collective-permute-start.1 = (f32[6,1,32,128]{3,2,1,0:T(8,128)}, f32[6,1,32,128]{3,2,1,0:T(8,128)S(1)}, u32[]{:S(2)}, u32[]{:S(2)}) collective-permute-start(f32[6,1,32,128]{3,2,1,0:T(8,128)} %get-tuple-element.46), channel_id=1, source_target_pairs={{4,0},{8,4},{12,8},{16,12},{20,16},{24,20},{28,24},{32,28},{36,32}... | collective-permute-start | bytes 294920 | tf_op jit(solution)/shard_map/ppermute | solution.py:527
  14.3 0.0 copy-start
  14.3 4.9 %rims.1 = (f32[54,2,32,128]{3,2,1,0:T(8,128)}, f32[54,2,32,128]{3,2,1,0:T(8,128)}, f32[54,4,2,128]{3,2,1,0:T(2,128)}, f32[54,4,2,128]{3,2,1,0:T(2,128)}) custom-call(f32[54,4,32,128]{3,2,1,0:T(8,128)} %y_ref.1), custom_call_target="tpu_custom_call" | custom-call | tf_op jit(solution)/shard_map/rims/pallas_call | solution.py:507
  19.2 0.0 collective-permute-done.lo_ref
  19.2 0.0 collective-permute-done.1.hi_ref
  19.2 0.0 copy-done
  19.3 0.0 copy-start.2
  19.3 10.4 %all-gather = f32[32,5760]{1,0:T(8,128)} all-gather(f32[8,5760]{1,0:T(8,128)S(1)} %assemble.1), channel_id=2, replica_groups=mesh['space'=64,'group'=4] {'group'}, dimensions={0}, use_global_device_ids=true | all-gather | bytes 921600 | tf_op jit(solution)/shard_map/all_gather | solution.py:542
  29.7 1.3 %collective-permute-start.2 = (f32[54,4,2,128]{3,2,1,0:T(2,128)}, f32[54,4,2,128]{3,2,1,0:T(2,128)S(1)}, u32[]{:S(2)}, u32[]{:S(2)}) collective-permute-start(f32[54,4,2,128]{3,2,1,0:T(2,128)} %get-tuple-element.59), channel_id=1, source_target_pairs={{0,1},{1,2},{2,3},{4,5},{5,6},{6,7},{8,9},{9,10},{10,11},{12,13},{... | collective-permute-start | bytes 663560 | tf_op jit(solution)/shard_map/ppermute | solution.py:547
  31.0 3.0 %collective-permute-start.3 = (f32[54,4,2,128]{3,2,1,0:T(2,128)}, f32[54,4,2,128]{3,2,1,0:T(2,128)S(1)}, u32[]{:S(2)}, u32[]{:S(2)}) collective-permute-start(f32[54,4,2,128]{3,2,1,0:T(2,128)} %get-tuple-element.60), channel_id=1, source_target_pairs={{1,0},{2,1},{3,2},{5,4},{6,5},{7,6},{9,8},{10,9},{11,10},{13,12},{... | collective-permute-start | bytes 663560 | tf_op jit(solution)/shard_map/ppermute | solution.py:548
  34.0 0.0 collective-permute-done.2.ylo_ref
  34.0 0.0 copy-start.4
  34.0 1.3 %collective-permute-done.3.yhi_ref = f32[54,4,2,128]{3,2,1,0:T(2,128)S(1)} collective-permute-done((f32[54,4,2,128]{3,2,1,0:T(2,128)}, f32[54,4,2,128]{3,2,1,0:T(2,128)S(1)}, u32[]{:S(2)}, u32[]{:S(2)}) %collective-permute-start.3) | collective-permute-done | bytes 221216 | tf_op jit(solution)/shard_map/ppermute | solution.py:548
  35.3 1.9 %collective-permute-start.4 = (f32[54,2,32,128]{3,2,1,0:T(8,128)}, f32[54,2,32,128]{3,2,1,0:T(8,128)}, u32[]{:S(2)}, u32[]{:S(2)}) collective-permute-start(f32[54,2,32,128]{3,2,1,0:T(8,128)} %get-tuple-element.61), channel_id=1, source_target_pairs={{0,4},{4,8},{8,12},{12,16},{16,20},{20,24},{24,28},{28,32},{32,36}... | collective-permute-start | bytes 5308424 | tf_op jit(solution)/shard_map/ppermute | solution.py:550
  37.2 7.6 %collective-permute-start.5 = (f32[54,2,32,128]{3,2,1,0:T(8,128)}, f32[54,2,32,128]{3,2,1,0:T(8,128)}, u32[]{:S(2)}, u32[]{:S(2)}) collective-permute-start(f32[54,2,32,128]{3,2,1,0:T(8,128)} %get-tuple-element.62), channel_id=1, source_target_pairs={{4,0},{8,4},{12,8},{16,12},{20,16},{24,20},{28,24},{32,28},{36,32}... | collective-permute-start | bytes 5308424 | tf_op jit(solution)/shard_map/ppermute | solution.py:551
  45.5 0.0 copy-done.1
  45.5 0.0 copy-done.2
  45.5 17.6 %parcels.1 = (f32[7,4,32,128]{3,2,1,0:T(8,128)}, f32[7,1,32,128]{3,2,1,0:T(8,128)}, f32[7,1,32,128]{3,2,1,0:T(8,128)}, f32[8,16896]{1,0:T(8,128)}, f32[128,128]{1,0:T(8,128)}, /*index=5*/s32[8,128]{1,0:T(8,128)}) custom-call(s32[1]{0:T(128)} %copy.16.count_ref, f32[4,8,5760]{2,1,0:T(8,128)} %bitcast.5, f32[6,1,32,128]{3,2,1,0:T(8,128)} %copy-done.1, ...), custom_call_target="tpu_custom_call" | custom-call | tf_op jit(solution)/shard_map/parcels/pallas_call | solution.py:555
  63.1 0.0 copy-done.4
  63.2 0.0 copy-done.5
  63.2 2.4 %collective-permute-start.6 = (f32[7,1,32,128]{3,2,1,0:T(8,128)}, f32[7,1,32,128]{3,2,1,0:T(8,128)S(1)}, u32[]{:S(2)}, u32[]{:S(2)}) collective-permute-start(f32[7,1,32,128]{3,2,1,0:T(8,128)} %get-tuple-element.67), channel_id=1, source_target_pairs={{0,4},{4,8},{8,12},{12,16},{16,20},{20,24},{24,28},{28,32},{32,36}... | collective-permute-start | bytes 344072 | tf_op jit(solution)/shard_map/ppermute | solution.py:603
  65.5 7.1 %collective-permute-start.7 = (f32[7,1,32,128]{3,2,1,0:T(8,128)}, f32[7,1,32,128]{3,2,1,0:T(8,128)S(1)}, u32[]{:S(2)}, u32[]{:S(2)}) collective-permute-start(f32[7,1,32,128]{3,2,1,0:T(8,128)} %get-tuple-element.68), channel_id=1, source_target_pairs={{4,0},{8,4},{12,8},{16,12},{20,16},{24,20},{28,24},{32,28},{36,32}... | collective-permute-start | bytes 344072 | tf_op jit(solution)/shard_map/ppermute | solution.py:604
  72.7 5.0 %spread.1 = (f32[8,4096]{1,0:T(8,128)}, f32[8,4096]{1,0:T(8,128)}, f32[8,4096]{1,0:T(8,128)}, f32[8,4096]{1,0:T(8,128)}) custom-call(s32[8,128]{1,0:T(8,128)} %get-tuple-element.70.off_ref, f32[128,128]{1,0:T(8,128)} %get-tuple-element.71.dst_ref, f32[8,16896]{1,0:T(8,128)} %get-tuple-element.72.state_ref), custom_call_target="tpu_custom_call" | custom-call | tf_op jit(solution)/shard_map/spread/pallas_call | solution.py:606
  77.7 1.3 %collective-permute-done.6.rest_1_ = f32[7,1,32,128]{3,2,1,0:T(8,128)S(1)} collective-permute-done((f32[7,1,32,128]{3,2,1,0:T(8,128)}, f32[7,1,32,128]{3,2,1,0:T(8,128)S(1)}, u32[]{:S(2)}, u32[]{:S(2)}) %collective-permute-start.6) | collective-permute-done | bytes 114720 | tf_op jit(solution)/shard_map/ppermute | solution.py:603
  78.9 0.9 collective-permute-done.7.rest_2_
  79.8 0.0 collective-permute-done.4.xlo_ref
  79.8 0.0 collective-permute-done.5.xhi_ref
  79.8 0.0 copy-done.7
  79.9 0.6 copy-done.8
  80.5 0.0 copy-start.6
  80.5 0.0 copy-start.9
  80.5 0.0 copy-start.10
  80.5 8.0 %transport.1 = (f32[54,4,32,128]{3,2,1,0:T(8,128)}, f32[7,4,32,128]{3,2,1,0:T(8,128)}) custom-call(f32[54]{0:T(128)} %diff_ref.1, f32[54,4,32,128]{3,2,1,0:T(8,128)} %y_ref.1, f32[54,2,32,128]{3,2,1,0:T(8,128)} %collective-permute-done.4.xlo_ref, f32[54,2,32,128]{3,2,1,0:T(8,128)} %collective-permute-done.5.xhi_ref, f32[54,4,2,128]{3,2,1,0:T(2,128)} %copy-done.4, ...), custom_call_target="tpu_custom_call" | custom-call | tf_op jit(solution)/shard_map/transport/pallas_call | solution.py:633
  88.5 0.0 copy-done.13
  88.5 6.6 %collective-permute-start.10 = (f32[8,4096]{1,0:T(8,128)S(1)}, f32[8,4096]{1,0:T(8,128)S(1)}, u32[]{:S(2)}, u32[]{:S(2)}) collective-permute-start(f32[8,4096]{1,0:T(8,128)S(1)} %copy-done.13), channel_id=1, source_target_pairs={{0,3},{1,0},{2,1},{3,2},{4,7},{5,4},{6,5},{7,6},{8,11},{9,8},{10,9... | collective-permute-start | bytes 393224 | tf_op jit(solution)/shard_map/ppermute | solution.py:661
  95.1 0.0 copy-done.12
  95.2 0.0 collective-permute-start.8
  95.2 0.0 copy-done.11
  95.2 6.5 %collective-permute-start.9 = (f32[8,4096]{1,0:T(8,128)S(1)}, f32[8,4096]{1,0:T(8,128)S(1)}, u32[]{:S(2)}, u32[]{:S(2)}) collective-permute-start(f32[8,4096]{1,0:T(8,128)S(1)} %copy-done.11), channel_id=1, source_target_pairs={{0,2},{1,3},{2,0},{3,1},{4,6},{5,7},{6,4},{7,5},{8,10},{9,11},{10,... | collective-permute-start | bytes 393224 | tf_op jit(solution)/shard_map/ppermute | solution.py:661
  101.7 0.0 collective-permute-done.10
  101.7 0.0 collective-permute-done.8
  101.7 5.1 %collective-permute-done.9 = f32[8,4096]{1,0:T(8,128)S(1)} collective-permute-done((f32[8,4096]{1,0:T(8,128)S(1)}, f32[8,4096]{1,0:T(8,128)S(1)}, u32[]{:S(2)}, u32[]{:S(2)}) %collective-permute-start.9) | collective-permute-done | bytes 131104 | tf_op jit(solution)/shard_map/ppermute | solution.py:661
  106.8 0.0 copy-done.3
  106.8 0.0 copy-done.6
  106.8 0.0 copy-done.9
  106.8 0.7 fusion
  (11 shorter events, 0.0 us)
Async XLA Ops:
  2.5 16.7 %collective-permute-start = (f32[6,1,32,128]{3,2,1,0:T(8,128)}, f32[6,1,32,128]{3,2,1,0:T(8,128)S(1)}, u32[]{:S(2)}, u32[]{:S(2)}) collective-permute-start(f32[6,1,32,128]{3,2,1,0:T(8,128)} %get-tuple-element.45), channel_id=1, source_target_pairs={{0,4},{4,8},{8,12},{12,16},{16,20},{20,24},{24,28},{28,32},{32,36}... | collective-permute-start | bytes 294920 | tf_op jit(solution)/shard_map/ppermute | solution.py:526
  5.7 13.6 %collective-permute-start.1 = (f32[6,1,32,128]{3,2,1,0:T(8,128)}, f32[6,1,32,128]{3,2,1,0:T(8,128)S(1)}, u32[]{:S(2)}, u32[]{:S(2)}) collective-permute-start(f32[6,1,32,128]{3,2,1,0:T(8,128)} %get-tuple-element.46), channel_id=1, source_target_pairs={{4,0},{8,4},{12,8},{16,12},{20,16},{24,20},{28,24},{32,28},{36,32}... | collective-permute-start | bytes 294920 | tf_op jit(solution)/shard_map/ppermute | solution.py:527
  14.3 4.9 %copy-start = (f32[8,5760]{1,0:T(8,128)S(1)}, f32[8,5760]{1,0:T(8,128)}, u32[]{:S(2)}) copy-start(f32[8,5760]{1,0:T(8,128)} %get-tuple-element.44.packed_ref) | copy-start | bytes 552964
  19.2 26.2 %copy-start.1 = (f32[6,1,32,128]{3,2,1,0:T(8,128)}, f32[6,1,32,128]{3,2,1,0:T(8,128)S(1)}, u32[]{:S(2)}) copy-start(f32[6,1,32,128]{3,2,1,0:T(8,128)S(1)} %collective-permute-done.lo_ref) | copy-start | bytes 294916
  19.3 26.2 %copy-start.2 = (f32[6,1,32,128]{3,2,1,0:T(8,128)}, f32[6,1,32,128]{3,2,1,0:T(8,128)S(1)}, u32[]{:S(2)}) copy-start(f32[6,1,32,128]{3,2,1,0:T(8,128)S(1)} %collective-permute-done.1.hi_ref) | copy-start | bytes 294916
  29.7 4.3 %collective-permute-start.2 = (f32[54,4,2,128]{3,2,1,0:T(2,128)}, f32[54,4,2,128]{3,2,1,0:T(2,128)S(1)}, u32[]{:S(2)}, u32[]{:S(2)}) collective-permute-start(f32[54,4,2,128]{3,2,1,0:T(2,128)} %get-tuple-element.59), channel_id=1, source_target_pairs={{0,1},{1,2},{2,3},{4,5},{5,6},{6,7},{8,9},{9,10},{10,11},{12,13},{... | collective-permute-start | bytes 663560 | tf_op jit(solution)/shard_map/ppermute | solution.py:547
  31.0 4.3 %collective-permute-start.3 = (f32[54,4,2,128]{3,2,1,0:T(2,128)}, f32[54,4,2,128]{3,2,1,0:T(2,128)S(1)}, u32[]{:S(2)}, u32[]{:S(2)}) collective-permute-start(f32[54,4,2,128]{3,2,1,0:T(2,128)} %get-tuple-element.60), channel_id=1, source_target_pairs={{1,0},{2,1},{3,2},{5,4},{6,5},{7,6},{9,8},{10,9},{11,10},{13,12},{... | collective-permute-start | bytes 663560 | tf_op jit(solution)/shard_map/ppermute | solution.py:548
  34.0 29.1 %copy-start.4 = (f32[54,4,2,128]{3,2,1,0:T(2,128)}, f32[54,4,2,128]{3,2,1,0:T(2,128)S(1)}, u32[]{:S(2)}) copy-start(f32[54,4,2,128]{3,2,1,0:T(2,128)S(1)} %collective-permute-done.2.ylo_ref) | copy-start | bytes 663556
  35.3 27.8 %copy-start.5 = (f32[54,4,2,128]{3,2,1,0:T(2,128)}, f32[54,4,2,128]{3,2,1,0:T(2,128)S(1)}, u32[]{:S(2)}) copy-start(f32[54,4,2,128]{3,2,1,0:T(2,128)S(1)} %collective-permute-done.3.yhi_ref) | copy-start | bytes 663556
  35.3 44.5 %collective-permute-start.4 = (f32[54,2,32,128]{3,2,1,0:T(8,128)}, f32[54,2,32,128]{3,2,1,0:T(8,128)}, u32[]{:S(2)}, u32[]{:S(2)}) collective-permute-start(f32[54,2,32,128]{3,2,1,0:T(8,128)} %get-tuple-element.61), channel_id=1, source_target_pairs={{0,4},{4,8},{8,12},{12,16},{16,20},{20,24},{24,28},{28,32},{32,36}... | collective-permute-start | bytes 5308424 | tf_op jit(solution)/shard_map/ppermute | solution.py:550
  37.2 42.6 %collective-permute-start.5 = (f32[54,2,32,128]{3,2,1,0:T(8,128)}, f32[54,2,32,128]{3,2,1,0:T(8,128)}, u32[]{:S(2)}, u32[]{:S(2)}) collective-permute-start(f32[54,2,32,128]{3,2,1,0:T(8,128)} %get-tuple-element.62), channel_id=1, source_target_pairs={{4,0},{8,4},{12,8},{16,12},{20,16},{24,20},{28,24},{32,28},{36,32}... | collective-permute-start | bytes 5308424 | tf_op jit(solution)/shard_map/ppermute | solution.py:551
  63.2 15.8 %collective-permute-start.6 = (f32[7,1,32,128]{3,2,1,0:T(8,128)}, f32[7,1,32,128]{3,2,1,0:T(8,128)S(1)}, u32[]{:S(2)}, u32[]{:S(2)}) collective-permute-start(f32[7,1,32,128]{3,2,1,0:T(8,128)} %get-tuple-element.67), channel_id=1, source_target_pairs={{0,4},{4,8},{8,12},{12,16},{16,20},{20,24},{24,28},{28,32},{32,36}... | collective-permute-start | bytes 344072 | tf_op jit(solution)/shard_map/ppermute | solution.py:603
  65.5 14.3 %collective-permute-start.7 = (f32[7,1,32,128]{3,2,1,0:T(8,128)}, f32[7,1,32,128]{3,2,1,0:T(8,128)S(1)}, u32[]{:S(2)}, u32[]{:S(2)}) collective-permute-start(f32[7,1,32,128]{3,2,1,0:T(8,128)} %get-tuple-element.68), channel_id=1, source_target_pairs={{4,0},{8,4},{12,8},{16,12},{20,16},{24,20},{28,24},{32,28},{36,32}... | collective-permute-start | bytes 344072 | tf_op jit(solution)/shard_map/ppermute | solution.py:604
  78.9 0.9 copy-start.7
  79.8 0.6 copy-start.8
  80.5 8.0 %copy-start.13 = (f32[8,4096]{1,0:T(8,128)S(1)}, f32[8,4096]{1,0:T(8,128)}, u32[]{:S(2)}) copy-start(f32[8,4096]{1,0:T(8,128)} %get-tuple-element.82) | copy-start | bytes 393220
  80.5 14.7 %copy-start.12 = (f32[8,4096]{1,0:T(8,128)S(1)}, f32[8,4096]{1,0:T(8,128)}, u32[]{:S(2)}) copy-start(f32[8,4096]{1,0:T(8,128)} %get-tuple-element.80) | copy-start | bytes 393220
  80.5 14.7 %copy-start.11 = (f32[8,4096]{1,0:T(8,128)S(1)}, f32[8,4096]{1,0:T(8,128)}, u32[]{:S(2)}) copy-start(f32[8,4096]{1,0:T(8,128)} %get-tuple-element.81) | copy-start | bytes 393220
  80.5 26.3 %copy-start.3 = (f32[3,4096]{1,0:T(4,128)S(1)}, f32[3,4096]{1,0:T(4,128)}, u32[]{:S(2)}) copy-start(f32[3,4096]{1,0:T(4,128)} %velocity_ref.1) | copy-start | bytes 147460
  80.5 26.3 %copy-start.6 = (f32[8,4096]{1,0:T(8,128)S(1)}, f32[8,4096]{1,0:T(8,128)}, u32[]{:S(2)}) copy-start(f32[8,4096]{1,0:T(8,128)} %get-tuple-element.79) | copy-start | bytes 393220
  80.5 26.3 %copy-start.9 = (f32[4096]{0:T(1024)S(1)}, f32[4096]{0:T(1024)}, u32[]{:S(2)}) copy-start(f32[4096]{0:T(1024)} %radius_ref.1) | copy-start | bytes 49156
  80.5 26.3 %copy-start.10 = (f32[4096]{0:T(1024)S(1)}, f32[4096]{0:T(1024)}, u32[]{:S(2)}) copy-start(f32[4096]{0:T(1024)} %temp_ref.2) | copy-start | bytes 49156
  88.5 13.1 %collective-permute-start.10 = (f32[8,4096]{1,0:T(8,128)S(1)}, f32[8,4096]{1,0:T(8,128)S(1)}, u32[]{:S(2)}, u32[]{:S(2)}) collective-permute-start(f32[8,4096]{1,0:T(8,128)S(1)} %copy-done.13), channel_id=1, source_target_pairs={{0,3},{1,0},{2,1},{3,2},{4,7},{5,4},{6,5},{7,6},{8,11},{9,8},{10,9... | collective-permute-start | bytes 393224 | tf_op jit(solution)/shard_map/ppermute | solution.py:661
  95.2 6.5 %collective-permute-start.8 = (f32[8,4096]{1,0:T(8,128)S(1)}, f32[8,4096]{1,0:T(8,128)S(1)}, u32[]{:S(2)}, u32[]{:S(2)}) collective-permute-start(f32[8,4096]{1,0:T(8,128)S(1)} %copy-done.12), channel_id=1, source_target_pairs={{0,1},{1,2},{2,3},{3,0},{4,5},{5,6},{6,7},{7,4},{8,9},{9,10},{10,1... | collective-permute-start | bytes 393224 | tf_op jit(solution)/shard_map/ppermute | solution.py:661
  95.2 11.6 %collective-permute-start.9 = (f32[8,4096]{1,0:T(8,128)S(1)}, f32[8,4096]{1,0:T(8,128)S(1)}, u32[]{:S(2)}, u32[]{:S(2)}) collective-permute-start(f32[8,4096]{1,0:T(8,128)S(1)} %copy-done.11), channel_id=1, source_target_pairs={{0,2},{1,3},{2,0},{3,1},{4,6},{5,7},{6,4},{7,5},{8,10},{9,11},{10,... | collective-permute-start | bytes 393224 | tf_op jit(solution)/shard_map/ppermute | solution.py:661

commit v5 on v3

--- a/solution.py
+++ b/solution.py
@@ -466,7 +466,8 @@
     smem = pl.BlockSpec(memory_space=pltpu.SMEM)
     hbm = pl.BlockSpec(memory_space=pl.ANY)
     shaped = lambda *shape: jax.ShapeDtypeStruct(shape, F32)
-    limit = pltpu.CompilerParams(vmem_limit_bytes=62 * 2**20)
+    limit = pltpu.CompilerParams(vmem_limit_bytes=63 * 2**20)
+    little = pltpu.CompilerParams(vmem_limit_bytes=2 * 2**20)
 
     def by_kind(first, *shape):
         return pl.BlockSpec((MANY,) + shape, lambda i: (first + i, 0, 0, 0))
@@ -532,7 +533,7 @@
         out_specs=pl.BlockSpec((8, tail), lambda i: (0, width // tail - 1)),
         out_shape=shaped(8, width),
         input_output_aliases={0: 0},
-        compiler_params=limit,
+        compiler_params=little,
         name="assemble",
     )(packed, field_lo, field_hi)
     sent, x_up, x_down, y_right, y_left = lax.optimization_barrier(

time: 103 us -> 108 us (1.049)
  the two profiles are of different devices: /device:TPU:1 before, /device:TPU:239 now
where the time goes in v5:
time: 108 us; the launch traced here: 107 us
  Pallas kernels  32.7 us (30%)
  starting transfers between devices  30.5 us (28%)
  waiting for transfers between devices  29.9 us (28%)
  blocking collectives  10.7 us (10%)
  other arithmetic  1.71 us (2%)
  between operations  1.57 us (1%)
    ppermute x1, waiting for transfers between devices, per_device(): y_lo = lax.ppermute(y_right, 'group', g_ahead)  29.9 us
    pallas_call x1, Pallas kernels, per_device(): pl.pallas_call(parcel_kernel, grid=(1,), in_specs=[smem, whole((groups, 8...  13 us
    all_gather x1, blocking collectives, per_device(): parcels = lax.all_gather(sent, 'group', axis=0)  10.7 us
    pallas_call x1, Pallas kernels, per_device(): pl.pallas_call(functools.partial(transport_kernel, c == 0, first), grid=(...  7.91 us
    ppermute x3, starting transfers between devices, per_device(): returned.append(lax.ppermute(spread[d], 'group', route))  7.28 us
    ppermute x1, starting transfers between devices, per_device(): x_hi = lax.ppermute(x_down, 'space', back)  5.23 us
    pallas_call x1, Pallas kernels, per_device(): pl.pallas_call(spread_kernel, grid=(1,), in_specs=[smem, whole((blocks, L...  4.97 us
    pallas_call x1, Pallas kernels, per_device(): pl.pallas_call(rims_kernel, grid=(kinds // MANY,), in_specs=[by_kind(0, p...  4.89 us
  transfers between devices with their start and end apart: 11, of which 1 were waited for; matrix products, arithmetic and copies ran while one was open for 0% of the time, Pallas kernels for 29%

profile of v5, /device:TPU:239, one launch (start us, length us, event | category | flops | bytes accessed | tf_op | source)
XLA Modules:
  0.0 107.1 jit_solution(16937897427659020028)
XLA Ops:
  0.6 1.9 %pack.1 = (f32[8,5760]{1,0:T(8,128)}, f32[6,1,32,128]{3,2,1,0:T(8,128)}, f32[6,1,32,128]{3,2,1,0:T(8,128)}) custom-call(s32[8,4096]{1,0:T(8,128)} %cells_ref.1, f32[8,4096]{1,0:T(8,128)} %weights_ref.1, f32[4096]{0:T(1024)} %radius_ref.1, f32[4096]{0:T(1024)} %temp_ref.2, f32[3,4096]{1,0:T(4,128)} %velocity_ref.1, f32[4,32,128]{2,1,0:T(8,128)} %temp_ref.3, ...), custom_call_target="tpu_custom_call" | custom-call | tf_op jit(solution)/shard_map/pack/pallas_call | solution.py:476
  2.5 1.3 %collective-permute-start = (f32[6,1,32,128]{3,2,1,0:T(8,128)}, f32[6,1,32,128]{3,2,1,0:T(8,128)S(1)}, u32[]{:S(2)}, u32[]{:S(2)}) collective-permute-start(f32[6,1,32,128]{3,2,1,0:T(8,128)} %get-tuple-element.52), channel_id=1, source_target_pairs={{0,4},{4,8},{8,12},{12,16},{16,20},{20,24},{24,28},{28,32},{32,36}... | collective-permute-start | bytes 294920 | tf_op jit(solution)/shard_map/ppermute | solution.py:526
  3.8 4.0 %collective-permute-start.1 = (f32[6,1,32,128]{3,2,1,0:T(8,128)}, f32[6,1,32,128]{3,2,1,0:T(8,128)S(1)}, u32[]{:S(2)}, u32[]{:S(2)}) collective-permute-start(f32[6,1,32,128]{3,2,1,0:T(8,128)} %get-tuple-element.53), channel_id=1, source_target_pairs={{4,0},{8,4},{12,8},{16,12},{20,16},{24,20},{28,24},{32,28},{36,32}... | collective-permute-start | bytes 294920 | tf_op jit(solution)/shard_map/ppermute | solution.py:527
  7.8 0.0 copy-start
  7.8 4.9 %rims.1 = (f32[54,2,32,128]{3,2,1,0:T(8,128)}, f32[54,2,32,128]{3,2,1,0:T(8,128)}, f32[54,4,2,128]{3,2,1,0:T(2,128)}, f32[54,4,2,128]{3,2,1,0:T(2,128)}) custom-call(f32[54,4,32,128]{3,2,1,0:T(8,128)} %y_ref.1), custom_call_target="tpu_custom_call" | custom-call | tf_op jit(solution)/shard_map/rims/pallas_call | solution.py:507
  12.7 0.0 collective-permute-done.lo_ref
  12.7 0.0 collective-permute-done.1.hi_ref
  12.7 0.0 copy-done
  12.8 0.0 copy-start.2
  12.8 10.7 %all-gather = f32[32,5760]{1,0:T(8,128)} all-gather(f32[8,5760]{1,0:T(8,128)S(1)} %assemble.1), channel_id=2, replica_groups=mesh['space'=64,'group'=4] {'group'}, dimensions={0}, use_global_device_ids=true | all-gather | bytes 921600 | tf_op jit(solution)/shard_map/all_gather | solution.py:542
  23.4 1.3 %collective-permute-start.2 = (f32[54,2,32,128]{3,2,1,0:T(8,128)}, f32[54,2,32,128]{3,2,1,0:T(8,128)}, u32[]{:S(2)}, u32[]{:S(2)}) collective-permute-start(f32[54,2,32,128]{3,2,1,0:T(8,128)} %get-tuple-element.64), channel_id=1, source_target_pairs={{0,4},{4,8},{8,12},{12,16},{16,20},{20,24},{24,28},{28,32},{32,36}... | collective-permute-start | bytes 5308424 | tf_op jit(solution)/shard_map/ppermute | solution.py:547
  24.7 5.2 %collective-permute-start.3 = (f32[54,2,32,128]{3,2,1,0:T(8,128)}, f32[54,2,32,128]{3,2,1,0:T(8,128)}, u32[]{:S(2)}, u32[]{:S(2)}) collective-permute-start(f32[54,2,32,128]{3,2,1,0:T(8,128)} %get-tuple-element.65), channel_id=1, source_target_pairs={{4,0},{8,4},{12,8},{16,12},{20,16},{24,20},{28,24},{32,28},{36,32}... | collective-permute-start | bytes 5308424 | tf_op jit(solution)/shard_map/ppermute | solution.py:548
  30.0 4.3 %collective-permute-start.4 = (f32[54,4,2,128]{3,2,1,0:T(2,128)}, f32[54,4,2,128]{3,2,1,0:T(2,128)S(1)}, u32[]{:S(2)}, u32[]{:S(2)}) collective-permute-start(f32[54,4,2,128]{3,2,1,0:T(2,128)} %get-tuple-element.66), channel_id=1, source_target_pairs={{0,1},{1,2},{2,3},{4,5},{5,6},{6,7},{8,9},{9,10},{10,11},{12,13},{... | collective-permute-start | bytes 663560 | tf_op jit(solution)/shard_map/ppermute | solution.py:549
  34.9 0.0 copy-done.1
  34.9 0.0 copy-done.2
  34.9 0.0 copy-start.11
  34.9 13.0 %parcels.1 = (f32[7,4,32,128]{3,2,1,0:T(8,128)}, f32[7,1,32,128]{3,2,1,0:T(8,128)}, f32[7,1,32,128]{3,2,1,0:T(8,128)}, f32[8,16896]{1,0:T(8,128)}, f32[128,128]{1,0:T(8,128)}, /*index=5*/s32[8,128]{1,0:T(8,128)}) custom-call(s32[1]{0:T(128)} %copy.16.count_ref, f32[4,8,5760]{2,1,0:T(8,128)} %bitcast.5, f32[6,1,32,128]{3,2,1,0:T(8,128)} %copy-done.1, ...), custom_call_target="tpu_custom_call" | custom-call | tf_op jit(solution)/shard_map/parcels/pallas_call | solution.py:553
  47.9 29.9 %collective-permute-done.4.ylo_ref = f32[54,4,2,128]{3,2,1,0:T(2,128)S(1)} collective-permute-done((f32[54,4,2,128]{3,2,1,0:T(2,128)}, f32[54,4,2,128]{3,2,1,0:T(2,128)S(1)}, u32[]{:S(2)}, u32[]{:S(2)}) %collective-permute-start.4) | collective-permute-done | bytes 221216 | tf_op jit(solution)/shard_map/ppermute | solution.py:549
  77.8 0.0 copy-done.11
  77.8 1.9 %collective-permute-start.5 = (f32[54,4,2,128]{3,2,1,0:T(2,128)S(1)}, f32[54,4,2,128]{3,2,1,0:T(2,128)S(1)}, u32[]{:S(2)}, u32[]{:S(2)}) collective-permute-start(f32[54,4,2,128]{3,2,1,0:T(2,128)S(1)} %copy-done.11), channel_id=1, source_target_pairs={{1,0},{2,1},{3,2},{5,4},{6,5},{7,6},{9,8},{10,9},{11,10},{13,12},{... | collective-permute-start | bytes 663560 | tf_op jit(solution)/shard_map/ppermute | solution.py:602
  79.7 1.3 %collective-permute-start.6 = (f32[7,1,32,128]{3,2,1,0:T(8,128)}, f32[7,1,32,128]{3,2,1,0:T(8,128)S(1)}, u32[]{:S(2)}, u32[]{:S(2)}) collective-permute-start(f32[7,1,32,128]{3,2,1,0:T(8,128)} %get-tuple-element.72), channel_id=1, source_target_pairs={{0,4},{4,8},{8,12},{12,16},{16,20},{20,24},{24,28},{28,32},{32,36}... | collective-permute-start | bytes 344072 | tf_op jit(solution)/shard_map/ppermute | solution.py:604
  81.0 4.0 %collective-permute-start.7 = (f32[7,1,32,128]{3,2,1,0:T(8,128)}, f32[7,1,32,128]{3,2,1,0:T(8,128)S(1)}, u32[]{:S(2)}, u32[]{:S(2)}) collective-permute-start(f32[7,1,32,128]{3,2,1,0:T(8,128)} %get-tuple-element.73), channel_id=1, source_target_pairs={{4,0},{8,4},{12,8},{16,12},{20,16},{24,20},{28,24},{32,28},{36,32}... | collective-permute-start | bytes 344072 | tf_op jit(solution)/shard_map/ppermute | solution.py:605
  85.0 5.0 %spread.1 = (f32[8,4096]{1,0:T(8,128)}, f32[8,4096]{1,0:T(8,128)}, f32[8,4096]{1,0:T(8,128)}, f32[8,4096]{1,0:T(8,128)}) custom-call(s32[8,128]{1,0:T(8,128)} %get-tuple-element.74.off_ref, f32[128,128]{1,0:T(8,128)} %get-tuple-element.75.dst_ref, f32[8,16896]{1,0:T(8,128)} %get-tuple-element.76.state_ref), custom_call_target="tpu_custom_call" | custom-call | tf_op jit(solution)/shard_map/spread/pallas_call | solution.py:607
  90.0 0.0 collective-permute-done.6.rest_1_
  90.0 0.0 collective-permute-done.7.rest_2_
  90.0 0.0 copy-start.8
  90.0 0.0 collective-permute-done.5.yhi_ref
  90.0 0.0 copy-start.5
  90.1 0.1 collective-permute-start.10
  90.1 4.5 %collective-permute-start.8 = (f32[8,4096]{1,0:T(8,128)}, f32[8,4096]{1,0:T(8,128)}, u32[]{:S(2)}, u32[]{:S(2)}) collective-permute-start(f32[8,4096]{1,0:T(8,128)} %get-tuple-element.88), channel_id=1, source_target_pairs={{0,1},{1,2},{2,3},{3,0},{4,5},{5,6},{6,7},{7,4},{8,9},{9,10},{10,1... | collective-permute-start | bytes 393224 | tf_op jit(solution)/shard_map/ppermute | solution.py:623
  94.6 2.7 %collective-permute-start.9 = (f32[8,4096]{1,0:T(8,128)}, f32[8,4096]{1,0:T(8,128)}, u32[]{:S(2)}, u32[]{:S(2)}) collective-permute-start(f32[8,4096]{1,0:T(8,128)} %get-tuple-element.89), channel_id=1, source_target_pairs={{0,2},{1,3},{2,0},{3,1},{4,6},{5,7},{6,4},{7,5},{8,10},{9,11},{10,... | collective-permute-start | bytes 393224 | tf_op jit(solution)/shard_map/ppermute | solution.py:623
  97.3 0.0 collective-permute-done.2.xlo_ref
  97.3 0.0 collective-permute-done.3.xhi_ref
  97.4 0.0 copy-done.8
  97.4 0.0 copy-done.4
  97.4 0.0 copy-done.7
  97.4 0.0 copy-done.5
  97.4 0.0 copy-start.3
  97.4 0.0 copy-start.6
  97.4 0.0 copy-start.9
  97.4 0.0 copy-start.10
  97.4 7.9 %transport.1 = (f32[54,4,32,128]{3,2,1,0:T(8,128)}, f32[7,4,32,128]{3,2,1,0:T(8,128)}) custom-call(f32[54]{0:T(128)} %diff_ref.1, f32[54,4,32,128]{3,2,1,0:T(8,128)} %y_ref.1, f32[54,2,32,128]{3,2,1,0:T(8,128)} %collective-permute-done.2.xlo_ref, f32[54,2,32,128]{3,2,1,0:T(8,128)} %collective-permute-done.3.xhi_ref, f32[54,4,2,128]{3,2,1,0:T(2,128)} %copy-done.4, ...), custom_call_target="tpu_custom_call" | custom-call | tf_op jit(solution)/shard_map/transport/pallas_call | solution.py:641
  105.4 0.0 collective-permute-done.10
  105.4 0.0 collective-permute-done.8
  105.4 0.0 collective-permute-done.9
  105.4 0.0 copy-done.3
  105.4 0.0 copy-done.6
  105.4 1.7 %fusion = f32[5,4096]{1,0:T(8,128)} fusion(f32[8,4096]{1,0:T(8,128)S(1)} %collective-permute-done.10, f32[8,4096]{1,0:T(8,128)} %collective-permute-done.9, f32[8,4096]{1,0:T(8,128)} %collective-permute-done.8, f32[8,4096]{1,0:T(8,128)S(1)} %copy-done.6, f32[3,4096]{1,0:T(4,128)S(1)} %copy-done.3, f32[1,4096]{1,0:T(1,128)S(1)} %bitcast.7, ...), kind=kLoop, calls=%fused_computation.1 | loop fusion | flops 122880 | bytes 495616 | tf_op jit(solution)/shard_map/jit(_where)/select_n | solution.py:670
  (7 shorter events, 0.0 us)
Async XLA Ops:
  2.5 10.2 %collective-permute-start = (f32[6,1,32,128]{3,2,1,0:T(8,128)}, f32[6,1,32,128]{3,2,1,0:T(8,128)S(1)}, u32[]{:S(2)}, u32[]{:S(2)}) collective-permute-start(f32[6,1,32,128]{3,2,1,0:T(8,128)} %get-tuple-element.52), channel_id=1, source_target_pairs={{0,4},{4,8},{8,12},{12,16},{16,20},{20,24},{24,28},{28,32},{32,36}... | collective-permute-start | bytes 294920 | tf_op jit(solution)/shard_map/ppermute | solution.py:526
  3.8 8.9 %collective-permute-start.1 = (f32[6,1,32,128]{3,2,1,0:T(8,128)}, f32[6,1,32,128]{3,2,1,0:T(8,128)S(1)}, u32[]{:S(2)}, u32[]{:S(2)}) collective-permute-start(f32[6,1,32,128]{3,2,1,0:T(8,128)} %get-tuple-element.53), channel_id=1, source_target_pairs={{4,0},{8,4},{12,8},{16,12},{20,16},{24,20},{28,24},{32,28},{36,32}... | collective-permute-start | bytes 294920 | tf_op jit(solution)/shard_map/ppermute | solution.py:527
  7.8 4.9 %copy-start = (f32[8,5760]{1,0:T(8,128)S(1)}, f32[8,5760]{1,0:T(8,128)}, u32[]{:S(2)}) copy-start(f32[8,5760]{1,0:T(8,128)} %get-tuple-element.51.packed_ref) | copy-start | bytes 552964
  12.7 22.2 %copy-start.1 = (f32[6,1,32,128]{3,2,1,0:T(8,128)}, f32[6,1,32,128]{3,2,1,0:T(8,128)S(1)}, u32[]{:S(2)}) copy-start(f32[6,1,32,128]{3,2,1,0:T(8,128)S(1)} %collective-permute-done.lo_ref) | copy-start | bytes 294916
  12.8 22.1 %copy-start.2 = (f32[6,1,32,128]{3,2,1,0:T(8,128)}, f32[6,1,32,128]{3,2,1,0:T(8,128)S(1)}, u32[]{:S(2)}) copy-start(f32[6,1,32,128]{3,2,1,0:T(8,128)S(1)} %collective-permute-done.1.hi_ref) | copy-start | bytes 294916
  23.4 73.9 %collective-permute-start.2 = (f32[54,2,32,128]{3,2,1,0:T(8,128)}, f32[54,2,32,128]{3,2,1,0:T(8,128)}, u32[]{:S(2)}, u32[]{:S(2)}) collective-permute-start(f32[54,2,32,128]{3,2,1,0:T(8,128)} %get-tuple-element.64), channel_id=1, source_target_pairs={{0,4},{4,8},{8,12},{12,16},{16,20},{20,24},{24,28},{28,32},{32,36}... | collective-permute-start | bytes 5308424 | tf_op jit(solution)/shard_map/ppermute | solution.py:547
  24.7 72.6 %collective-permute-start.3 = (f32[54,2,32,128]{3,2,1,0:T(8,128)}, f32[54,2,32,128]{3,2,1,0:T(8,128)}, u32[]{:S(2)}, u32[]{:S(2)}) collective-permute-start(f32[54,2,32,128]{3,2,1,0:T(8,128)} %get-tuple-element.65), channel_id=1, source_target_pairs={{4,0},{8,4},{12,8},{16,12},{20,16},{24,20},{28,24},{32,28},{36,32}... | collective-permute-start | bytes 5308424 | tf_op jit(solution)/shard_map/ppermute | solution.py:548
  30.0 47.9 %collective-permute-start.4 = (f32[54,4,2,128]{3,2,1,0:T(2,128)}, f32[54,4,2,128]{3,2,1,0:T(2,128)S(1)}, u32[]{:S(2)}, u32[]{:S(2)}) collective-permute-start(f32[54,4,2,128]{3,2,1,0:T(2,128)} %get-tuple-element.66), channel_id=1, source_target_pairs={{0,1},{1,2},{2,3},{4,5},{5,6},{6,7},{8,9},{9,10},{10,11},{12,13},{... | collective-permute-start | bytes 663560 | tf_op jit(solution)/shard_map/ppermute | solution.py:549
  34.9 42.9 %copy-start.11 = (f32[54,4,2,128]{3,2,1,0:T(2,128)S(1)}, f32[54,4,2,128]{3,2,1,0:T(2,128)}, u32[]{:S(2)}) copy-start(f32[54,4,2,128]{3,2,1,0:T(2,128)} %get-tuple-element.71) | copy-start | bytes 663556
  77.8 19.6 %copy-start.4 = (f32[54,4,2,128]{3,2,1,0:T(2,128)}, f32[54,4,2,128]{3,2,1,0:T(2,128)S(1)}, u32[]{:S(2)}) copy-start(f32[54,4,2,128]{3,2,1,0:T(2,128)S(1)} %collective-permute-done.4.ylo_ref) | copy-start | bytes 663556
  77.8 12.2 %collective-permute-start.5 = (f32[54,4,2,128]{3,2,1,0:T(2,128)S(1)}, f32[54,4,2,128]{3,2,1,0:T(2,128)S(1)}, u32[]{:S(2)}, u32[]{:S(2)}) collective-permute-start(f32[54,4,2,128]{3,2,1,0:T(2,128)S(1)} %copy-done.11), channel_id=1, source_target_pairs={{1,0},{2,1},{3,2},{5,4},{6,5},{7,6},{9,8},{10,9},{11,10},{13,12},{... | collective-permute-start | bytes 663560 | tf_op jit(solution)/shard_map/ppermute | solution.py:602
  79.7 10.3 %collective-permute-start.6 = (f32[7,1,32,128]{3,2,1,0:T(8,128)}, f32[7,1,32,128]{3,2,1,0:T(8,128)S(1)}, u32[]{:S(2)}, u32[]{:S(2)}) collective-permute-start(f32[7,1,32,128]{3,2,1,0:T(8,128)} %get-tuple-element.72), channel_id=1, source_target_pairs={{0,4},{4,8},{8,12},{12,16},{16,20},{20,24},{24,28},{28,32},{32,36}... | collective-permute-start | bytes 344072 | tf_op jit(solution)/shard_map/ppermute | solution.py:604
  81.0 9.0 %collective-permute-start.7 = (f32[7,1,32,128]{3,2,1,0:T(8,128)}, f32[7,1,32,128]{3,2,1,0:T(8,128)S(1)}, u32[]{:S(2)}, u32[]{:S(2)}) collective-permute-start(f32[7,1,32,128]{3,2,1,0:T(8,128)} %get-tuple-element.73), channel_id=1, source_target_pairs={{4,0},{8,4},{12,8},{16,12},{20,16},{24,20},{28,24},{32,28},{36,32}... | collective-permute-start | bytes 344072 | tf_op jit(solution)/shard_map/ppermute | solution.py:605
  90.0 7.4 %copy-start.7 = (f32[7,1,32,128]{3,2,1,0:T(8,128)}, f32[7,1,32,128]{3,2,1,0:T(8,128)S(1)}, u32[]{:S(2)}) copy-start(f32[7,1,32,128]{3,2,1,0:T(8,128)S(1)} %collective-permute-done.6.rest_1_) | copy-start | bytes 344068
  90.0 7.3 %copy-start.8 = (f32[7,1,32,128]{3,2,1,0:T(8,128)}, f32[7,1,32,128]{3,2,1,0:T(8,128)S(1)}, u32[]{:S(2)}) copy-start(f32[7,1,32,128]{3,2,1,0:T(8,128)S(1)} %collective-permute-done.7.rest_2_) | copy-start | bytes 344068
  90.0 7.4 %copy-start.5 = (f32[54,4,2,128]{3,2,1,0:T(2,128)}, f32[54,4,2,128]{3,2,1,0:T(2,128)S(1)}, u32[]{:S(2)}) copy-start(f32[54,4,2,128]{3,2,1,0:T(2,128)S(1)} %collective-permute-done.5.yhi_ref) | copy-start | bytes 663556
  90.1 15.3 %collective-permute-start.10 = (f32[8,4096]{1,0:T(8,128)}, f32[8,4096]{1,0:T(8,128)S(1)}, u32[]{:S(2)}, u32[]{:S(2)}) collective-permute-start(f32[8,4096]{1,0:T(8,128)} %get-tuple-element.90), channel_id=1, source_target_pairs={{0,3},{1,0},{2,1},{3,2},{4,7},{5,4},{6,5},{7,6},{8,11},{9,8},{10,9... | collective-permute-start | bytes 393224 | tf_op jit(solution)/shard_map/ppermute | solution.py:623
  90.1 15.2 %collective-permute-start.8 = (f32[8,4096]{1,0:T(8,128)}, f32[8,4096]{1,0:T(8,128)}, u32[]{:S(2)}, u32[]{:S(2)}) collective-permute-start(f32[8,4096]{1,0:T(8,128)} %get-tuple-element.88), channel_id=1, source_target_pairs={{0,1},{1,2},{2,3},{3,0},{4,5},{5,6},{6,7},{7,4},{8,9},{9,10},{10,1... | collective-permute-start | bytes 393224 | tf_op jit(solution)/shard_map/ppermute | solution.py:623
  94.6 10.8 %collective-permute-start.9 = (f32[8,4096]{1,0:T(8,128)}, f32[8,4096]{1,0:T(8,128)}, u32[]{:S(2)}, u32[]{:S(2)}) collective-permute-start(f32[8,4096]{1,0:T(8,128)} %get-tuple-element.89), channel_id=1, source_target_pairs={{0,2},{1,3},{2,0},{3,1},{4,6},{5,7},{6,4},{7,5},{8,10},{9,11},{10,... | collective-permute-start | bytes 393224 | tf_op jit(solution)/shard_map/ppermute | solution.py:623
  97.4 8.0 %copy-start.3 = (f32[3,4096]{1,0:T(4,128)S(1)}, f32[3,4096]{1,0:T(4,128)}, u32[]{:S(2)}) copy-start(f32[3,4096]{1,0:T(4,128)} %velocity_ref.1) | copy-start | bytes 147460
  97.4 8.0 %copy-start.6 = (f32[8,4096]{1,0:T(8,128)S(1)}, f32[8,4096]{1,0:T(8,128)}, u32[]{:S(2)}) copy-start(f32[8,4096]{1,0:T(8,128)} %get-tuple-element.93) | copy-start | bytes 393220
  97.4 8.0 %copy-start.9 = (f32[4096]{0:T(1024)S(1)}, f32[4096]{0:T(1024)}, u32[]{:S(2)}) copy-start(f32[4096]{0:T(1024)} %radius_ref.1) | copy-start | bytes 49156
  97.4 8.0 %copy-start.10 = (f32[4096]{0:T(1024)S(1)}, f32[4096]{0:T(1024)}, u32[]{:S(2)}) copy-start(f32[4096]{0:T(1024)} %temp_ref.2) | copy-start | bytes 49156

commit v6 on v5

--- a/solution.py
+++ b/solution.py
@@ -544,9 +544,11 @@
     x_up, x_down, y_right, y_left, parcels = lax.optimization_barrier(
         (x_up, x_down, y_right, y_left, parcels)
     )
+    y_lo = lax.ppermute(y_right, "group", g_ahead)
+    y_hi = lax.ppermute(y_left, "group", g_back)
+    x_up, x_down, y_lo = lax.optimization_barrier((x_up, x_down, y_lo))
     x_lo = lax.ppermute(x_up, "space", ahead)
     x_hi = lax.ppermute(x_down, "space", back)
-    y_lo = lax.ppermute(y_right, "group", g_ahead)
 
     chunks = pl.cdiv(slots, CHUNK)
     reach = max(chunks * CHUNK, slots + WINDOW)
@@ -597,9 +599,6 @@
         compiler_params=limit,
         name="parcels",
     )(parcel_counts, parcels, field_lo, gas_temp, gas_density, gas_velocity, species, field_hi)
-
-    y_lo, y_left, state = lax.optimization_barrier((y_lo, y_left, state))
-    y_hi = lax.ppermute(y_left, "group", g_back)
 
     from_below = lax.ppermute(dep_hi, "space", ahead)
     from_above = lax.ppermute(dep_lo, "space", back)

time: 108 us -> 101 us (0.935)
  the two profiles are of different devices: /device:TPU:239 before, /device:TPU:1 now
where the time goes in v6:
time: 101 us; the launch traced here: 100 us
  Pallas kernels  37.4 us (37%)
  starting transfers between devices  25.4 us (25%)
  waiting for transfers between devices  22.9 us (23%)
  blocking collectives  12 us (12%)
  between operations  1.54 us (2%)
    pallas_call x1, Pallas kernels, per_device(): pl.pallas_call(parcel_kernel, grid=(1,), in_specs=[smem, whole((groups, 8...  17.7 us
    all_gather x1, blocking collectives, per_device(): parcels = lax.all_gather(sent, 'group', axis=0)  12 us
    ppermute x1, waiting for transfers between devices, per_device(): y_hi = lax.ppermute(y_left, 'group', g_back)  9.1 us
    pallas_call x1, Pallas kernels, per_device(): pl.pallas_call(functools.partial(transport_kernel, c == 0, first), grid=(...  7.91 us
    ppermute x1, waiting for transfers between devices, per_device(): from_below = lax.ppermute(dep_hi, 'space', ahead)  5.39 us
    ppermute x1, starting transfers between devices, per_device(): x_lo = lax.ppermute(x_up, 'space', ahead)  5.19 us
    ppermute x1, waiting for transfers between devices, per_device(): from_above = lax.ppermute(dep_lo, 'space', back)  5.19 us
    pallas_call x1, Pallas kernels, per_device(): pl.pallas_call(spread_kernel, grid=(1,), in_specs=[smem, whole((blocks, L...  4.99 us
  transfers between devices with their start and end apart: 11, of which 4 were waited for; matrix products, arithmetic and copies ran while one was open for 0% of the time, Pallas kernels for 35%

profile of v6, /device:TPU:1, one launch (start us, length us, event | category | flops | bytes accessed | tf_op | source)
XLA Modules:
  0.0 100.0 jit_solution(438409155373167357)
XLA Ops:
  0.6 1.9 %pack.1 = (f32[8,5760]{1,0:T(8,128)}, f32[6,1,32,128]{3,2,1,0:T(8,128)}, f32[6,1,32,128]{3,2,1,0:T(8,128)}) custom-call(s32[8,4096]{1,0:T(8,128)} %cells_ref.1, f32[8,4096]{1,0:T(8,128)} %weights_ref.1, f32[4096]{0:T(1024)} %radius_ref.1, f32[4096]{0:T(1024)} %temp_ref.2, f32[3,4096]{1,0:T(4,128)} %velocity_ref.1, f32[4,32,128]{2,1,0:T(8,128)} %temp_ref.3, ...), custom_call_target="tpu_custom_call" | custom-call | tf_op jit(solution)/shard_map/pack/pallas_call | solution.py:476
  2.5 3.9 %collective-permute-start = (f32[6,1,32,128]{3,2,1,0:T(8,128)}, f32[6,1,32,128]{3,2,1,0:T(8,128)S(1)}, u32[]{:S(2)}, u32[]{:S(2)}) collective-permute-start(f32[6,1,32,128]{3,2,1,0:T(8,128)} %get-tuple-element.52), channel_id=1, source_target_pairs={{0,4},{4,8},{8,12},{12,16},{16,20},{20,24},{24,28},{28,32},{32,36}... | collective-permute-start | bytes 294920 | tf_op jit(solution)/shard_map/ppermute | solution.py:526
  6.5 1.3 %collective-permute-start.1 = (f32[6,1,32,128]{3,2,1,0:T(8,128)}, f32[6,1,32,128]{3,2,1,0:T(8,128)S(1)}, u32[]{:S(2)}, u32[]{:S(2)}) collective-permute-start(f32[6,1,32,128]{3,2,1,0:T(8,128)} %get-tuple-element.53), channel_id=1, source_target_pairs={{4,0},{8,4},{12,8},{16,12},{20,16},{24,20},{28,24},{32,28},{36,32}... | collective-permute-start | bytes 294920 | tf_op jit(solution)/shard_map/ppermute | solution.py:527
  7.8 0.0 copy-start
  7.8 4.9 %rims.1 = (f32[54,2,32,128]{3,2,1,0:T(8,128)}, f32[54,2,32,128]{3,2,1,0:T(8,128)}, f32[54,4,2,128]{3,2,1,0:T(2,128)}, f32[54,4,2,128]{3,2,1,0:T(2,128)}) custom-call(f32[54,4,32,128]{3,2,1,0:T(8,128)} %y_ref.1), custom_call_target="tpu_custom_call" | custom-call | tf_op jit(solution)/shard_map/rims/pallas_call | solution.py:507
  12.7 0.0 collective-permute-done.lo_ref
  12.7 0.0 copy-start.1
  12.7 0.0 collective-permute-done.1.hi_ref
  12.7 0.0 copy-done
  12.7 0.0 copy-start.2
  12.7 12.0 %all-gather = f32[32,5760]{1,0:T(8,128)} all-gather(f32[8,5760]{1,0:T(8,128)S(1)} %assemble.1), channel_id=2, replica_groups=mesh['space'=64,'group'=4] {'group'}, dimensions={0}, use_global_device_ids=true | all-gather | bytes 921600 | tf_op jit(solution)/shard_map/all_gather | solution.py:542
  24.7 3.3 %collective-permute-start.2 = (f32[54,4,2,128]{3,2,1,0:T(2,128)}, f32[54,4,2,128]{3,2,1,0:T(2,128)S(1)}, u32[]{:S(2)}, u32[]{:S(2)}) collective-permute-start(f32[54,4,2,128]{3,2,1,0:T(2,128)} %get-tuple-element.66), channel_id=1, source_target_pairs={{0,1},{1,2},{2,3},{4,5},{5,6},{6,7},{8,9},{9,10},{10,11},{12,13},{... | collective-permute-start | bytes 663560 | tf_op jit(solution)/shard_map/ppermute | solution.py:547
  28.0 3.2 %collective-permute-done.2.ylo_ref = f32[54,4,2,128]{3,2,1,0:T(2,128)S(1)} collective-permute-done((f32[54,4,2,128]{3,2,1,0:T(2,128)}, f32[54,4,2,128]{3,2,1,0:T(2,128)S(1)}, u32[]{:S(2)}, u32[]{:S(2)}) %collective-permute-start.2) | collective-permute-done | bytes 221216 | tf_op jit(solution)/shard_map/ppermute | solution.py:547
  31.2 0.0 copy-start.4
  31.2 5.2 %collective-permute-start.3 = (f32[54,2,32,128]{3,2,1,0:T(8,128)}, f32[54,2,32,128]{3,2,1,0:T(8,128)}, u32[]{:S(2)}, u32[]{:S(2)}) collective-permute-start(f32[54,2,32,128]{3,2,1,0:T(8,128)} %get-tuple-element.67), channel_id=1, source_target_pairs={{0,4},{4,8},{8,12},{12,16},{16,20},{20,24},{24,28},{28,32},{32,36}... | collective-permute-start | bytes 5308424 | tf_op jit(solution)/shard_map/ppermute | solution.py:550
  36.4 1.3 %collective-permute-start.4 = (f32[54,2,32,128]{3,2,1,0:T(8,128)}, f32[54,2,32,128]{3,2,1,0:T(8,128)}, u32[]{:S(2)}, u32[]{:S(2)}) collective-permute-start(f32[54,2,32,128]{3,2,1,0:T(8,128)} %get-tuple-element.68), channel_id=1, source_target_pairs={{4,0},{8,4},{12,8},{16,12},{20,16},{24,20},{28,24},{32,28},{36,32}... | collective-permute-start | bytes 5308424 | tf_op jit(solution)/shard_map/ppermute | solution.py:551
  37.7 1.9 %collective-permute-start.5 = (f32[54,4,2,128]{3,2,1,0:T(2,128)}, f32[54,4,2,128]{3,2,1,0:T(2,128)S(1)}, u32[]{:S(2)}, u32[]{:S(2)}) collective-permute-start(f32[54,4,2,128]{3,2,1,0:T(2,128)} %get-tuple-element.70), channel_id=1, source_target_pairs={{1,0},{2,1},{3,2},{5,4},{6,5},{7,6},{9,8},{10,9},{11,10},{13,12},{... | collective-permute-start | bytes 663560 | tf_op jit(solution)/shard_map/ppermute | solution.py:548
  40.2 0.0 copy-done.1
  40.2 0.0 copy-done.2
  40.3 17.7 %parcels.1 = (f32[7,4,32,128]{3,2,1,0:T(8,128)}, f32[7,1,32,128]{3,2,1,0:T(8,128)}, f32[7,1,32,128]{3,2,1,0:T(8,128)}, f32[8,16896]{1,0:T(8,128)}, f32[128,128]{1,0:T(8,128)}, /*index=5*/s32[8,128]{1,0:T(8,128)}) custom-call(s32[1]{0:T(128)} %copy.16.count_ref, f32[4,8,5760]{2,1,0:T(8,128)} %bitcast.5, f32[6,1,32,128]{3,2,1,0:T(8,128)} %copy-done.1, ...), custom_call_target="tpu_custom_call" | custom-call | tf_op jit(solution)/shard_map/parcels/pallas_call | solution.py:555
  57.9 0.0 copy-done.4
  57.9 4.0 %collective-permute-start.6 = (f32[7,1,32,128]{3,2,1,0:T(8,128)}, f32[7,1,32,128]{3,2,1,0:T(8,128)S(1)}, u32[]{:S(2)}, u32[]{:S(2)}) collective-permute-start(f32[7,1,32,128]{3,2,1,0:T(8,128)} %get-tuple-element.72), channel_id=1, source_target_pairs={{0,4},{4,8},{8,12},{12,16},{16,20},{20,24},{24,28},{28,32},{32,36}... | collective-permute-start | bytes 344072 | tf_op jit(solution)/shard_map/ppermute | solution.py:603
  62.0 1.3 %collective-permute-start.7 = (f32[7,1,32,128]{3,2,1,0:T(8,128)}, f32[7,1,32,128]{3,2,1,0:T(8,128)S(1)}, u32[]{:S(2)}, u32[]{:S(2)}) collective-permute-start(f32[7,1,32,128]{3,2,1,0:T(8,128)} %get-tuple-element.73), channel_id=1, source_target_pairs={{4,0},{8,4},{12,8},{16,12},{20,16},{24,20},{28,24},{32,28},{36,32}... | collective-permute-start | bytes 344072 | tf_op jit(solution)/shard_map/ppermute | solution.py:604
  63.3 5.0 %spread.1 = (f32[8,4096]{1,0:T(8,128)}, f32[8,4096]{1,0:T(8,128)}, f32[8,4096]{1,0:T(8,128)}, f32[8,4096]{1,0:T(8,128)}) custom-call(s32[8,128]{1,0:T(8,128)} %get-tuple-element.74.off_ref, f32[128,128]{1,0:T(8,128)} %get-tuple-element.75.dst_ref, f32[8,16896]{1,0:T(8,128)} %get-tuple-element.76.state_ref), custom_call_target="tpu_custom_call" | custom-call | tf_op jit(solution)/shard_map/spread/pallas_call | solution.py:606
  68.2 5.4 %collective-permute-done.6.rest_1_ = f32[7,1,32,128]{3,2,1,0:T(8,128)S(1)} collective-permute-done((f32[7,1,32,128]{3,2,1,0:T(8,128)}, f32[7,1,32,128]{3,2,1,0:T(8,128)S(1)}, u32[]{:S(2)}, u32[]{:S(2)}) %collective-permute-start.6) | collective-permute-done | bytes 114720 | tf_op jit(solution)/shard_map/ppermute | solution.py:603
  73.6 5.2 %collective-permute-done.7.rest_2_ = f32[7,1,32,128]{3,2,1,0:T(8,128)S(1)} collective-permute-done((f32[7,1,32,128]{3,2,1,0:T(8,128)}, f32[7,1,32,128]{3,2,1,0:T(8,128)S(1)}, u32[]{:S(2)}, u32[]{:S(2)}) %collective-permute-start.7) | collective-permute-done | bytes 114720 | tf_op jit(solution)/shard_map/ppermute | solution.py:604
  78.8 9.1 %collective-permute-done.5.yhi_ref = f32[54,4,2,128]{3,2,1,0:T(2,128)S(1)} collective-permute-done((f32[54,4,2,128]{3,2,1,0:T(2,128)}, f32[54,4,2,128]{3,2,1,0:T(2,128)S(1)}, u32[]{:S(2)}, u32[]{:S(2)}) %collective-permute-start.5) | collective-permute-done | bytes 221216 | tf_op jit(solution)/shard_map/ppermute | solution.py:548
  87.9 0.0 collective-permute-start.10
  87.9 3.2 %collective-permute-start.8 = (f32[8,4096]{1,0:T(8,128)}, f32[8,4096]{1,0:T(8,128)S(1)}, u32[]{:S(2)}, u32[]{:S(2)}) collective-permute-start(f32[8,4096]{1,0:T(8,128)} %get-tuple-element.88), channel_id=1, source_target_pairs={{0,1},{1,2},{2,3},{3,0},{4,5},{5,6},{6,7},{7,4},{8,9},{9,10},{10,1... | collective-permute-start | bytes 393224 | tf_op jit(solution)/shard_map/ppermute | solution.py:622
  91.2 0.0 collective-permute-start.9
  91.2 0.0 collective-permute-done.3.xlo_ref
  91.2 0.0 collective-permute-done.4.xhi_ref
  91.2 0.0 copy-done.8
  91.2 0.0 copy-done.7
  91.2 0.0 copy-done.5
  91.2 0.0 copy-start.3
  91.3 0.0 copy-start.6
  91.3 0.0 copy-start.9
  91.3 0.0 copy-start.10
  91.3 7.9 %transport.1 = (f32[54,4,32,128]{3,2,1,0:T(8,128)}, f32[7,4,32,128]{3,2,1,0:T(8,128)}) custom-call(f32[54]{0:T(128)} %diff_ref.1, f32[54,4,32,128]{3,2,1,0:T(8,128)} %y_ref.1, f32[54,2,32,128]{3,2,1,0:T(8,128)} %collective-permute-done.3.xlo_ref, f32[54,2,32,128]{3,2,1,0:T(8,128)} %collective-permute-done.4.xhi_ref, f32[54,4,2,128]{3,2,1,0:T(2,128)} %copy-done.4, ...), custom_call_target="tpu_custom_call" | custom-call | tf_op jit(solution)/shard_map/transport/pallas_call | solution.py:640
  99.2 0.0 collective-permute-done.10
  99.2 0.0 collective-permute-done.8
  99.2 0.0 collective-permute-done.9
  99.2 0.0 copy-done.3
  99.2 0.0 copy-done.6
  99.3 0.0 copy-done.9
  99.3 0.0 copy-done.10
  99.3 0.7 fusion
  (5 shorter events, 0.0 us)
Async XLA Ops:
  2.5 10.1 %collective-permute-start = (f32[6,1,32,128]{3,2,1,0:T(8,128)}, f32[6,1,32,128]{3,2,1,0:T(8,128)S(1)}, u32[]{:S(2)}, u32[]{:S(2)}) collective-permute-start(f32[6,1,32,128]{3,2,1,0:T(8,128)} %get-tuple-element.52), channel_id=1, source_target_pairs={{0,4},{4,8},{8,12},{12,16},{16,20},{20,24},{24,28},{28,32},{32,36}... | collective-permute-start | bytes 294920 | tf_op jit(solution)/shard_map/ppermute | solution.py:526
  6.5 6.2 %collective-permute-start.1 = (f32[6,1,32,128]{3,2,1,0:T(8,128)}, f32[6,1,32,128]{3,2,1,0:T(8,128)S(1)}, u32[]{:S(2)}, u32[]{:S(2)}) collective-permute-start(f32[6,1,32,128]{3,2,1,0:T(8,128)} %get-tuple-element.53), channel_id=1, source_target_pairs={{4,0},{8,4},{12,8},{16,12},{20,16},{24,20},{28,24},{32,28},{36,32}... | collective-permute-start | bytes 294920 | tf_op jit(solution)/shard_map/ppermute | solution.py:527
  7.8 4.9 %copy-start = (f32[8,5760]{1,0:T(8,128)S(1)}, f32[8,5760]{1,0:T(8,128)}, u32[]{:S(2)}) copy-start(f32[8,5760]{1,0:T(8,128)} %get-tuple-element.51.packed_ref) | copy-start | bytes 552964
  12.7 27.6 %copy-start.1 = (f32[6,1,32,128]{3,2,1,0:T(8,128)}, f32[6,1,32,128]{3,2,1,0:T(8,128)S(1)}, u32[]{:S(2)}) copy-start(f32[6,1,32,128]{3,2,1,0:T(8,128)S(1)} %collective-permute-done.lo_ref) | copy-start | bytes 294916
  12.7 27.5 %copy-start.2 = (f32[6,1,32,128]{3,2,1,0:T(8,128)}, f32[6,1,32,128]{3,2,1,0:T(8,128)S(1)}, u32[]{:S(2)}) copy-start(f32[6,1,32,128]{3,2,1,0:T(8,128)S(1)} %collective-permute-done.1.hi_ref) | copy-start | bytes 294916
  24.7 6.4 %collective-permute-start.2 = (f32[54,4,2,128]{3,2,1,0:T(2,128)}, f32[54,4,2,128]{3,2,1,0:T(2,128)S(1)}, u32[]{:S(2)}, u32[]{:S(2)}) collective-permute-start(f32[54,4,2,128]{3,2,1,0:T(2,128)} %get-tuple-element.66), channel_id=1, source_target_pairs={{0,1},{1,2},{2,3},{4,5},{5,6},{6,7},{8,9},{9,10},{10,11},{12,13},{... | collective-permute-start | bytes 663560 | tf_op jit(solution)/shard_map/ppermute | solution.py:547
  31.2 26.8 %copy-start.4 = (f32[54,4,2,128]{3,2,1,0:T(2,128)}, f32[54,4,2,128]{3,2,1,0:T(2,128)S(1)}, u32[]{:S(2)}) copy-start(f32[54,4,2,128]{3,2,1,0:T(2,128)S(1)} %collective-permute-done.2.ylo_ref) | copy-start | bytes 663556
  31.2 60.0 %collective-permute-start.3 = (f32[54,2,32,128]{3,2,1,0:T(8,128)}, f32[54,2,32,128]{3,2,1,0:T(8,128)}, u32[]{:S(2)}, u32[]{:S(2)}) collective-permute-start(f32[54,2,32,128]{3,2,1,0:T(8,128)} %get-tuple-element.67), channel_id=1, source_target_pairs={{0,4},{4,8},{8,12},{12,16},{16,20},{20,24},{24,28},{28,32},{32,36}... | collective-permute-start | bytes 5308424 | tf_op jit(solution)/shard_map/ppermute | solution.py:550
  36.4 54.8 %collective-permute-start.4 = (f32[54,2,32,128]{3,2,1,0:T(8,128)}, f32[54,2,32,128]{3,2,1,0:T(8,128)}, u32[]{:S(2)}, u32[]{:S(2)}) collective-permute-start(f32[54,2,32,128]{3,2,1,0:T(8,128)} %get-tuple-element.68), channel_id=1, source_target_pairs={{4,0},{8,4},{12,8},{16,12},{20,16},{24,20},{28,24},{32,28},{36,32}... | collective-permute-start | bytes 5308424 | tf_op jit(solution)/shard_map/ppermute | solution.py:551
  37.7 50.3 %collective-permute-start.5 = (f32[54,4,2,128]{3,2,1,0:T(2,128)}, f32[54,4,2,128]{3,2,1,0:T(2,128)S(1)}, u32[]{:S(2)}, u32[]{:S(2)}) collective-permute-start(f32[54,4,2,128]{3,2,1,0:T(2,128)} %get-tuple-element.70), channel_id=1, source_target_pairs={{1,0},{2,1},{3,2},{5,4},{6,5},{7,6},{9,8},{10,9},{11,10},{13,12},{... | collective-permute-start | bytes 663560 | tf_op jit(solution)/shard_map/ppermute | solution.py:548
  57.9 15.7 %collective-permute-start.6 = (f32[7,1,32,128]{3,2,1,0:T(8,128)}, f32[7,1,32,128]{3,2,1,0:T(8,128)S(1)}, u32[]{:S(2)}, u32[]{:S(2)}) collective-permute-start(f32[7,1,32,128]{3,2,1,0:T(8,128)} %get-tuple-element.72), channel_id=1, source_target_pairs={{0,4},{4,8},{8,12},{12,16},{16,20},{20,24},{24,28},{28,32},{32,36}... | collective-permute-start | bytes 344072 | tf_op jit(solution)/shard_map/ppermute | solution.py:603
  62.0 16.9 %collective-permute-start.7 = (f32[7,1,32,128]{3,2,1,0:T(8,128)}, f32[7,1,32,128]{3,2,1,0:T(8,128)S(1)}, u32[]{:S(2)}, u32[]{:S(2)}) collective-permute-start(f32[7,1,32,128]{3,2,1,0:T(8,128)} %get-tuple-element.73), channel_id=1, source_target_pairs={{4,0},{8,4},{12,8},{16,12},{20,16},{24,20},{28,24},{32,28},{36,32}... | collective-permute-start | bytes 344072 | tf_op jit(solution)/shard_map/ppermute | solution.py:604
  73.6 17.6 %copy-start.7 = (f32[7,1,32,128]{3,2,1,0:T(8,128)}, f32[7,1,32,128]{3,2,1,0:T(8,128)S(1)}, u32[]{:S(2)}) copy-start(f32[7,1,32,128]{3,2,1,0:T(8,128)S(1)} %collective-permute-done.6.rest_1_) | copy-start | bytes 344068
  78.8 12.4 %copy-start.8 = (f32[7,1,32,128]{3,2,1,0:T(8,128)}, f32[7,1,32,128]{3,2,1,0:T(8,128)S(1)}, u32[]{:S(2)}) copy-start(f32[7,1,32,128]{3,2,1,0:T(8,128)S(1)} %collective-permute-done.7.rest_2_) | copy-start | bytes 344068
  87.9 3.3 %copy-start.5 = (f32[54,4,2,128]{3,2,1,0:T(2,128)}, f32[54,4,2,128]{3,2,1,0:T(2,128)S(1)}, u32[]{:S(2)}) copy-start(f32[54,4,2,128]{3,2,1,0:T(2,128)S(1)} %collective-permute-done.5.yhi_ref) | copy-start | bytes 663556
  87.9 11.3 %collective-permute-start.10 = (f32[8,4096]{1,0:T(8,128)}, f32[8,4096]{1,0:T(8,128)S(1)}, u32[]{:S(2)}, u32[]{:S(2)}) collective-permute-start(f32[8,4096]{1,0:T(8,128)} %get-tuple-element.90), channel_id=1, source_target_pairs={{0,3},{1,0},{2,1},{3,2},{4,7},{5,4},{6,5},{7,6},{8,11},{9,8},{10,9... | collective-permute-start | bytes 393224 | tf_op jit(solution)/shard_map/ppermute | solution.py:622
  87.9 11.3 %collective-permute-start.8 = (f32[8,4096]{1,0:T(8,128)}, f32[8,4096]{1,0:T(8,128)S(1)}, u32[]{:S(2)}, u32[]{:S(2)}) collective-permute-start(f32[8,4096]{1,0:T(8,128)} %get-tuple-element.88), channel_id=1, source_target_pairs={{0,1},{1,2},{2,3},{3,0},{4,5},{5,6},{6,7},{7,4},{8,9},{9,10},{10,1... | collective-permute-start | bytes 393224 | tf_op jit(solution)/shard_map/ppermute | solution.py:622
  91.2 8.0 %collective-permute-start.9 = (f32[8,4096]{1,0:T(8,128)}, f32[8,4096]{1,0:T(8,128)S(1)}, u32[]{:S(2)}, u32[]{:S(2)}) collective-permute-start(f32[8,4096]{1,0:T(8,128)} %get-tuple-element.89), channel_id=1, source_target_pairs={{0,2},{1,3},{2,0},{3,1},{4,6},{5,7},{6,4},{7,5},{8,10},{9,11},{10,... | collective-permute-start | bytes 393224 | tf_op jit(solution)/shard_map/ppermute | solution.py:622
  91.2 8.0 %copy-start.3 = (f32[3,4096]{1,0:T(4,128)S(1)}, f32[3,4096]{1,0:T(4,128)}, u32[]{:S(2)}) copy-start(f32[3,4096]{1,0:T(4,128)} %velocity_ref.1) | copy-start | bytes 147460
  91.3 8.0 %copy-start.6 = (f32[8,4096]{1,0:T(8,128)S(1)}, f32[8,4096]{1,0:T(8,128)}, u32[]{:S(2)}) copy-start(f32[8,4096]{1,0:T(8,128)} %get-tuple-element.93) | copy-start | bytes 393220
  91.3 8.0 %copy-start.9 = (f32[4096]{0:T(1024)S(1)}, f32[4096]{0:T(1024)}, u32[]{:S(2)}) copy-start(f32[4096]{0:T(1024)} %radius_ref.1) | copy-start | bytes 49156
  91.3 8.0 %copy-start.10 = (f32[4096]{0:T(1024)S(1)}, f32[4096]{0:T(1024)}, u32[]{:S(2)}) copy-start(f32[4096]{0:T(1024)} %temp_ref.2) | copy-start | bytes 49156
